TPU v7x, 32 devices: a whole 2x2x4 slice. The times are simulated.
32 devices in a mesh: blk: 8 (over z, y), dp: 4 (over x, core).
Axes of the slice: x: 2, y: 2, z: 4, core: 2. Of those that a mesh axis runs over, the one named last changes fastest.
Arguments:
- frames: bfloat16 [131072, 768], P(('blk', 'dp')), may hold values from -6 to 6
- lengths: int32 [4096], P(('blk', 'dp')), may hold values from 1 to 32, as said below
- routes: int32 [32, 4, 512], P(('blk', 'dp')), may hold values from -1 to 2047, as said below
- w_first: bfloat16 [768, 512], replicated, may hold values from -0.21875 to 0.21875
- b_first: float32 [512], replicated, may hold values from -3 to 3
- w_second: bfloat16 [512, 512], replicated, may hold values from -0.25 to 0.25
- captions: bfloat16 [4096, 512], P(('blk', 'dp')), may hold values from -6 to 6
- logit_scale: float32 [], replicated, may hold values from 10 to 30
Outputs:
- grad_pooled: float32 [4096, 512], P(('blk', 'dp'))
- grad_text: float32 [4096, 512], P(('blk', 'dp'))
Inputs may be any that keep to these rules, and one draw needn't show every extreme that they name: Each device has at most 2048 live frame rows (the sum of its clips' lengths), and exactly 2048 on some device. `routes`: every live frame row of a device appears exactly once in its table and no other row appears; each owner's slots are filled from the front; on some device every slot is filled.
All inputs are finite; a program needn't handle non-finite values.
Results may differ from a plain program's by a relative error of at most 0.0061.
Values may be sent and summed in bfloat16 or wider, within the bound.
No kernel may reach another device: no remote copies, remote signals or barrier semaphores. Data moves between devices by JAX's collectives and lax.ppermute only.
A program may use at most 64 MiB of HBM per device.

v0:
```python
import jax
import jax.numpy as jnp
from jax import lax
from jax.sharding import PartitionSpec as P

epsilon = 1e-06
very_low = -1e30


def from_behind(block, axis, distance):
    devices = range(lax.axis_size(axis))
    route = [((i - distance) % len(devices), i) for i in devices]
    return lax.ppermute(block, axis, route)


def frame_project(frame_rows, w_first, b_first, w_second):
    before = jnp.dot(frame_rows, w_first, preferred_element_type=jnp.float32) + b_first
    active = jax.nn.gelu(before).astype(jnp.bfloat16)
    return jnp.dot(active, w_second, preferred_element_type=jnp.float32).astype(jnp.bfloat16)


def unit_rows(values):
    radius = jnp.sqrt(jnp.sum(values * values, axis=-1, keepdims=True) + epsilon)
    return (values / radius, radius)


def unit_backward(unit_vec, radius, upstream):
    return (upstream - unit_vec * jnp.sum(unit_vec * upstream, axis=-1, keepdims=True)) / radius


def online_update(run_max, run_sum, logits, axis_index):
    new_max = jnp.maximum(run_max, jnp.max(logits, axis=axis_index))
    expanded = jnp.expand_dims(new_max, axis_index)
    new_sum = run_sum * jnp.exp(run_max - new_max) + jnp.sum(
        jnp.exp(logits - expanded), axis=axis_index
    )
    return (new_max, new_sum)


def local(frames, lengths, routes, w_first, b_first, w_second, captions, logit_scale):
    clip_count = lengths.shape[0]
    cycle_size = lax.axis_size("blk")
    pair_count = clip_count * cycle_size * lax.axis_size("dp")
    route_table = routes[0]
    clip_ends = jnp.cumsum(lengths)
    positions = jnp.arange(frames.shape[0], dtype=jnp.int32)
    clip_ids = jnp.sum((clip_ends[None, :] <= positions[:, None]).astype(jnp.int32), axis=1)
    is_live = route_table >= 0
    safe_rows = jnp.where(is_live, route_table, 0)
    picked = jnp.take(frames, safe_rows, axis=0)
    slot_clips = jnp.where(is_live, jnp.take(clip_ids, safe_rows), -1)
    clip_iota = jnp.arange(clip_count, dtype=jnp.int32)
    hidden = frame_project(
        lax.all_to_all(picked, "dp", split_axis=0, concat_axis=0, tiled=True),
        w_first,
        b_first,
        w_second,
    )
    owner_clips = lax.all_to_all(slot_clips, "dp", split_axis=0, concat_axis=0, tiled=True)
    onehot = (owner_clips[:, :, None] == clip_iota).astype(jnp.bfloat16)
    partial_value = jnp.einsum("jsc,jse->jce", onehot, hidden, preferred_element_type=jnp.float32)
    returned = lax.all_to_all(partial_value, "dp", split_axis=0, concat_axis=0, tiled=True)
    pooled_sums = jnp.sum(returned, axis=0)
    pooled = pooled_sums / lengths.astype(jnp.float32)[:, None]
    audio_unit, audio_radius = unit_rows(pooled)
    text_unit, text_radius = unit_rows(captions.astype(jnp.float32))
    audio_low = audio_unit.astype(jnp.bfloat16)
    text_low = text_unit.astype(jnp.bfloat16)

    def score_tile(text_block):
        return logit_scale * lax.dot_general(
            audio_low, text_block, (((1,), (1,)), ((), ())), preferred_element_type=jnp.float32
        )

    low_start = jnp.full((clip_count,), very_low, jnp.float32)
    zero_start = jnp.zeros((clip_count,), jnp.float32)

    def lap_step(turn_index, running):
        text_block, col_max, col_sum, row_max, row_sum = running
        logits = score_tile(text_block)
        row_max, row_sum = online_update(row_max, row_sum, logits, 1)
        col_max, col_sum = online_update(col_max, col_sum, logits, 0)
        text_block = from_behind(text_block, "blk", 1)
        col_max, col_sum = from_behind((col_max, col_sum), "blk", 1)
        return (text_block, col_max, col_sum, row_max, row_sum)

    finished = lax.fori_loop(
        0, cycle_size, lap_step, (text_low, low_start, zero_start, low_start, zero_start)
    )
    col_lse = finished[1] + jnp.log(finished[2])
    row_lse = finished[3] + jnp.log(finished[4])
    identity_tile = jnp.eye(clip_count, dtype=jnp.float32)
    grad_start = jnp.zeros((clip_count, audio_low.shape[1]), jnp.float32)

    def grad_step(turn_index, running):
        text_block, block_lse, grad_caption, grad_audio = running
        logits = score_tile(text_block)
        own_block = (turn_index == 0).astype(jnp.float32)
        weights = (
            (
                jnp.exp(logits - row_lse[:, None])
                + jnp.exp(logits - block_lse[None, :])
                - 2.0 * own_block * identity_tile
            )
            / (2.0 * pair_count)
        ).astype(jnp.bfloat16)
        grad_audio = grad_audio + logit_scale * jnp.dot(
            weights, text_block, preferred_element_type=jnp.float32
        )
        grad_caption = grad_caption + logit_scale * lax.dot_general(
            weights, audio_low, (((0,), (0,)), ((), ())), preferred_element_type=jnp.float32
        )
        text_block = from_behind(text_block, "blk", 1)
        block_lse, grad_caption = from_behind((block_lse, grad_caption), "blk", 1)
        return (text_block, block_lse, grad_caption, grad_audio)

    finished_grad = lax.fori_loop(
        0, cycle_size, grad_step, (text_low, col_lse, grad_start, grad_start)
    )
    grad_caption = finished_grad[2]
    grad_audio = finished_grad[3]
    grad_pooled = unit_backward(audio_unit, audio_radius, grad_audio)
    grad_text = unit_backward(text_unit, text_radius, grad_caption)
    return (grad_pooled, grad_text)


def solution(mesh):
    return jax.shard_map(
        local,
        mesh=mesh,
        in_specs=(
            P(("blk", "dp"), None),
            P(("blk", "dp")),
            P(("blk", "dp"), None, None),
            P(),
            P(),
            P(),
            P(("blk", "dp"), None),
            P(),
        ),
        out_specs=(P(("blk", "dp"), None), P(("blk", "dp"), None)),
        check_vma=False,
    )
```

profile of v0, /device:TPU:0, one launch (start us, length us, event | category | flops | bytes accessed | tf_op | source)
XLA Modules:
  0.0 284.6 jit_solution(603033820969494812)
XLA Ops:
  3.1 11.8 %gather_fusion = s32[2048]{0:T(1024)S(1)} fusion(s32[4096]{0:T(1024)S(1)} %convert_reduce_fusion, s32[2048]{0:T(1024)S(1)} %broadcast_clamp_fusion), kind=kCustom, calls=%fused_computation | custom fusion | bytes 24576 | tf_op jit(solution)/shard_map/jit(_take)/gather | solution.py:51
  19.8 13.7 %gather_fusion.1 = bf16[2048,768]{1,0:T(8,128)(2,1)} fusion(bf16[4096,768]{1,0:T(8,128)(2,1)} %param.12, s32[2048]{0:T(1024)S(1)} %broadcast_clamp_fusion), kind=kCustom, calls=%fused_computation.1 | custom fusion | bytes 6299648 | tf_op jit(solution)/shard_map/jit(_take)/gather | solution.py:50
  36.7 4.6 %all-to-all-start.1 = ((bf16[4,512,768]{2,1,0:T(8,128)(2,1)}), bf16[4,512,768]{2,1,0:T(8,128)(2,1)}, u32[]{:S(2)}, u32[]{:S(2)}) async-start(bf16[4,512,768]{2,1,0:T(8,128)(2,1)} %broadcast_select_fusion.2), calls=%async_computation.1 | async-start | bytes 6291456 | tf_op jit(solution)/shard_map/all_to_all | solution.py:54
  41.4 37.0 %all-to-all-done.1 = bf16[4,512,768]{2,1,0:T(8,128)(2,1)} async-done(((bf16[4,512,768]{2,1,0:T(8,128)(2,1)}), bf16[4,512,768]{2,1,0:T(8,128)(2,1)}, u32[]{:S(2)}, u32[]{:S(2)}) %all-to-all-start.1) | async-done | bytes 3145760 | tf_op jit(solution)/shard_map/all_to_all | solution.py:54
  78.4 5.6 %fusion.25 = f32[4,512,512]{2,1,0:T(8,128)} fusion(bf16[4,512,768]{2,1,0:T(8,128)(2,1)} %all-to-all-done.1, bf16[768,512]{1,0:T(8,128)(2,1)S(1)} %copy-done), kind=kOutput, calls=%fused_computation.37 | convolution fusion | flops 1610612736 | bytes 8126464 | tf_op jit(solution)/shard_map/dot_general | solution.py:17
  84.0 5.2 %fusion.17 = f32[4,128,512]{2,1,0:T(8,128)} fusion(f32[4,512,512]{2,1,0:T(8,128)} %fusion.25, f32[512]{0:T(512)S(1)} %copy-done.5, bf16[512,512]{1,0:T(8,128)(2,1)S(1)} %copy-done.4, s32[4,512]{1,0:T(4,128)S(1)} %bitcast.51), kind=kOutput, calls=%fused_computation.31 | convolution fusion | flops 1353973760 | bytes 5777408 | tf_op jit(solution)/shard_map/jsc,jse->jce/dot_general | solution.py:61
  93.1 14.1 %all-to-all-done.2 = f32[4,128,512]{2,1,0:T(8,128)S(1)} async-done(((f32[4,128,512]{2,1,0:T(8,128)}), f32[4,128,512]{2,1,0:T(8,128)S(1)}, u32[]{:S(2)}, u32[]{:S(2)}) %all-to-all-start.2) | async-done | bytes 1048608 | tf_op jit(solution)/shard_map/all_to_all | solution.py:62
  107.7 73.0 %while.39 = (s32[]{:T(128)}, bf16[128,512]{1,0:T(8,128)(2,1)S(1)}, f32[128]{0:T(128)S(1)}, f32[128]{0:T(128)S(1)}, f32[128]{0:T(128)S(1)}, /*index=5*/f32[128]{0...) while((s32[]{:T(128)}, bf16[128,512]{1,0:T(8,128)(2,1)S(1)}, ...), condition=%wide.region_10.11_spmd.clone, body=%wide.region_5.10_spmd.clone.sunk | while | flops 16892800 | bytes 1197292 | solution.py:87
  121.9 4.6 %collective-permute-done.1 = f32[128]{0:T(128)S(1)} collective-permute-done((f32[128]{0:T(128)S(1)}, f32[128]{0:T(128)S(1)}, u32[]{:S(2)}, u32[]{:S(2)}) %collective-permute-start.1) | collective-permute-done | bytes 544 | tf_op jit(solution)/shard_map/while/body/eval_jaxpr/ppermute | solution.py:13
  130.1 5.2 %collective-permute-done.1 = f32[128]{0:T(128)S(1)} collective-permute-done((f32[128]{0:T(128)S(1)}, f32[128]{0:T(128)S(1)}, u32[]{:S(2)}, u32[]{:S(2)}) %collective-permute-start.1) | collective-permute-done | bytes 544 | tf_op jit(solution)/shard_map/while/body/eval_jaxpr/ppermute | solution.py:13
  139.2 5.9 %collective-permute-done.1 = f32[128]{0:T(128)S(1)} collective-permute-done((f32[128]{0:T(128)S(1)}, f32[128]{0:T(128)S(1)}, u32[]{:S(2)}, u32[]{:S(2)}) %collective-permute-start.1) | collective-permute-done | bytes 544 | tf_op jit(solution)/shard_map/while/body/eval_jaxpr/ppermute | solution.py:13
  148.1 5.8 %collective-permute-done.1 = f32[128]{0:T(128)S(1)} collective-permute-done((f32[128]{0:T(128)S(1)}, f32[128]{0:T(128)S(1)}, u32[]{:S(2)}, u32[]{:S(2)}) %collective-permute-start.1) | collective-permute-done | bytes 544 | tf_op jit(solution)/shard_map/while/body/eval_jaxpr/ppermute | solution.py:13
  156.9 5.2 %collective-permute-done.1 = f32[128]{0:T(128)S(1)} collective-permute-done((f32[128]{0:T(128)S(1)}, f32[128]{0:T(128)S(1)}, u32[]{:S(2)}, u32[]{:S(2)}) %collective-permute-start.1) | collective-permute-done | bytes 544 | tf_op jit(solution)/shard_map/while/body/eval_jaxpr/ppermute | solution.py:13
  165.7 5.2 %collective-permute-done.1 = f32[128]{0:T(128)S(1)} collective-permute-done((f32[128]{0:T(128)S(1)}, f32[128]{0:T(128)S(1)}, u32[]{:S(2)}, u32[]{:S(2)}) %collective-permute-start.1) | collective-permute-done | bytes 544 | tf_op jit(solution)/shard_map/while/body/eval_jaxpr/ppermute | solution.py:13
  174.8 5.1 %collective-permute-done.1 = f32[128]{0:T(128)S(1)} collective-permute-done((f32[128]{0:T(128)S(1)}, f32[128]{0:T(128)S(1)}, u32[]{:S(2)}, u32[]{:S(2)}) %collective-permute-start.1) | collective-permute-done | bytes 544 | tf_op jit(solution)/shard_map/while/body/eval_jaxpr/ppermute | solution.py:13
  180.7 101.8 %while.40 = (s32[]{:T(128)}, bf16[128,512]{1,0:T(8,128)(2,1)S(1)}, f32[128]{0:T(128)S(1)}, f32[128,512]{1,0:T(8,128)S(1)}, f32[128,512]{1,0:T(8,128)S(1)}, /*ind...) while((s32[]{:T(128)}, bf16[128,512]{1,0:T(8,128)(2,1)S(1)}, ...), condition=%wide.region_12.13_spmd.clone, body=%wide.region_11.12_spmd.clone.sunk | while | flops 50806788 | bytes 3510548 | solution.py:117
  185.1 9.1 %collective-permute-done.4 = f32[128]{0:T(128)S(1)} collective-permute-done((f32[128]{0:T(128)S(1)}, f32[128]{0:T(128)S(1)}, u32[]{:S(2)}, u32[]{:S(2)}) %collective-permute-start.4) | collective-permute-done | bytes 544 | tf_op jit(solution)/shard_map/while/body/eval_jaxpr/ppermute | solution.py:13
  197.0 9.7 %collective-permute-done.4 = f32[128]{0:T(128)S(1)} collective-permute-done((f32[128]{0:T(128)S(1)}, f32[128]{0:T(128)S(1)}, u32[]{:S(2)}, u32[]{:S(2)}) %collective-permute-start.4) | collective-permute-done | bytes 544 | tf_op jit(solution)/shard_map/while/body/eval_jaxpr/ppermute | solution.py:13
  209.5 9.5 %collective-permute-done.4 = f32[128]{0:T(128)S(1)} collective-permute-done((f32[128]{0:T(128)S(1)}, f32[128]{0:T(128)S(1)}, u32[]{:S(2)}, u32[]{:S(2)}) %collective-permute-start.4) | collective-permute-done | bytes 544 | tf_op jit(solution)/shard_map/while/body/eval_jaxpr/ppermute | solution.py:13
  221.9 9.5 %collective-permute-done.4 = f32[128]{0:T(128)S(1)} collective-permute-done((f32[128]{0:T(128)S(1)}, f32[128]{0:T(128)S(1)}, u32[]{:S(2)}, u32[]{:S(2)}) %collective-permute-start.4) | collective-permute-done | bytes 544 | tf_op jit(solution)/shard_map/while/body/eval_jaxpr/ppermute | solution.py:13
  234.2 9.8 %collective-permute-done.4 = f32[128]{0:T(128)S(1)} collective-permute-done((f32[128]{0:T(128)S(1)}, f32[128]{0:T(128)S(1)}, u32[]{:S(2)}, u32[]{:S(2)}) %collective-permute-start.4) | collective-permute-done | bytes 544 | tf_op jit(solution)/shard_map/while/body/eval_jaxpr/ppermute | solution.py:13
  246.9 10.9 %collective-permute-done.4 = f32[128]{0:T(128)S(1)} collective-permute-done((f32[128]{0:T(128)S(1)}, f32[128]{0:T(128)S(1)}, u32[]{:S(2)}, u32[]{:S(2)}) %collective-permute-start.4) | collective-permute-done | bytes 544 | tf_op jit(solution)/shard_map/while/body/eval_jaxpr/ppermute | solution.py:13
  260.6 9.5 %collective-permute-done.4 = f32[128]{0:T(128)S(1)} collective-permute-done((f32[128]{0:T(128)S(1)}, f32[128]{0:T(128)S(1)}, u32[]{:S(2)}, u32[]{:S(2)}) %collective-permute-start.4) | collective-permute-done | bytes 544 | tf_op jit(solution)/shard_map/while/body/eval_jaxpr/ppermute | solution.py:13
  273.0 9.5 %collective-permute-done.4 = f32[128]{0:T(128)S(1)} collective-permute-done((f32[128]{0:T(128)S(1)}, f32[128]{0:T(128)S(1)}, u32[]{:S(2)}, u32[]{:S(2)}) %collective-permute-start.4) | collective-permute-done | bytes 544 | tf_op jit(solution)/shard_map/while/body/eval_jaxpr/ppermute | solution.py:13
  (239 shorter events, 76.0 us)
Async XLA Ops:
  15.5 21.2 %all-to-all-start = ((s32[4,1,512]{2,1,0:T(1,128)}), s32[4,1,512]{2,1,0:T(1,128)S(1)}, u32[]{:S(2)}, u32[]{:S(2)}) async-start(s32[4,1,512]{2,1,0:T(1,128)} %compare_select_fusion.1), calls=%async_computation | async-start | bytes 16384 | tf_op jit(solution)/shard_map/all_to_all | solution.py:59
  36.7 41.7 %all-to-all-start.1 = ((bf16[4,512,768]{2,1,0:T(8,128)(2,1)}), bf16[4,512,768]{2,1,0:T(8,128)(2,1)}, u32[]{:S(2)}, u32[]{:S(2)}) async-start(bf16[4,512,768]{2,1,0:T(8,128)(2,1)} %broadcast_select_fusion.2), calls=%async_computation.1 | async-start | bytes 6291456 | tf_op jit(solution)/shard_map/all_to_all | solution.py:54
  89.3 18.0 %all-to-all-start.2 = ((f32[4,128,512]{2,1,0:T(8,128)}), f32[4,128,512]{2,1,0:T(8,128)S(1)}, u32[]{:S(2)}, u32[]{:S(2)}) async-start(f32[4,128,512]{2,1,0:T(8,128)} %fusion.17), calls=%async_computation.2 | async-start | bytes 2097152 | tf_op jit(solution)/shard_map/all_to_all | solution.py:62
  107.7 11.0 %collective-permute-start = (bf16[128,512]{1,0:T(8,128)(2,1)S(1)}, bf16[128,512]{1,0:T(8,128)(2,1)S(1)}, u32[]{:S(2)}, u32[]{:S(2)}) collective-permute-start(bf16[128,512]{1,0:T(8,128)(2,1)S(1)} %copy.25), channel_id=1, source_target_pairs={{28,0},{0,4},{4,8},{8,12},{12,16},{16,20},{20,24},{24,28},{29,1},{... | collective-permute-start | bytes 393224 | tf_op jit(solution)/shard_map/while/body/eval_jaxpr/ppermute | solution.py:13
  182.5 11.7 %collective-permute-start.5 = (f32[128,512]{1,0:T(8,128)S(1)}, f32[128,512]{1,0:T(8,128)S(1)}, u32[]{:S(2)}, u32[]{:S(2)}) collective-permute-start(f32[128,512]{1,0:T(8,128)S(1)} %fusion.78), channel_id=1, source_target_pairs={{28,0},{0,4},{4,8},{8,12},{12,16},{16,20},{20,24},{24,28},{29,1},{... | collective-permute-start | bytes 786440 | tf_op jit(solution)/shard_map/while/body/eval_jaxpr/ppermute | solution.py:13
  182.5 11.7 %collective-permute-start.3 = (bf16[128,512]{1,0:T(8,128)(2,1)S(1)}, bf16[128,512]{1,0:T(8,128)(2,1)S(1)}, u32[]{:S(2)}, u32[]{:S(2)}) collective-permute-start(bf16[128,512]{1,0:T(8,128)(2,1)S(1)} %copy.42), channel_id=1, source_target_pairs={{28,0},{0,4},{4,8},{8,12},{12,16},{16,20},{20,24},{24,28},{29,1},{... | collective-permute-start | bytes 393224 | tf_op jit(solution)/shard_map/while/body/eval_jaxpr/ppermute | solution.py:13
  196.0 10.8 %collective-permute-start.5 = (f32[128,512]{1,0:T(8,128)S(1)}, f32[128,512]{1,0:T(8,128)S(1)}, u32[]{:S(2)}, u32[]{:S(2)}) collective-permute-start(f32[128,512]{1,0:T(8,128)S(1)} %fusion.78), channel_id=1, source_target_pairs={{28,0},{0,4},{4,8},{8,12},{12,16},{16,20},{20,24},{24,28},{29,1},{... | collective-permute-start | bytes 786440 | tf_op jit(solution)/shard_map/while/body/eval_jaxpr/ppermute | solution.py:13
  196.0 10.7 %collective-permute-start.3 = (bf16[128,512]{1,0:T(8,128)(2,1)S(1)}, bf16[128,512]{1,0:T(8,128)(2,1)S(1)}, u32[]{:S(2)}, u32[]{:S(2)}) collective-permute-start(bf16[128,512]{1,0:T(8,128)(2,1)S(1)} %copy.42), channel_id=1, source_target_pairs={{28,0},{0,4},{4,8},{8,12},{12,16},{16,20},{20,24},{24,28},{29,1},{... | collective-permute-start | bytes 393224 | tf_op jit(solution)/shard_map/while/body/eval_jaxpr/ppermute | solution.py:13
  196.1 10.6 %collective-permute-start.4 = (f32[128]{0:T(128)S(1)}, f32[128]{0:T(128)S(1)}, u32[]{:S(2)}, u32[]{:S(2)}) collective-permute-start(f32[128]{0:T(128)S(1)} %copy.43), channel_id=1, source_target_pairs={{28,0},{0,4},{4,8},{8,12},{12,16},{16,20},{20,24},{24,28},{29,1},{... | collective-permute-start | bytes 1544 | tf_op jit(solution)/shard_map/while/body/eval_jaxpr/ppermute | solution.py:13
  208.5 10.6 %collective-permute-start.5 = (f32[128,512]{1,0:T(8,128)S(1)}, f32[128,512]{1,0:T(8,128)S(1)}, u32[]{:S(2)}, u32[]{:S(2)}) collective-permute-start(f32[128,512]{1,0:T(8,128)S(1)} %fusion.78), channel_id=1, source_target_pairs={{28,0},{0,4},{4,8},{8,12},{12,16},{16,20},{20,24},{24,28},{29,1},{... | collective-permute-start | bytes 786440 | tf_op jit(solution)/shard_map/while/body/eval_jaxpr/ppermute | solution.py:13
  208.5 10.5 %collective-permute-start.3 = (bf16[128,512]{1,0:T(8,128)(2,1)S(1)}, bf16[128,512]{1,0:T(8,128)(2,1)S(1)}, u32[]{:S(2)}, u32[]{:S(2)}) collective-permute-start(bf16[128,512]{1,0:T(8,128)(2,1)S(1)} %copy.42), channel_id=1, source_target_pairs={{28,0},{0,4},{4,8},{8,12},{12,16},{16,20},{20,24},{24,28},{29,1},{... | collective-permute-start | bytes 393224 | tf_op jit(solution)/shard_map/while/body/eval_jaxpr/ppermute | solution.py:13
  208.6 10.5 %collective-permute-start.4 = (f32[128]{0:T(128)S(1)}, f32[128]{0:T(128)S(1)}, u32[]{:S(2)}, u32[]{:S(2)}) collective-permute-start(f32[128]{0:T(128)S(1)} %copy.43), channel_id=1, source_target_pairs={{28,0},{0,4},{4,8},{8,12},{12,16},{16,20},{20,24},{24,28},{29,1},{... | collective-permute-start | bytes 1544 | tf_op jit(solution)/shard_map/while/body/eval_jaxpr/ppermute | solution.py:13
  220.8 10.6 %collective-permute-start.5 = (f32[128,512]{1,0:T(8,128)S(1)}, f32[128,512]{1,0:T(8,128)S(1)}, u32[]{:S(2)}, u32[]{:S(2)}) collective-permute-start(f32[128,512]{1,0:T(8,128)S(1)} %fusion.78), channel_id=1, source_target_pairs={{28,0},{0,4},{4,8},{8,12},{12,16},{16,20},{20,24},{24,28},{29,1},{... | collective-permute-start | bytes 786440 | tf_op jit(solution)/shard_map/while/body/eval_jaxpr/ppermute | solution.py:13
  220.9 10.5 %collective-permute-start.3 = (bf16[128,512]{1,0:T(8,128)(2,1)S(1)}, bf16[128,512]{1,0:T(8,128)(2,1)S(1)}, u32[]{:S(2)}, u32[]{:S(2)}) collective-permute-start(bf16[128,512]{1,0:T(8,128)(2,1)S(1)} %copy.42), channel_id=1, source_target_pairs={{28,0},{0,4},{4,8},{8,12},{12,16},{16,20},{20,24},{24,28},{29,1},{... | collective-permute-start | bytes 393224 | tf_op jit(solution)/shard_map/while/body/eval_jaxpr/ppermute | solution.py:13
  233.2 10.9 %collective-permute-start.5 = (f32[128,512]{1,0:T(8,128)S(1)}, f32[128,512]{1,0:T(8,128)S(1)}, u32[]{:S(2)}, u32[]{:S(2)}) collective-permute-start(f32[128,512]{1,0:T(8,128)S(1)} %fusion.78), channel_id=1, source_target_pairs={{28,0},{0,4},{4,8},{8,12},{12,16},{16,20},{20,24},{24,28},{29,1},{... | collective-permute-start | bytes 786440 | tf_op jit(solution)/shard_map/while/body/eval_jaxpr/ppermute | solution.py:13
  233.2 10.8 %collective-permute-start.3 = (bf16[128,512]{1,0:T(8,128)(2,1)S(1)}, bf16[128,512]{1,0:T(8,128)(2,1)S(1)}, u32[]{:S(2)}, u32[]{:S(2)}) collective-permute-start(bf16[128,512]{1,0:T(8,128)(2,1)S(1)} %copy.42), channel_id=1, source_target_pairs={{28,0},{0,4},{4,8},{8,12},{12,16},{16,20},{20,24},{24,28},{29,1},{... | collective-permute-start | bytes 393224 | tf_op jit(solution)/shard_map/while/body/eval_jaxpr/ppermute | solution.py:13
  233.3 10.8 %collective-permute-start.4 = (f32[128]{0:T(128)S(1)}, f32[128]{0:T(128)S(1)}, u32[]{:S(2)}, u32[]{:S(2)}) collective-permute-start(f32[128]{0:T(128)S(1)} %copy.43), channel_id=1, source_target_pairs={{28,0},{0,4},{4,8},{8,12},{12,16},{16,20},{20,24},{24,28},{29,1},{... | collective-permute-start | bytes 1544 | tf_op jit(solution)/shard_map/while/body/eval_jaxpr/ppermute | solution.py:13
  245.8 12.0 %collective-permute-start.5 = (f32[128,512]{1,0:T(8,128)S(1)}, f32[128,512]{1,0:T(8,128)S(1)}, u32[]{:S(2)}, u32[]{:S(2)}) collective-permute-start(f32[128,512]{1,0:T(8,128)S(1)} %fusion.78), channel_id=1, source_target_pairs={{28,0},{0,4},{4,8},{8,12},{12,16},{16,20},{20,24},{24,28},{29,1},{... | collective-permute-start | bytes 786440 | tf_op jit(solution)/shard_map/while/body/eval_jaxpr/ppermute | solution.py:13
  245.9 11.9 %collective-permute-start.3 = (bf16[128,512]{1,0:T(8,128)(2,1)S(1)}, bf16[128,512]{1,0:T(8,128)(2,1)S(1)}, u32[]{:S(2)}, u32[]{:S(2)}) collective-permute-start(bf16[128,512]{1,0:T(8,128)(2,1)S(1)} %copy.42), channel_id=1, source_target_pairs={{28,0},{0,4},{4,8},{8,12},{12,16},{16,20},{20,24},{24,28},{29,1},{... | collective-permute-start | bytes 393224 | tf_op jit(solution)/shard_map/while/body/eval_jaxpr/ppermute | solution.py:13
  246.0 11.8 %collective-permute-start.4 = (f32[128]{0:T(128)S(1)}, f32[128]{0:T(128)S(1)}, u32[]{:S(2)}, u32[]{:S(2)}) collective-permute-start(f32[128]{0:T(128)S(1)} %copy.43), channel_id=1, source_target_pairs={{28,0},{0,4},{4,8},{8,12},{12,16},{16,20},{20,24},{24,28},{29,1},{... | collective-permute-start | bytes 1544 | tf_op jit(solution)/shard_map/while/body/eval_jaxpr/ppermute | solution.py:13
  259.6 10.6 %collective-permute-start.5 = (f32[128,512]{1,0:T(8,128)S(1)}, f32[128,512]{1,0:T(8,128)S(1)}, u32[]{:S(2)}, u32[]{:S(2)}) collective-permute-start(f32[128,512]{1,0:T(8,128)S(1)} %fusion.78), channel_id=1, source_target_pairs={{28,0},{0,4},{4,8},{8,12},{12,16},{16,20},{20,24},{24,28},{29,1},{... | collective-permute-start | bytes 786440 | tf_op jit(solution)/shard_map/while/body/eval_jaxpr/ppermute | solution.py:13
  259.6 10.5 %collective-permute-start.3 = (bf16[128,512]{1,0:T(8,128)(2,1)S(1)}, bf16[128,512]{1,0:T(8,128)(2,1)S(1)}, u32[]{:S(2)}, u32[]{:S(2)}) collective-permute-start(bf16[128,512]{1,0:T(8,128)(2,1)S(1)} %copy.42), channel_id=1, source_target_pairs={{28,0},{0,4},{4,8},{8,12},{12,16},{16,20},{20,24},{24,28},{29,1},{... | collective-permute-start | bytes 393224 | tf_op jit(solution)/shard_map/while/body/eval_jaxpr/ppermute | solution.py:13
  271.9 10.6 %collective-permute-start.5 = (f32[128,512]{1,0:T(8,128)S(1)}, f32[128,512]{1,0:T(8,128)S(1)}, u32[]{:S(2)}, u32[]{:S(2)}) collective-permute-start(f32[128,512]{1,0:T(8,128)S(1)} %fusion.78), channel_id=1, source_target_pairs={{28,0},{0,4},{4,8},{8,12},{12,16},{16,20},{20,24},{24,28},{29,1},{... | collective-permute-start | bytes 786440 | tf_op jit(solution)/shard_map/while/body/eval_jaxpr/ppermute | solution.py:13
  272.0 10.5 %collective-permute-start.3 = (bf16[128,512]{1,0:T(8,128)(2,1)S(1)}, bf16[128,512]{1,0:T(8,128)(2,1)S(1)}, u32[]{:S(2)}, u32[]{:S(2)}) collective-permute-start(bf16[128,512]{1,0:T(8,128)(2,1)S(1)} %copy.42), channel_id=1, source_target_pairs={{28,0},{0,4},{4,8},{8,12},{12,16},{16,20},{20,24},{24,28},{29,1},{... | collective-permute-start | bytes 393224 | tf_op jit(solution)/shard_map/while/body/eval_jaxpr/ppermute | solution.py:13
  (33 other events, 403.2 us)
where the time goes:
time: 285 us
  waiting for transfers between devices  176 us (62%)
  matrix products  38.5 us (14%)
  starting transfers between devices  32.1 us (11%)
  local copies, waits for them, and re-layouts  26.5 us (9%)
  other arithmetic  10 us (4%)
    ppermute x48, waiting for transfers between devices, from_behind(): return lax.ppermute(block, axis, route)  125 us
    all_to_all x1, waiting for transfers between devices, local(): lax.all_to_all(picked, 'dp', split_axis=0, concat_axis=0, tiled=True)  37 us
    ppermute x48, starting transfers between devices, from_behind(): return lax.ppermute(block, axis, route)  19.8 us
    all_to_all x1, waiting for transfers between devices, local(): lax.all_to_all(partial_value, 'dp', split_axis=0, concat_axis=0, tiled=True)  14.1 us
    dot_general x16, matrix products, score_tile(): lax.dot_general(audio_low, text_block, (((1,), (1,)), ((), ())), preferre...  14.1 us
    gather x1, local copies, waits for them, and re-layouts, local(): picked = jnp.take(frames, safe_rows, axis=0)  13.7 us
    gather x1, local copies, waits for them, and re-layouts, local(): slot_clips = jnp.where(is_live, jnp.take(clip_ids, safe_rows), -1)  11.8 us
    dot_general x8, matrix products, grad_step(): lax.dot_general(weights, audio_low, (((0,), (0,)), ((), ())), preferred_e...  6.86 us
  transfers between devices with their start and end apart: 51, of which 25 were waited for; matrix products, arithmetic and copies ran while one was open for 12% of the time, Pallas kernels for 0%

commit v1 on v0

v1 whole, which is shorter than its diff:
```python
import functools
import math

import jax
import jax.numpy as jnp
from jax import lax
from jax.experimental import pallas as pl
from jax.experimental.pallas import tpu as pltpu
from jax.sharding import PartitionSpec as P

epsilon = 1e-06
LOG2E = math.log2(math.e)
F32 = jnp.float32
BF16 = jnp.bfloat16
VMEM = pl.BlockSpec(memory_space=pltpu.VMEM)
SMEM = pl.BlockSpec(memory_space=pltpu.SMEM)
HBM = pl.BlockSpec(memory_space=pl.ANY)
PARAMS = pltpu.CompilerParams(vmem_limit_bytes=40 * 1024 * 1024)


def mm(left, right, left_dim=1, right_dim=0):
    return lax.dot_general(
        left, right, (((left_dim,), (right_dim,)), ((), ())), preferred_element_type=F32
    )


def swap(block, offset):
    count = lax.axis_size("blk")
    return lax.ppermute(block, "blk", [(i ^ offset, i) for i in range(count)])


def text_kernel(captions_ref, low_ref):
    values = captions_ref[...].astype(F32)
    radius = jnp.sqrt(jnp.sum(values * values, axis=1, keepdims=True) + epsilon)
    low_ref[...] = (values / radius).astype(BF16)


def frames_kernel(
    rows, step, lengths_ref, bias_ref, first_ref, second_ref, frames_ref, pooled_ref, low_ref, held, sems
):
    steps = rows // step
    copies = [
        pltpu.make_async_copy(
            frames_ref.at[pl.ds(k * step, step)], held.at[pl.ds(k * step, step)], sems.at[k]
        )
        for k in range(steps)
    ]
    for copy in copies:
        copy.start()
    clips = lengths_ref.shape[1]
    lengths = lengths_ref[...].astype(F32)
    row_id = lax.broadcasted_iota(jnp.int32, (clips, clips), 0)
    col_id = lax.broadcasted_iota(jnp.int32, (clips, clips), 1)
    ends = jnp.sum(jnp.where(col_id <= row_id, lengths, 0.0), axis=1, keepdims=True)
    sizes = jnp.sum(jnp.where(col_id == row_id, lengths, 0.0), axis=1, keepdims=True)
    starts = ends - sizes
    bias = bias_ref[...]
    first = first_ref[...]
    slot = lax.broadcasted_iota(jnp.int32, (clips, step), 1).astype(F32)
    total = jnp.zeros(pooled_ref.shape, F32)
    root = math.sqrt(2.0 / math.pi)
    for k in range(steps):
        copies[k].wait()
        before = mm(held[pl.ds(k * step, step), :], first) + bias
        half = before * 0.5
        inner = before * (root + (root * 0.044715) * (before * before))
        active = (half + half * jnp.tanh(inner)).astype(BF16)
        place = slot + float(k * step)
        onehot = jnp.where((place >= starts) & (place < ends), 1.0, 0.0).astype(BF16)
        total = total + mm(onehot, active)
    high = total.astype(BF16)
    rest = (total - high.astype(F32)).astype(BF16)
    second = second_ref[...]
    pooled = (mm(high, second) + mm(rest, second)) / sizes
    pooled_ref[...] = pooled
    radius = jnp.sqrt(jnp.sum(pooled * pooled, axis=1, keepdims=True) + epsilon)
    low_ref[...] = (pooled / radius).astype(BF16)


def tile_kernel(row_blocks, col_blocks, scale_ref, *refs):
    audio = refs[:row_blocks]
    text = refs[row_blocks : row_blocks + col_blocks]
    grown_ref, row_ref, col_ref = refs[row_blocks + col_blocks :]
    block = audio[0].shape[0]
    factor = scale_ref[0, 0] * LOG2E
    col_sums = [None] * col_blocks
    for r in range(row_blocks):
        rows = audio[r][...]
        partial = None
        for c in range(col_blocks):
            grown = jnp.exp2(mm(rows, text[c][...], 1, 1) * factor)
            grown_ref[pl.ds(r * block, block), pl.ds(c * block, block)] = grown
            down = jnp.sum(grown, axis=0, keepdims=True)
            col_sums[c] = down if r == 0 else col_sums[c] + down
            partial = grown if c == 0 else partial + grown
        row_ref[pl.ds(r, 1), :] = jnp.sum(partial.T, axis=0, keepdims=True)
    for c in range(col_blocks):
        col_ref[pl.ds(c, 1), :] = col_sums[c]


def grad_kernel(row_blocks, col_blocks, *refs):
    refs = list(refs)
    grown_ref, row_ref, col_ref = refs[:3]
    others_row = refs[3 : 3 + row_blocks - 1]
    others_col = refs[2 + row_blocks : 2 + row_blocks + col_blocks - 1]
    at = 1 + row_blocks + col_blocks
    audio = refs[at : at + row_blocks]
    text = refs[at + row_blocks : at + row_blocks + col_blocks]
    outs = refs[at + row_blocks + col_blocks :]
    audio_outs, text_outs = outs[:row_blocks], outs[row_blocks:]
    block = audio[0].shape[0]
    row_inverse = []
    for r in range(row_blocks):
        total = row_ref[pl.ds(r, 1), :]
        for m in range(1, row_blocks):
            total = total + others_row[m - 1][pl.ds(m ^ r, 1), :]
        spread = jnp.broadcast_to(1.0 / total, (block, block))
        row_inverse.append(spread.T)
    col_inverse = []
    for c in range(col_blocks):
        total = col_ref[pl.ds(c, 1), :]
        for m in range(1, col_blocks):
            total = total + others_col[m - 1][pl.ds(m ^ c, 1), :]
        col_inverse.append(1.0 / total)
    weights = [
        [
            (
                grown_ref[pl.ds(r * block, block), pl.ds(c * block, block)]
                * (row_inverse[r] + col_inverse[c])
            ).astype(BF16)
            for c in range(col_blocks)
        ]
        for r in range(row_blocks)
    ]
    for r in reversed(range(row_blocks)):
        total = sum(mm(weights[r][c], text[c][...]) for c in range(col_blocks))
        audio_outs[r][...] = total.astype(audio_outs[r].dtype)
    for c in reversed(range(col_blocks)):
        total = sum(mm(weights[r][c], audio[r][...], 0, 0) for r in range(row_blocks))
        text_outs[c][...] = total.astype(text_outs[c].dtype)


def final_kernel(row_blocks, col_blocks, pair_count, scale_ref, *refs):
    pooled_ref, captions_ref, audio_ref, text_ref = refs[:4]
    audio_parts = refs[4 : 4 + row_blocks]
    text_parts = refs[4 + row_blocks : 4 + row_blocks + col_blocks]
    audio_out, text_out = refs[4 + row_blocks + col_blocks :]
    factor = scale_ref[0, 0] / (2.0 * pair_count)

    def back(values, parts, partner, out):
        total = parts[0][...] - 2.0 * partner.astype(F32)
        for part in parts[1:]:
            total = total + part[...].astype(F32)
        total = total * factor
        radius = jnp.sqrt(jnp.sum(values * values, axis=1, keepdims=True) + epsilon)
        inverse = 1.0 / radius
        unit = values * inverse
        along = jnp.sum(unit * total, axis=1, keepdims=True)
        out[...] = (total - unit * along) * inverse

    back(pooled_ref[...], audio_parts, text_ref[...], audio_out)
    back(captions_ref[...].astype(F32), text_parts, audio_ref[...], text_out)


def local(frames, lengths, routes, w_first, b_first, w_second, captions, logit_scale):
    clips = lengths.shape[0]
    width = w_second.shape[1]
    group = lax.axis_size("blk")
    pair_count = clips * group * lax.axis_size("dp")
    col_blocks = min(4, group)
    row_blocks = group // col_blocks
    live_rows = min(routes.shape[1] * routes.shape[2], frames.shape[0])
    step = min(256, live_rows)
    scale = logit_scale.reshape(1, 1)
    block_low = jax.ShapeDtypeStruct((clips, width), BF16)
    block_full = jax.ShapeDtypeStruct((clips, width), F32)

    text_low = pl.pallas_call(
        text_kernel, out_shape=block_low, in_specs=[VMEM], out_specs=VMEM, compiler_params=PARAMS
    )(captions)
    text = [text_low] + [swap(text_low, c) for c in range(1, col_blocks)]
    pooled, audio_low = pl.pallas_call(
        functools.partial(frames_kernel, live_rows, step),
        out_shape=(block_full, block_low),
        in_specs=[VMEM] * 4 + [HBM],
        out_specs=(VMEM, VMEM),
        scratch_shapes=[
            pltpu.VMEM((live_rows, frames.shape[1]), BF16),
            pltpu.SemaphoreType.DMA((live_rows // step,)),
        ],
        compiler_params=PARAMS,
    )(lengths.reshape(1, clips), b_first.reshape(1, -1), w_first, w_second, frames)
    audio = [audio_low] + [swap(audio_low, col_blocks * r) for r in range(1, row_blocks)]
    grown, row_sum, col_sum = pl.pallas_call(
        functools.partial(tile_kernel, row_blocks, col_blocks),
        out_shape=(
            jax.ShapeDtypeStruct((row_blocks * clips, col_blocks * clips), F32),
            jax.ShapeDtypeStruct((row_blocks, clips), F32),
            jax.ShapeDtypeStruct((col_blocks, clips), F32),
        ),
        in_specs=[SMEM] + [VMEM] * (row_blocks + col_blocks),
        out_specs=(VMEM, VMEM, VMEM),
        compiler_params=PARAMS,
    )(scale, *audio, *text)
    row_others = [swap(row_sum, col_blocks * r) for r in range(1, row_blocks)]
    col_others = [swap(col_sum, c) for c in range(1, col_blocks)]
    parts = pl.pallas_call(
        functools.partial(grad_kernel, row_blocks, col_blocks),
        out_shape=[block_full if r == 0 else block_low for r in range(row_blocks)]
        + [block_full if c == 0 else block_low for c in range(col_blocks)],
        in_specs=[VMEM] * (1 + 2 * (row_blocks + col_blocks)),
        out_specs=[VMEM] * (row_blocks + col_blocks),
        compiler_params=PARAMS,
    )(grown, row_sum, col_sum, *row_others, *col_others, *audio, *text)
    audio_parts = [parts[0]] + [swap(parts[r], col_blocks * r) for r in range(1, row_blocks)]
    text_parts = [parts[row_blocks]] + [
        swap(parts[row_blocks + c], c) for c in range(1, col_blocks)
    ]
    return pl.pallas_call(
        functools.partial(final_kernel, row_blocks, col_blocks, pair_count),
        out_shape=(block_full, block_full),
        in_specs=[SMEM] + [VMEM] * (4 + row_blocks + col_blocks),
        out_specs=(VMEM, VMEM),
        compiler_params=PARAMS,
    )(scale, pooled, captions, audio_low, text_low, *audio_parts, *text_parts)


def solution(mesh):
    rows = P(("blk", "dp"))
    return jax.shard_map(
        local,
        mesh=mesh,
        in_specs=(rows, rows, rows, P(), P(), P(), rows, P()),
        out_specs=(rows, rows),
        check_vma=False,
    )
```

time: 285 us -> 49.8 us (0.17)
  waiting for transfers between devices: 176 us -> 12.9 us
  matrix products: 38.5 us -> 0 us
  local copies, waits for them, and re-layouts: 26.5 us -> 7.19 us
  starting transfers between devices: 32.1 us -> 19.1 us
  other arithmetic: 10 us -> 0 us
  Pallas kernels: 0 us -> 8.92 us
    ppermute x48 -> x12, waiting for transfers between devices: 125 us -> 12.9 us  [swap(): return lax.ppermute(block, 'blk', [(i ^ offset, i) for i in range(count)])]
    all_to_all x3 -> x0, waiting for transfers between devices: 51.1 us -> none  [the longest x1 37 us: local(): lax.all_to_all(picked, 'dp', split_axis=0, concat_axis=0, tiled=True)]
    dot_general x34 -> x0, matrix products: 38.5 us -> none  [the longest x16 14.1 us: score_tile(): lax.dot_general(audio_low, text_block, (((1,), (1,)), ((), ())), preferre...]
    gather x2 -> x0, local copies, waits for them, and re-layouts: 25.5 us -> none  [the longest x1 13.7 us: local(): picked = jnp.take(frames, safe_rows, axis=0)]
    all_to_all x3 -> x0, starting transfers between devices: 12.4 us -> none  [the longest x1 4.64 us: local(): lax.all_to_all(picked, 'dp', split_axis=0, concat_axis=0, tiled=True)]
    pallas_call x0 -> x5, Pallas kernels: none -> 8.92 us  [the longest x1 6.4 us: local(): pl.pallas_call(functools.partial(frames_kernel, live_rows, step), out_sha...]
    unnamed x15 -> x14, local copies, waits for them, and re-layouts: 0.06 us -> 7.19 us
    select_n x2 -> x0, other arithmetic: 3.93 us -> none  [the longest x1 3.31 us: local(): picked = jnp.take(frames, safe_rows, axis=0)]
  transfers between devices with their start and end apart: 51 -> 12, of which waited for: 25 -> 6; matrix products, arithmetic and copies ran while one was open for 12% -> 0% of each run, Pallas kernels for 0% -> 13%
where the time goes in v1:
time: 49.8 us; the launch traced here: 49.5 us
  starting transfers between devices  19.1 us (38%)
  waiting for transfers between devices  12.9 us (26%)
  Pallas kernels  8.92 us (18%)
  local copies, waits for them, and re-layouts  7.19 us (14%)
  between operations  1.35 us (3%)
    ppermute x12, starting transfers between devices, swap(): return lax.ppermute(block, 'blk', [(i ^ offset, i) for i in range(count)])  19.1 us
    ppermute x12, waiting for transfers between devices, swap(): return lax.ppermute(block, 'blk', [(i ^ offset, i) for i in range(count)])  12.9 us
    unnamed x14, local copies, waits for them, and re-layouts  7.19 us
    pallas_call x1, Pallas kernels, local(): pl.pallas_call(functools.partial(frames_kernel, live_rows, step), out_sha...  6.4 us
    pallas_call x1, Pallas kernels, local(): pl.pallas_call(functools.partial(final_kernel, row_blocks, col_blocks, pa...  1.1 us
  transfers between devices with their start and end apart: 12, of which 6 were waited for; matrix products, arithmetic and copies ran while one was open for 0% of the time, Pallas kernels for 13%

profile of v1, /device:TPU:0, one launch (start us, length us, event | category | flops | bytes accessed | tf_op | source)
XLA Modules:
  0.0 49.5 jit_solution(8493963252148808901)
XLA Ops:
  0.6 0.9 %copy-done.3 = bf16[128,512]{1,0:T(8,128)(2,1)S(1)} copy-done((bf16[128,512]{1,0:T(8,128)(2,1)S(1)}, bf16[128,512]{1,0:T(8,128)(2,1)}, u32[]{:S(2)}) %copy-start.3) | copy-done | bytes 131096
  1.7 4.0 %collective-permute-start.3 = (bf16[128,512]{1,0:T(8,128)(2,1)S(1)}, bf16[128,512]{1,0:T(8,128)(2,1)S(1)}, u32[]{:S(2)}, u32[]{:S(2)}) collective-permute-start(bf16[128,512]{1,0:T(8,128)(2,1)S(1)} %shard_map.87.refs_2_.refs_9_.refs_3_), channel_id=1, source_target_pairs={{12,0},{8,4},{4,8},{0,12},{28,16},{24,20},{20,24},{16,28},{13,1},{... | collective-permute-start | bytes 393224 | tf_op jit(solution)/shard_map/ppermute | solution.py:29
  6.4 2.8 %copy-done = bf16[4096,768]{1,0:T(8,128)(2,1)S(1)} copy-done((bf16[4096,768]{1,0:T(8,128)(2,1)S(1)}, bf16[4096,768]{1,0:T(8,128)(2,1)}, u32[]{:S(2)}) %copy-start) | copy-done | bytes 6291480
  9.1 1.1 %copy-done.1 = bf16[768,512]{1,0:T(8,128)(2,1)S(1)} copy-done((bf16[768,512]{1,0:T(8,128)(2,1)S(1)}, bf16[768,512]{1,0:T(8,128)(2,1)}, u32[]{:S(2)}) %copy-start.1) | copy-done | bytes 786456
  10.3 1.0 %copy-done.2 = bf16[512,512]{1,0:T(8,128)(2,1)S(1)} copy-done((bf16[512,512]{1,0:T(8,128)(2,1)S(1)}, bf16[512,512]{1,0:T(8,128)(2,1)}, u32[]{:S(2)}) %copy-start.2) | copy-done | bytes 524312
  11.3 0.7 %copy-done.5 = f32[512]{0:T(512)S(1)} copy-done((f32[512]{0:T(512)S(1)}, f32[512]{0:T(512)}, u32[]{:S(2)}) %copy-start.5) | copy-done | bytes 2072
  12.0 0.7 %copy-done.6 = s32[128]{0:T(128)S(1)} copy-done((s32[128]{0:T(128)S(1)}, s32[128]{0:T(128)}, u32[]{:S(2)}) %copy-start.6) | copy-done | bytes 536
  12.7 6.4 %shard_map.86 = (f32[128,512]{1,0:T(8,128)S(1)}, bf16[128,512]{1,0:T(8,128)(2,1)S(1)}) custom-call(s32[1,128]{1,0:T(1,128)S(1)} %bitcast.6, f32[1,512]{1,0:T(1,128)S(1)} %bitcast.5, bf16[768,512]{1,0:T(8,128)(2,1)S(1)} %copy-done.1, bf16[512,512]{1,0:T(8,128)(2,1)S(1)} %copy-done.2, bf16[4096,768]{1,0:T(8,128)(2,1)S(1)} %copy-done), custom_call_target="tpu_custom_call" | custom-call | tf_op jit(solution)/shard_map/pallas_call | solution.py:182
  19.1 3.0 %collective-permute-start = (bf16[128,512]{1,0:T(8,128)(2,1)S(1)}, bf16[128,512]{1,0:T(8,128)(2,1)S(1)}, u32[]{:S(2)}, u32[]{:S(2)}) collective-permute-start(bf16[128,512]{1,0:T(8,128)(2,1)S(1)} %get-tuple-element.14.refs_0_.refs_7_.refs_2_), channel_id=1, source_target_pairs={{16,0},{20,4},{24,8},{28,12},{0,16},{4,20},{8,24},{12,28},{17,1},{... | collective-permute-start | bytes 393224 | tf_op jit(solution)/shard_map/ppermute | solution.py:29
  22.7 4.8 %collective-permute-done.refs_1_.refs_8_ = bf16[128,512]{1,0:T(8,128)(2,1)S(1)} collective-permute-done((bf16[128,512]{1,0:T(8,128)(2,1)S(1)}, bf16[128,512]{1,0:T(8,128)(2,1)S(1)}, u32[]{:S(2)}, u32[]{:S(2)}) %collective-permute-start) | collective-permute-done | bytes 131104 | tf_op jit(solution)/shard_map/ppermute | solution.py:29
  27.5 0.5 %shard_map.88 = (f32[256,512]{1,0:T(8,128)S(1)}, f32[2,128]{1,0:T(2,128)S(1)}, f32[4,128]{1,0:T(4,128)S(1)}) custom-call(f32[1,1]{1,0:T(1,128)} %bitcast.3.scale_ref, bf16[128,512]{1,0:T(8,128)(2,1)S(1)} %get-tuple-element.14.refs_0_.refs_7_.refs_2_, bf16[128,512]{1,0:T(8,128)(2,1)S(1)} %collective-permute-done.refs_1_.refs_8_, ...), custom_call_target="tpu_custom_call" | custom-call | tf_op jit(solution)/shard_map/pallas_call | solution.py:194
  28.0 1.7 %collective-permute-start.7 = (f32[4,128]{1,0:T(4,128)S(1)}, f32[4,128]{1,0:T(4,128)S(1)}, u32[]{:S(2)}, u32[]{:S(2)}) collective-permute-start(f32[4,128]{1,0:T(4,128)S(1)} %get-tuple-element.17.refs_2_), channel_id=1, source_target_pairs={{12,0},{8,4},{4,8},{0,12},{28,16},{24,20},{20,24},{16,28},{13,1},{... | collective-permute-start | bytes 6152 | tf_op jit(solution)/shard_map/ppermute | solution.py:29
  29.8 1.4 %collective-permute-start.6 = (f32[4,128]{1,0:T(4,128)S(1)}, f32[4,128]{1,0:T(4,128)S(1)}, u32[]{:S(2)}, u32[]{:S(2)}) collective-permute-start(f32[4,128]{1,0:T(4,128)S(1)} %get-tuple-element.17.refs_2_), channel_id=1, source_target_pairs={{8,0},{12,4},{0,8},{4,12},{24,16},{28,20},{16,24},{20,28},{9,1},{1... | collective-permute-start | bytes 6152 | tf_op jit(solution)/shard_map/ppermute | solution.py:29
  31.6 2.2 %collective-permute-start.4 = (f32[2,128]{1,0:T(2,128)S(1)}, f32[2,128]{1,0:T(2,128)S(1)}, u32[]{:S(2)}, u32[]{:S(2)}) collective-permute-start(f32[2,128]{1,0:T(2,128)S(1)} %get-tuple-element.16.refs_1_), channel_id=1, source_target_pairs={{16,0},{20,4},{24,8},{28,12},{0,16},{4,20},{8,24},{12,28},{17,1},{... | collective-permute-start | bytes 3080 | tf_op jit(solution)/shard_map/ppermute | solution.py:29
  33.8 2.3 %collective-permute-done.4.refs_3_ = f32[2,128]{1,0:T(2,128)S(1)} collective-permute-done((f32[2,128]{1,0:T(2,128)S(1)}, f32[2,128]{1,0:T(2,128)S(1)}, u32[]{:S(2)}, u32[]{:S(2)}) %collective-permute-start.4) | collective-permute-done | bytes 1056 | tf_op jit(solution)/shard_map/ppermute | solution.py:29
  36.1 0.8 %shard_map.89 = (f32[128,512]{1,0:T(8,128)S(1)}, bf16[128,512]{1,0:T(8,128)(2,1)S(1)}, f32[128,512]{1,0:T(8,128)S(1)}, bf16[128,512]{1,0:T(8,128)(2,1)S(1)}, bf1...) custom-call(f32[256,512]{1,0:T(8,128)S(1)} %get-tuple-element.15.refs_0_, ...), custom_call_target="tpu_custom_call" | custom-call | tf_op jit(solution)/shard_map/pallas_call | solution.py:207
  36.8 2.3 %collective-permute-start.8 = (bf16[128,512]{1,0:T(8,128)(2,1)S(1)}, bf16[128,512]{1,0:T(8,128)(2,1)S(1)}, u32[]{:S(2)}, u32[]{:S(2)}) collective-permute-start(bf16[128,512]{1,0:T(8,128)(2,1)S(1)} %get-tuple-element.19), channel_id=1, source_target_pairs={{16,0},{20,4},{24,8},{28,12},{0,16},{4,20},{8,24},{12,28},{17,1},{... | collective-permute-start | bytes 393224 | tf_op jit(solution)/shard_map/ppermute | solution.py:29
  39.1 1.4 %collective-permute-start.9 = (bf16[128,512]{1,0:T(8,128)(2,1)S(1)}, bf16[128,512]{1,0:T(8,128)(2,1)S(1)}, u32[]{:S(2)}, u32[]{:S(2)}) collective-permute-start(bf16[128,512]{1,0:T(8,128)(2,1)S(1)} %get-tuple-element.21), channel_id=1, source_target_pairs={{4,0},{0,4},{12,8},{8,12},{20,16},{16,20},{28,24},{24,28},{5,1},{1... | collective-permute-start | bytes 393224 | tf_op jit(solution)/shard_map/ppermute | solution.py:29
  40.5 2.0 %collective-permute-start.10 = (bf16[128,512]{1,0:T(8,128)(2,1)S(1)}, bf16[128,512]{1,0:T(8,128)(2,1)S(1)}, u32[]{:S(2)}, u32[]{:S(2)}) collective-permute-start(bf16[128,512]{1,0:T(8,128)(2,1)S(1)} %get-tuple-element.22), channel_id=1, source_target_pairs={{8,0},{12,4},{0,8},{4,12},{24,16},{28,20},{16,24},{20,28},{9,1},{1... | collective-permute-start | bytes 393224 | tf_op jit(solution)/shard_map/ppermute | solution.py:29
  42.6 0.9 %collective-permute-done.8.refs_5_ = bf16[128,512]{1,0:T(8,128)(2,1)S(1)} collective-permute-done((bf16[128,512]{1,0:T(8,128)(2,1)S(1)}, bf16[128,512]{1,0:T(8,128)(2,1)S(1)}, u32[]{:S(2)}, u32[]{:S(2)}) %collective-permute-start.8) | collective-permute-done | bytes 131104 | tf_op jit(solution)/shard_map/ppermute | solution.py:29
  43.5 1.5 %collective-permute-done.9.refs_7_ = bf16[128,512]{1,0:T(8,128)(2,1)S(1)} collective-permute-done((bf16[128,512]{1,0:T(8,128)(2,1)S(1)}, bf16[128,512]{1,0:T(8,128)(2,1)S(1)}, u32[]{:S(2)}, u32[]{:S(2)}) %collective-permute-start.9) | collective-permute-done | bytes 131104 | tf_op jit(solution)/shard_map/ppermute | solution.py:29
  45.0 1.1 %collective-permute-done.10.refs_8_ = bf16[128,512]{1,0:T(8,128)(2,1)S(1)} collective-permute-done((bf16[128,512]{1,0:T(8,128)(2,1)S(1)}, bf16[128,512]{1,0:T(8,128)(2,1)S(1)}, u32[]{:S(2)}, u32[]{:S(2)}) %collective-permute-start.10) | collective-permute-done | bytes 131104 | tf_op jit(solution)/shard_map/ppermute | solution.py:29
  46.0 2.3 %collective-permute-done.11.refs_9_ = bf16[128,512]{1,0:T(8,128)(2,1)S(1)} collective-permute-done((bf16[128,512]{1,0:T(8,128)(2,1)S(1)}, bf16[128,512]{1,0:T(8,128)(2,1)S(1)}, u32[]{:S(2)}, u32[]{:S(2)}) %collective-permute-start.11) | collective-permute-done | bytes 131104 | tf_op jit(solution)/shard_map/ppermute | solution.py:29
  48.4 1.1 %shard_map.90 = (f32[128,512]{1,0:T(8,128)}, f32[128,512]{1,0:T(8,128)}) custom-call(f32[1,1]{1,0:T(1,128)} %bitcast.4.scale_ref, f32[128,512]{1,0:T(8,128)S(1)} %get-tuple-element.13.refs_0_, bf16[128,512]{1,0:T(8,128)(2,1)S(1)} %copy-done.4, bf16[128,512]{1,0:T(8,128)(2,1)S(1)} %get-tuple-element.14.refs_0_.refs_7_.refs_2_, ...), custom_call_target="tpu_custom_call" | custom-call | tf_op jit(solution)/shard_map/pallas_call | solution.py:219
  (19 shorter events, 1.4 us)
Async XLA Ops:
  0.6 0.9 %copy-start.3 = (bf16[128,512]{1,0:T(8,128)(2,1)S(1)}, bf16[128,512]{1,0:T(8,128)(2,1)}, u32[]{:S(2)}) copy-start(bf16[128,512]{1,0:T(8,128)(2,1)} %refs_1_.1) | copy-start | bytes 393220
  1.5 46.9 %copy-start.4 = (bf16[128,512]{1,0:T(8,128)(2,1)S(1)}, bf16[128,512]{1,0:T(8,128)(2,1)}, u32[]{:S(2)}) copy-start(bf16[128,512]{1,0:T(8,128)(2,1)} %refs_1_.1) | copy-start | bytes 393220
  1.7 21.0 %collective-permute-start.3 = (bf16[128,512]{1,0:T(8,128)(2,1)S(1)}, bf16[128,512]{1,0:T(8,128)(2,1)S(1)}, u32[]{:S(2)}, u32[]{:S(2)}) collective-permute-start(bf16[128,512]{1,0:T(8,128)(2,1)S(1)} %shard_map.87.refs_2_.refs_9_.refs_3_), channel_id=1, source_target_pairs={{12,0},{8,4},{4,8},{0,12},{28,16},{24,20},{20,24},{16,28},{13,1},{... | collective-permute-start | bytes 393224 | tf_op jit(solution)/shard_map/ppermute | solution.py:29
  5.7 17.0 %collective-permute-start.2 = (bf16[128,512]{1,0:T(8,128)(2,1)S(1)}, bf16[128,512]{1,0:T(8,128)(2,1)S(1)}, u32[]{:S(2)}, u32[]{:S(2)}) collective-permute-start(bf16[128,512]{1,0:T(8,128)(2,1)S(1)} %shard_map.87.refs_2_.refs_9_.refs_3_), channel_id=1, source_target_pairs={{8,0},{12,4},{0,8},{4,12},{24,16},{28,20},{16,24},{20,28},{9,1},{1... | collective-permute-start | bytes 393224 | tf_op jit(solution)/shard_map/ppermute | solution.py:29
  6.2 16.5 %collective-permute-start.1 = (bf16[128,512]{1,0:T(8,128)(2,1)S(1)}, bf16[128,512]{1,0:T(8,128)(2,1)S(1)}, u32[]{:S(2)}, u32[]{:S(2)}) collective-permute-start(bf16[128,512]{1,0:T(8,128)(2,1)S(1)} %shard_map.87.refs_2_.refs_9_.refs_3_), channel_id=1, source_target_pairs={{4,0},{0,4},{12,8},{8,12},{20,16},{16,20},{28,24},{24,28},{5,1},{1... | collective-permute-start | bytes 393224 | tf_op jit(solution)/shard_map/ppermute | solution.py:29
  6.4 2.8 %copy-start = (bf16[4096,768]{1,0:T(8,128)(2,1)S(1)}, bf16[4096,768]{1,0:T(8,128)(2,1)}, u32[]{:S(2)}) copy-start(bf16[4096,768]{1,0:T(8,128)(2,1)} %frames_ref.1) | copy-start | bytes 18874372
  9.1 1.1 %copy-start.1 = (bf16[768,512]{1,0:T(8,128)(2,1)S(1)}, bf16[768,512]{1,0:T(8,128)(2,1)}, u32[]{:S(2)}) copy-start(bf16[768,512]{1,0:T(8,128)(2,1)} %first_ref.1) | copy-start | bytes 2359300
  10.3 1.0 %copy-start.2 = (bf16[512,512]{1,0:T(8,128)(2,1)S(1)}, bf16[512,512]{1,0:T(8,128)(2,1)}, u32[]{:S(2)}) copy-start(bf16[512,512]{1,0:T(8,128)(2,1)} %second_ref.1) | copy-start | bytes 1572868
  11.3 0.7 %copy-start.5 = (f32[512]{0:T(512)S(1)}, f32[512]{0:T(512)}, u32[]{:S(2)}) copy-start(f32[512]{0:T(512)} %param.11) | copy-start | bytes 6148
  12.0 0.7 %copy-start.6 = (s32[128]{0:T(128)S(1)}, s32[128]{0:T(128)}, u32[]{:S(2)}) copy-start(s32[128]{0:T(128)} %param.9) | copy-start | bytes 1540
  19.1 8.5 %collective-permute-start = (bf16[128,512]{1,0:T(8,128)(2,1)S(1)}, bf16[128,512]{1,0:T(8,128)(2,1)S(1)}, u32[]{:S(2)}, u32[]{:S(2)}) collective-permute-start(bf16[128,512]{1,0:T(8,128)(2,1)S(1)} %get-tuple-element.14.refs_0_.refs_7_.refs_2_), channel_id=1, source_target_pairs={{16,0},{20,4},{24,8},{28,12},{0,16},{4,20},{8,24},{12,28},{17,1},{... | collective-permute-start | bytes 393224 | tf_op jit(solution)/shard_map/ppermute | solution.py:29
  28.0 8.0 %collective-permute-start.7 = (f32[4,128]{1,0:T(4,128)S(1)}, f32[4,128]{1,0:T(4,128)S(1)}, u32[]{:S(2)}, u32[]{:S(2)}) collective-permute-start(f32[4,128]{1,0:T(4,128)S(1)} %get-tuple-element.17.refs_2_), channel_id=1, source_target_pairs={{12,0},{8,4},{4,8},{0,12},{28,16},{24,20},{20,24},{16,28},{13,1},{... | collective-permute-start | bytes 6152 | tf_op jit(solution)/shard_map/ppermute | solution.py:29
  29.8 6.3 %collective-permute-start.6 = (f32[4,128]{1,0:T(4,128)S(1)}, f32[4,128]{1,0:T(4,128)S(1)}, u32[]{:S(2)}, u32[]{:S(2)}) collective-permute-start(f32[4,128]{1,0:T(4,128)S(1)} %get-tuple-element.17.refs_2_), channel_id=1, source_target_pairs={{8,0},{12,4},{0,8},{4,12},{24,16},{28,20},{16,24},{20,28},{9,1},{1... | collective-permute-start | bytes 6152 | tf_op jit(solution)/shard_map/ppermute | solution.py:29
  31.1 5.0 %collective-permute-start.5 = (f32[4,128]{1,0:T(4,128)S(1)}, f32[4,128]{1,0:T(4,128)S(1)}, u32[]{:S(2)}, u32[]{:S(2)}) collective-permute-start(f32[4,128]{1,0:T(4,128)S(1)} %get-tuple-element.17.refs_2_), channel_id=1, source_target_pairs={{4,0},{0,4},{12,8},{8,12},{20,16},{16,20},{28,24},{24,28},{5,1},{1... | collective-permute-start | bytes 6152 | tf_op jit(solution)/shard_map/ppermute | solution.py:29
  31.6 4.5 %collective-permute-start.4 = (f32[2,128]{1,0:T(2,128)S(1)}, f32[2,128]{1,0:T(2,128)S(1)}, u32[]{:S(2)}, u32[]{:S(2)}) collective-permute-start(f32[2,128]{1,0:T(2,128)S(1)} %get-tuple-element.16.refs_1_), channel_id=1, source_target_pairs={{16,0},{20,4},{24,8},{28,12},{0,16},{4,20},{8,24},{12,28},{17,1},{... | collective-permute-start | bytes 3080 | tf_op jit(solution)/shard_map/ppermute | solution.py:29
  36.8 6.7 %collective-permute-start.8 = (bf16[128,512]{1,0:T(8,128)(2,1)S(1)}, bf16[128,512]{1,0:T(8,128)(2,1)S(1)}, u32[]{:S(2)}, u32[]{:S(2)}) collective-permute-start(bf16[128,512]{1,0:T(8,128)(2,1)S(1)} %get-tuple-element.19), channel_id=1, source_target_pairs={{16,0},{20,4},{24,8},{28,12},{0,16},{4,20},{8,24},{12,28},{17,1},{... | collective-permute-start | bytes 393224 | tf_op jit(solution)/shard_map/ppermute | solution.py:29
  39.1 5.9 %collective-permute-start.9 = (bf16[128,512]{1,0:T(8,128)(2,1)S(1)}, bf16[128,512]{1,0:T(8,128)(2,1)S(1)}, u32[]{:S(2)}, u32[]{:S(2)}) collective-permute-start(bf16[128,512]{1,0:T(8,128)(2,1)S(1)} %get-tuple-element.21), channel_id=1, source_target_pairs={{4,0},{0,4},{12,8},{8,12},{20,16},{16,20},{28,24},{24,28},{5,1},{1... | collective-permute-start | bytes 393224 | tf_op jit(solution)/shard_map/ppermute | solution.py:29
  40.5 5.6 %collective-permute-start.10 = (bf16[128,512]{1,0:T(8,128)(2,1)S(1)}, bf16[128,512]{1,0:T(8,128)(2,1)S(1)}, u32[]{:S(2)}, u32[]{:S(2)}) collective-permute-start(bf16[128,512]{1,0:T(8,128)(2,1)S(1)} %get-tuple-element.22), channel_id=1, source_target_pairs={{8,0},{12,4},{0,8},{4,12},{24,16},{28,20},{16,24},{20,28},{9,1},{1... | collective-permute-start | bytes 393224 | tf_op jit(solution)/shard_map/ppermute | solution.py:29
  42.5 5.9 %collective-permute-start.11 = (bf16[128,512]{1,0:T(8,128)(2,1)S(1)}, bf16[128,512]{1,0:T(8,128)(2,1)S(1)}, u32[]{:S(2)}, u32[]{:S(2)}) collective-permute-start(bf16[128,512]{1,0:T(8,128)(2,1)S(1)} %get-tuple-element.23), channel_id=1, source_target_pairs={{12,0},{8,4},{4,8},{0,12},{28,16},{24,20},{20,24},{16,28},{13,1},{... | collective-permute-start | bytes 393224 | tf_op jit(solution)/shard_map/ppermute | solution.py:29

commit v2 on v1

--- a/solution.py
+++ b/solution.py
@@ -14,7 +14,7 @@
 BF16 = jnp.bfloat16
 VMEM = pl.BlockSpec(memory_space=pltpu.VMEM)
 SMEM = pl.BlockSpec(memory_space=pltpu.SMEM)
-HBM = pl.BlockSpec(memory_space=pl.ANY)
+HBM = pl.BlockSpec(memory_space=pltpu.HBM)
 PARAMS = pltpu.CompilerParams(vmem_limit_bytes=40 * 1024 * 1024)
 
 
@@ -24,57 +24,87 @@
     )
 
 
+def in_hbm(array):
+    return pltpu.with_memory_space_constraint(array, pltpu.HBM)
+
+
 def swap(block, offset):
     count = lax.axis_size("blk")
     return lax.ppermute(block, "blk", [(i ^ offset, i) for i in range(count)])
 
 
-def text_kernel(captions_ref, low_ref):
-    values = captions_ref[...].astype(F32)
-    radius = jnp.sqrt(jnp.sum(values * values, axis=1, keepdims=True) + epsilon)
-    low_ref[...] = (values / radius).astype(BF16)
-
-
-def frames_kernel(
-    rows, step, lengths_ref, bias_ref, first_ref, second_ref, frames_ref, pooled_ref, low_ref, held, sems
-):
-    steps = rows // step
-    copies = [
-        pltpu.make_async_copy(
-            frames_ref.at[pl.ds(k * step, step)], held.at[pl.ds(k * step, step)], sems.at[k]
-        )
-        for k in range(steps)
-    ]
-    for copy in copies:
+def unit_low(values):
+    return values * lax.rsqrt(jnp.sum(values * values, axis=1, keepdims=True) + epsilon)
+
+
+def frames_kernel(chunks, *refs):
+    lengths_hbm, bias_hbm, first_hbm, second_hbm, captions_hbm, frames_hbm = refs[:6]
+    pooled_ref, audio_ref, text_ref = refs[6:9]
+    lengths_ref, bias_ref, first_ref, second_ref, captions_ref, held, sems = refs[9:]
+    copies = []
+    at = 0
+    for k, rows in enumerate(chunks):
+        part = pl.ds(at, rows)
+        copies.append(pltpu.make_async_copy(frames_hbm.at[part], held.at[part], sems.at[k]))
+        at += rows
+    extra = []
+    for k, pair in enumerate(
+        [
+            (first_hbm, first_ref),
+            (lengths_hbm, lengths_ref),
+            (bias_hbm, bias_ref),
+            (captions_hbm, captions_ref),
+            (second_hbm, second_ref),
+        ]
+    ):
+        extra.append(pltpu.make_async_copy(*pair, sems.at[len(chunks) + k]))
+    first_copy, lengths_copy, bias_copy, captions_copy, second_copy = extra
+    for copy in [lengths_copy, first_copy, copies[0], captions_copy, bias_copy, *copies[1:], second_copy]:
         copy.start()
     clips = lengths_ref.shape[1]
+    lengths_copy.wait()
     lengths = lengths_ref[...].astype(F32)
     row_id = lax.broadcasted_iota(jnp.int32, (clips, clips), 0)
     col_id = lax.broadcasted_iota(jnp.int32, (clips, clips), 1)
     ends = jnp.sum(jnp.where(col_id <= row_id, lengths, 0.0), axis=1, keepdims=True)
     sizes = jnp.sum(jnp.where(col_id == row_id, lengths, 0.0), axis=1, keepdims=True)
     starts = ends - sizes
-    bias = bias_ref[...]
-    first = first_ref[...]
-    slot = lax.broadcasted_iota(jnp.int32, (clips, step), 1).astype(F32)
-    total = jnp.zeros(pooled_ref.shape, F32)
+    live = jnp.sum(lengths_ref[...])
+    captions_copy.wait()
+    text_ref[...] = unit_low(captions_ref[...].astype(F32)).astype(BF16)
+    bias_copy.wait()
+    first_copy.wait()
     root = math.sqrt(2.0 / math.pi)
-    for k in range(steps):
-        copies[k].wait()
-        before = mm(held[pl.ds(k * step, step), :], first) + bias
+
+    def pooled_chunk(at, rows):
+        before = mm(held[pl.ds(at, rows), :], first_ref[...]) + bias_ref[...]
         half = before * 0.5
         inner = before * (root + (root * 0.044715) * (before * before))
         active = (half + half * jnp.tanh(inner)).astype(BF16)
-        place = slot + float(k * step)
+        place = lax.broadcasted_iota(jnp.int32, (clips, rows), 1).astype(F32) + float(at)
         onehot = jnp.where((place >= starts) & (place < ends), 1.0, 0.0).astype(BF16)
-        total = total + mm(onehot, active)
+        return mm(onehot, active)
+
+    at = 0
+    for k, rows in enumerate(chunks):
+        copies[k].wait()
+        if k == 0:
+            pooled_ref[...] = pooled_chunk(at, rows)
+        else:
+
+            @pl.when(live > at)
+            def _():
+                pooled_ref[...] += pooled_chunk(at, rows)
+
+        at += rows
+    second_copy.wait()
+    total = pooled_ref[...]
     high = total.astype(BF16)
     rest = (total - high.astype(F32)).astype(BF16)
     second = second_ref[...]
     pooled = (mm(high, second) + mm(rest, second)) / sizes
     pooled_ref[...] = pooled
-    radius = jnp.sqrt(jnp.sum(pooled * pooled, axis=1, keepdims=True) + epsilon)
-    low_ref[...] = (pooled / radius).astype(BF16)
+    audio_ref[...] = unit_low(pooled).astype(BF16)
 
 
 def tile_kernel(row_blocks, col_blocks, scale_ref, *refs):
@@ -170,26 +200,34 @@
     col_blocks = min(4, group)
     row_blocks = group // col_blocks
     live_rows = min(routes.shape[1] * routes.shape[2], frames.shape[0])
-    step = min(256, live_rows)
+    chunks = [live_rows // 2, live_rows // 4]
+    chunks.append(live_rows - sum(chunks))
     scale = logit_scale.reshape(1, 1)
     block_low = jax.ShapeDtypeStruct((clips, width), BF16)
     block_full = jax.ShapeDtypeStruct((clips, width), F32)
 
-    text_low = pl.pallas_call(
-        text_kernel, out_shape=block_low, in_specs=[VMEM], out_specs=VMEM, compiler_params=PARAMS
-    )(captions)
+    pooled, audio_low, text_low = pl.pallas_call(
+        functools.partial(frames_kernel, chunks),
+        out_shape=(block_full, block_low, block_low),
+        in_specs=[HBM] * 6,
+        out_specs=(VMEM, VMEM, VMEM),
+        scratch_shapes=[
+            pltpu.VMEM((1, clips), lengths.dtype),
+            pltpu.VMEM((1, width), F32),
+            pltpu.VMEM(w_first.shape, BF16),
+            pltpu.VMEM(w_second.shape, BF16),
+            pltpu.VMEM((clips, width), BF16),
+            pltpu.VMEM((live_rows, frames.shape[1]), BF16),
+            pltpu.SemaphoreType.DMA((len(chunks) + 5,)),
+        ],
+        compiler_params=PARAMS,
+    )(
+        *map(
+            in_hbm,
+            (lengths.reshape(1, clips), b_first.reshape(1, width), w_first, w_second, captions, frames),
+        )
+    )
     text = [text_low] + [swap(text_low, c) for c in range(1, col_blocks)]
-    pooled, audio_low = pl.pallas_call(
-        functools.partial(frames_kernel, live_rows, step),
-        out_shape=(block_full, block_low),
-        in_specs=[VMEM] * 4 + [HBM],
-        out_specs=(VMEM, VMEM),
-        scratch_shapes=[
-            pltpu.VMEM((live_rows, frames.shape[1]), BF16),
-            pltpu.SemaphoreType.DMA((live_rows // step,)),
-        ],
-        compiler_params=PARAMS,
-    )(lengths.reshape(1, clips), b_first.reshape(1, -1), w_first, w_second, frames)
     audio = [audio_low] + [swap(audio_low, col_blocks * r) for r in range(1, row_blocks)]
     grown, row_sum, col_sum = pl.pallas_call(
         functools.partial(tile_kernel, row_blocks, col_blocks),

time: 49.8 us -> 39.6 us (0.80)
  local copies, waits for them, and re-layouts: 7.19 us -> 0.01 us
  starting transfers between devices: 19.1 us -> 16.8 us
  Pallas kernels: 8.92 us -> 6.76 us
  waiting for transfers between devices: 12.9 us -> 14.6 us
    unnamed x14 -> x2, local copies, waits for them, and re-layouts: 7.19 us -> 0.01 us
    ppermute x12, starting transfers between devices: 19.1 us -> 16.8 us  [swap(): return lax.ppermute(block, 'blk', [(i ^ offset, i) for i in range(count)])]
    pallas_call x2 -> x1, Pallas kernels: 6.53 us -> 4.37 us  [local(): pl.pallas_call(functools.partial(frames_kernel, chunks), out_shape=(block...]
    ppermute x12, waiting for transfers between devices: 12.9 us -> 14.6 us  [swap(): return lax.ppermute(block, 'blk', [(i ^ offset, i) for i in range(count)])]
  transfers between devices with their start and end apart: 12 -> 12, of which waited for: 6 -> 7; matrix products, arithmetic and copies ran while one was open for 0% -> 0% of each run, Pallas kernels for 13% -> 0%
where the time goes in v2:
time: 39.6 us; the launch traced here: 39.5 us
  starting transfers between devices  16.8 us (42%)
  waiting for transfers between devices  14.6 us (37%)
  Pallas kernels  6.76 us (17%)
  between operations  1.32 us (3%)
    ppermute x12, starting transfers between devices, swap(): return lax.ppermute(block, 'blk', [(i ^ offset, i) for i in range(count)])  16.8 us
    ppermute x12, waiting for transfers between devices, swap(): return lax.ppermute(block, 'blk', [(i ^ offset, i) for i in range(count)])  14.6 us
    pallas_call x1, Pallas kernels, local(): pl.pallas_call(functools.partial(frames_kernel, chunks), out_shape=(block...  4.37 us
    pallas_call x1, Pallas kernels, local(): pl.pallas_call(functools.partial(final_kernel, row_blocks, col_blocks, pa...  1.1 us
  transfers between devices with their start and end apart: 12, of which 7 were waited for; matrix products, arithmetic and copies ran while one was open for 0% of the time, Pallas kernels for 0%

profile of v2, /device:TPU:0, one launch (start us, length us, event | category | flops | bytes accessed | tf_op | source)
XLA Modules:
  0.0 39.5 jit_solution(9419371846700383963)
XLA Ops:
  0.6 4.4 %shard_map.86 = (f32[128,512]{1,0:T(8,128)S(1)}, bf16[128,512]{1,0:T(8,128)(2,1)S(1)}, bf16[128,512]{1,0:T(8,128)(2,1)S(1)}) custom-call(s32[1,128]{1,0:T(1,128)} %bitcast.6, f32[1,512]{1,0:T(1,128)} %bitcast.5, bf16[768,512]{1,0:T(8,128)(2,1)} %refs_2_.1, bf16[512,512]{1,0:T(8,128)(2,1)} %refs_3_.1, bf16[128,512]{1,0:T(8,128)(2,1)} %refs_1_.1, ...), custom_call_target="tpu_custom_call" | custom-call | tf_op jit(solution)/shard_map/pallas_call | solution.py:209
  5.0 4.1 %collective-permute-start = (bf16[128,512]{1,0:T(8,128)(2,1)S(1)}, bf16[128,512]{1,0:T(8,128)(2,1)S(1)}, u32[]{:S(2)}, u32[]{:S(2)}) collective-permute-start(bf16[128,512]{1,0:T(8,128)(2,1)S(1)} %get-tuple-element.15.refs_0_.refs_7_.refs_2_), channel_id=1, source_target_pairs={{16,0},{20,4},{24,8},{28,12},{0,16},{4,20},{8,24},{12,28},{17,1},{... | collective-permute-start | bytes 393224 | tf_op jit(solution)/shard_map/ppermute | solution.py:33
  9.1 2.5 %collective-permute-start.3 = (bf16[128,512]{1,0:T(8,128)(2,1)S(1)}, bf16[128,512]{1,0:T(8,128)(2,1)S(1)}, u32[]{:S(2)}, u32[]{:S(2)}) collective-permute-start(bf16[128,512]{1,0:T(8,128)(2,1)S(1)} %get-tuple-element.16.refs_2_.refs_9_.refs_3_), channel_id=1, source_target_pairs={{12,0},{8,4},{4,8},{0,12},{28,16},{24,20},{20,24},{16,28},{13,1},{... | collective-permute-start | bytes 393224 | tf_op jit(solution)/shard_map/ppermute | solution.py:33
  11.6 0.5 %collective-permute-start.2 = (bf16[128,512]{1,0:T(8,128)(2,1)S(1)}, bf16[128,512]{1,0:T(8,128)(2,1)S(1)}, u32[]{:S(2)}, u32[]{:S(2)}) collective-permute-start(bf16[128,512]{1,0:T(8,128)(2,1)S(1)} %get-tuple-element.16.refs_2_.refs_9_.refs_3_), channel_id=1, source_target_pairs={{8,0},{12,4},{0,8},{4,12},{24,16},{28,20},{16,24},{20,28},{9,1},{1... | collective-permute-start | bytes 393224 | tf_op jit(solution)/shard_map/ppermute | solution.py:33
  12.1 0.5 %collective-permute-start.1 = (bf16[128,512]{1,0:T(8,128)(2,1)S(1)}, bf16[128,512]{1,0:T(8,128)(2,1)S(1)}, u32[]{:S(2)}, u32[]{:S(2)}) collective-permute-start(bf16[128,512]{1,0:T(8,128)(2,1)S(1)} %get-tuple-element.16.refs_2_.refs_9_.refs_3_), channel_id=1, source_target_pairs={{4,0},{0,4},{12,8},{8,12},{20,16},{16,20},{28,24},{24,28},{5,1},{1... | collective-permute-start | bytes 393224 | tf_op jit(solution)/shard_map/ppermute | solution.py:33
  13.2 2.3 %collective-permute-done.refs_1_.refs_8_ = bf16[128,512]{1,0:T(8,128)(2,1)S(1)} collective-permute-done((bf16[128,512]{1,0:T(8,128)(2,1)S(1)}, bf16[128,512]{1,0:T(8,128)(2,1)S(1)}, u32[]{:S(2)}, u32[]{:S(2)}) %collective-permute-start) | collective-permute-done | bytes 131104 | tf_op jit(solution)/shard_map/ppermute | solution.py:33
  15.5 2.5 %collective-permute-done.3.refs_5_.refs_12_ = bf16[128,512]{1,0:T(8,128)(2,1)S(1)} collective-permute-done((bf16[128,512]{1,0:T(8,128)(2,1)S(1)}, bf16[128,512]{1,0:T(8,128)(2,1)S(1)}, u32[]{:S(2)}, u32[]{:S(2)}) %collective-permute-start.3) | collective-permute-done | bytes 131104 | tf_op jit(solution)/shard_map/ppermute | solution.py:33
  18.0 1.5 %collective-permute-done.2.refs_4_.refs_11_ = bf16[128,512]{1,0:T(8,128)(2,1)S(1)} collective-permute-done((bf16[128,512]{1,0:T(8,128)(2,1)S(1)}, bf16[128,512]{1,0:T(8,128)(2,1)S(1)}, u32[]{:S(2)}, u32[]{:S(2)}) %collective-permute-start.2) | collective-permute-done | bytes 131104 | tf_op jit(solution)/shard_map/ppermute | solution.py:33
  19.5 0.0 collective-permute-done.1.refs_3_.refs_10_
  19.5 0.5 %shard_map.87 = (f32[256,512]{1,0:T(8,128)S(1)}, f32[2,128]{1,0:T(2,128)S(1)}, f32[4,128]{1,0:T(4,128)S(1)}) custom-call(f32[1,1]{1,0:T(1,128)} %bitcast.3.scale_ref, bf16[128,512]{1,0:T(8,128)(2,1)S(1)} %get-tuple-element.15.refs_0_.refs_7_.refs_2_, bf16[128,512]{1,0:T(8,128)(2,1)S(1)} %collective-permute-done.refs_1_.refs_8_, ...), custom_call_target="tpu_custom_call" | custom-call | tf_op jit(solution)/shard_map/pallas_call | solution.py:232
  20.0 1.5 %collective-permute-start.7 = (f32[4,128]{1,0:T(4,128)S(1)}, f32[4,128]{1,0:T(4,128)S(1)}, u32[]{:S(2)}, u32[]{:S(2)}) collective-permute-start(f32[4,128]{1,0:T(4,128)S(1)} %get-tuple-element.19.refs_2_), channel_id=1, source_target_pairs={{12,0},{8,4},{4,8},{0,12},{28,16},{24,20},{20,24},{16,28},{13,1},{... | collective-permute-start | bytes 6152 | tf_op jit(solution)/shard_map/ppermute | solution.py:33
  21.5 0.6 %collective-permute-start.6 = (f32[4,128]{1,0:T(4,128)S(1)}, f32[4,128]{1,0:T(4,128)S(1)}, u32[]{:S(2)}, u32[]{:S(2)}) collective-permute-start(f32[4,128]{1,0:T(4,128)S(1)} %get-tuple-element.19.refs_2_), channel_id=1, source_target_pairs={{8,0},{12,4},{0,8},{4,12},{24,16},{28,20},{16,24},{20,28},{9,1},{1... | collective-permute-start | bytes 6152 | tf_op jit(solution)/shard_map/ppermute | solution.py:33
  22.1 1.5 %collective-permute-start.5 = (f32[4,128]{1,0:T(4,128)S(1)}, f32[4,128]{1,0:T(4,128)S(1)}, u32[]{:S(2)}, u32[]{:S(2)}) collective-permute-start(f32[4,128]{1,0:T(4,128)S(1)} %get-tuple-element.19.refs_2_), channel_id=1, source_target_pairs={{4,0},{0,4},{12,8},{8,12},{20,16},{16,20},{28,24},{24,28},{5,1},{1... | collective-permute-start | bytes 6152 | tf_op jit(solution)/shard_map/ppermute | solution.py:33
  23.5 1.1 %collective-permute-start.4 = (f32[2,128]{1,0:T(2,128)S(1)}, f32[2,128]{1,0:T(2,128)S(1)}, u32[]{:S(2)}, u32[]{:S(2)}) collective-permute-start(f32[2,128]{1,0:T(2,128)S(1)} %get-tuple-element.18.refs_1_), channel_id=1, source_target_pairs={{16,0},{20,4},{24,8},{28,12},{0,16},{4,20},{8,24},{12,28},{17,1},{... | collective-permute-start | bytes 3080 | tf_op jit(solution)/shard_map/ppermute | solution.py:33
  24.6 3.4 %collective-permute-done.4.refs_3_ = f32[2,128]{1,0:T(2,128)S(1)} collective-permute-done((f32[2,128]{1,0:T(2,128)S(1)}, f32[2,128]{1,0:T(2,128)S(1)}, u32[]{:S(2)}, u32[]{:S(2)}) %collective-permute-start.4) | collective-permute-done | bytes 1056 | tf_op jit(solution)/shard_map/ppermute | solution.py:33
  28.0 0.8 %shard_map.88 = (f32[128,512]{1,0:T(8,128)S(1)}, bf16[128,512]{1,0:T(8,128)(2,1)S(1)}, f32[128,512]{1,0:T(8,128)S(1)}, bf16[128,512]{1,0:T(8,128)(2,1)S(1)}, bf1...) custom-call(f32[256,512]{1,0:T(8,128)S(1)} %get-tuple-element.17.refs_0_, ...), custom_call_target="tpu_custom_call" | custom-call | tf_op jit(solution)/shard_map/pallas_call | solution.py:245
  28.8 1.1 %collective-permute-start.8 = (bf16[128,512]{1,0:T(8,128)(2,1)S(1)}, bf16[128,512]{1,0:T(8,128)(2,1)S(1)}, u32[]{:S(2)}, u32[]{:S(2)}) collective-permute-start(bf16[128,512]{1,0:T(8,128)(2,1)S(1)} %get-tuple-element.21), channel_id=1, source_target_pairs={{16,0},{20,4},{24,8},{28,12},{0,16},{4,20},{8,24},{12,28},{17,1},{... | collective-permute-start | bytes 393224 | tf_op jit(solution)/shard_map/ppermute | solution.py:33
  29.9 0.9 %collective-permute-start.9 = (bf16[128,512]{1,0:T(8,128)(2,1)S(1)}, bf16[128,512]{1,0:T(8,128)(2,1)S(1)}, u32[]{:S(2)}, u32[]{:S(2)}) collective-permute-start(bf16[128,512]{1,0:T(8,128)(2,1)S(1)} %get-tuple-element.23), channel_id=1, source_target_pairs={{4,0},{0,4},{12,8},{8,12},{20,16},{16,20},{28,24},{24,28},{5,1},{1... | collective-permute-start | bytes 393224 | tf_op jit(solution)/shard_map/ppermute | solution.py:33
  30.8 1.7 %collective-permute-start.10 = (bf16[128,512]{1,0:T(8,128)(2,1)S(1)}, bf16[128,512]{1,0:T(8,128)(2,1)S(1)}, u32[]{:S(2)}, u32[]{:S(2)}) collective-permute-start(bf16[128,512]{1,0:T(8,128)(2,1)S(1)} %get-tuple-element.24), channel_id=1, source_target_pairs={{8,0},{12,4},{0,8},{4,12},{24,16},{28,20},{16,24},{20,28},{9,1},{1... | collective-permute-start | bytes 393224 | tf_op jit(solution)/shard_map/ppermute | solution.py:33
  32.5 0.9 %collective-permute-start.11 = (bf16[128,512]{1,0:T(8,128)(2,1)S(1)}, bf16[128,512]{1,0:T(8,128)(2,1)S(1)}, u32[]{:S(2)}, u32[]{:S(2)}) collective-permute-start(bf16[128,512]{1,0:T(8,128)(2,1)S(1)} %get-tuple-element.25), channel_id=1, source_target_pairs={{12,0},{8,4},{4,8},{0,12},{28,16},{24,20},{20,24},{16,28},{13,1},{... | collective-permute-start | bytes 393224 | tf_op jit(solution)/shard_map/ppermute | solution.py:33
  33.4 2.8 %collective-permute-done.8.refs_5_ = bf16[128,512]{1,0:T(8,128)(2,1)S(1)} collective-permute-done((bf16[128,512]{1,0:T(8,128)(2,1)S(1)}, bf16[128,512]{1,0:T(8,128)(2,1)S(1)}, u32[]{:S(2)}, u32[]{:S(2)}) %collective-permute-start.8) | collective-permute-done | bytes 131104 | tf_op jit(solution)/shard_map/ppermute | solution.py:33
  36.3 0.2 collective-permute-done.10.refs_8_
  36.5 1.9 %collective-permute-done.11.refs_9_ = bf16[128,512]{1,0:T(8,128)(2,1)S(1)} collective-permute-done((bf16[128,512]{1,0:T(8,128)(2,1)S(1)}, bf16[128,512]{1,0:T(8,128)(2,1)S(1)}, u32[]{:S(2)}, u32[]{:S(2)}) %collective-permute-start.11) | collective-permute-done | bytes 131104 | tf_op jit(solution)/shard_map/ppermute | solution.py:33
  38.4 1.1 %shard_map.89 = (f32[128,512]{1,0:T(8,128)}, f32[128,512]{1,0:T(8,128)}) custom-call(f32[1,1]{1,0:T(1,128)} %bitcast.4.scale_ref, f32[128,512]{1,0:T(8,128)S(1)} %get-tuple-element.14.refs_0_, bf16[128,512]{1,0:T(8,128)(2,1)S(1)} %copy-done, bf16[128,512]{1,0:T(8,128)(2,1)S(1)} %get-tuple-element.15.refs_0_.refs_7_.refs_2_, ...), custom_call_target="tpu_custom_call" | custom-call | tf_op jit(solution)/shard_map/pallas_call | solution.py:257
  (6 shorter events, 0.0 us)
Async XLA Ops:
  0.6 37.7 %copy-start = (bf16[128,512]{1,0:T(8,128)(2,1)S(1)}, bf16[128,512]{1,0:T(8,128)(2,1)}, u32[]{:S(2)}) copy-start(bf16[128,512]{1,0:T(8,128)(2,1)} %refs_1_.1) | copy-start | bytes 393220
  5.0 10.5 %collective-permute-start = (bf16[128,512]{1,0:T(8,128)(2,1)S(1)}, bf16[128,512]{1,0:T(8,128)(2,1)S(1)}, u32[]{:S(2)}, u32[]{:S(2)}) collective-permute-start(bf16[128,512]{1,0:T(8,128)(2,1)S(1)} %get-tuple-element.15.refs_0_.refs_7_.refs_2_), channel_id=1, source_target_pairs={{16,0},{20,4},{24,8},{28,12},{0,16},{4,20},{8,24},{12,28},{17,1},{... | collective-permute-start | bytes 393224 | tf_op jit(solution)/shard_map/ppermute | solution.py:33
  9.1 8.9 %collective-permute-start.3 = (bf16[128,512]{1,0:T(8,128)(2,1)S(1)}, bf16[128,512]{1,0:T(8,128)(2,1)S(1)}, u32[]{:S(2)}, u32[]{:S(2)}) collective-permute-start(bf16[128,512]{1,0:T(8,128)(2,1)S(1)} %get-tuple-element.16.refs_2_.refs_9_.refs_3_), channel_id=1, source_target_pairs={{12,0},{8,4},{4,8},{0,12},{28,16},{24,20},{20,24},{16,28},{13,1},{... | collective-permute-start | bytes 393224 | tf_op jit(solution)/shard_map/ppermute | solution.py:33
  11.6 7.8 %collective-permute-start.2 = (bf16[128,512]{1,0:T(8,128)(2,1)S(1)}, bf16[128,512]{1,0:T(8,128)(2,1)S(1)}, u32[]{:S(2)}, u32[]{:S(2)}) collective-permute-start(bf16[128,512]{1,0:T(8,128)(2,1)S(1)} %get-tuple-element.16.refs_2_.refs_9_.refs_3_), channel_id=1, source_target_pairs={{8,0},{12,4},{0,8},{4,12},{24,16},{28,20},{16,24},{20,28},{9,1},{1... | collective-permute-start | bytes 393224 | tf_op jit(solution)/shard_map/ppermute | solution.py:33
  12.1 7.4 %collective-permute-start.1 = (bf16[128,512]{1,0:T(8,128)(2,1)S(1)}, bf16[128,512]{1,0:T(8,128)(2,1)S(1)}, u32[]{:S(2)}, u32[]{:S(2)}) collective-permute-start(bf16[128,512]{1,0:T(8,128)(2,1)S(1)} %get-tuple-element.16.refs_2_.refs_9_.refs_3_), channel_id=1, source_target_pairs={{4,0},{0,4},{12,8},{8,12},{20,16},{16,20},{28,24},{24,28},{5,1},{1... | collective-permute-start | bytes 393224 | tf_op jit(solution)/shard_map/ppermute | solution.py:33
  20.0 8.0 %collective-permute-start.7 = (f32[4,128]{1,0:T(4,128)S(1)}, f32[4,128]{1,0:T(4,128)S(1)}, u32[]{:S(2)}, u32[]{:S(2)}) collective-permute-start(f32[4,128]{1,0:T(4,128)S(1)} %get-tuple-element.19.refs_2_), channel_id=1, source_target_pairs={{12,0},{8,4},{4,8},{0,12},{28,16},{24,20},{20,24},{16,28},{13,1},{... | collective-permute-start | bytes 6152 | tf_op jit(solution)/shard_map/ppermute | solution.py:33
  21.5 6.5 %collective-permute-start.6 = (f32[4,128]{1,0:T(4,128)S(1)}, f32[4,128]{1,0:T(4,128)S(1)}, u32[]{:S(2)}, u32[]{:S(2)}) collective-permute-start(f32[4,128]{1,0:T(4,128)S(1)} %get-tuple-element.19.refs_2_), channel_id=1, source_target_pairs={{8,0},{12,4},{0,8},{4,12},{24,16},{28,20},{16,24},{20,28},{9,1},{1... | collective-permute-start | bytes 6152 | tf_op jit(solution)/shard_map/ppermute | solution.py:33
  22.1 5.9 %collective-permute-start.5 = (f32[4,128]{1,0:T(4,128)S(1)}, f32[4,128]{1,0:T(4,128)S(1)}, u32[]{:S(2)}, u32[]{:S(2)}) collective-permute-start(f32[4,128]{1,0:T(4,128)S(1)} %get-tuple-element.19.refs_2_), channel_id=1, source_target_pairs={{4,0},{0,4},{12,8},{8,12},{20,16},{16,20},{28,24},{24,28},{5,1},{1... | collective-permute-start | bytes 6152 | tf_op jit(solution)/shard_map/ppermute | solution.py:33
  23.5 4.5 %collective-permute-start.4 = (f32[2,128]{1,0:T(2,128)S(1)}, f32[2,128]{1,0:T(2,128)S(1)}, u32[]{:S(2)}, u32[]{:S(2)}) collective-permute-start(f32[2,128]{1,0:T(2,128)S(1)} %get-tuple-element.18.refs_1_), channel_id=1, source_target_pairs={{16,0},{20,4},{24,8},{28,12},{0,16},{4,20},{8,24},{12,28},{17,1},{... | collective-permute-start | bytes 3080 | tf_op jit(solution)/shard_map/ppermute | solution.py:33
  28.8 7.4 %collective-permute-start.8 = (bf16[128,512]{1,0:T(8,128)(2,1)S(1)}, bf16[128,512]{1,0:T(8,128)(2,1)S(1)}, u32[]{:S(2)}, u32[]{:S(2)}) collective-permute-start(bf16[128,512]{1,0:T(8,128)(2,1)S(1)} %get-tuple-element.21), channel_id=1, source_target_pairs={{16,0},{20,4},{24,8},{28,12},{0,16},{4,20},{8,24},{12,28},{17,1},{... | collective-permute-start | bytes 393224 | tf_op jit(solution)/shard_map/ppermute | solution.py:33
  29.9 6.3 %collective-permute-start.9 = (bf16[128,512]{1,0:T(8,128)(2,1)S(1)}, bf16[128,512]{1,0:T(8,128)(2,1)S(1)}, u32[]{:S(2)}, u32[]{:S(2)}) collective-permute-start(bf16[128,512]{1,0:T(8,128)(2,1)S(1)} %get-tuple-element.23), channel_id=1, source_target_pairs={{4,0},{0,4},{12,8},{8,12},{20,16},{16,20},{28,24},{24,28},{5,1},{1... | collective-permute-start | bytes 393224 | tf_op jit(solution)/shard_map/ppermute | solution.py:33
  30.8 5.7 %collective-permute-start.10 = (bf16[128,512]{1,0:T(8,128)(2,1)S(1)}, bf16[128,512]{1,0:T(8,128)(2,1)S(1)}, u32[]{:S(2)}, u32[]{:S(2)}) collective-permute-start(bf16[128,512]{1,0:T(8,128)(2,1)S(1)} %get-tuple-element.24), channel_id=1, source_target_pairs={{8,0},{12,4},{0,8},{4,12},{24,16},{28,20},{16,24},{20,28},{9,1},{1... | collective-permute-start | bytes 393224 | tf_op jit(solution)/shard_map/ppermute | solution.py:33
  32.5 5.9 %collective-permute-start.11 = (bf16[128,512]{1,0:T(8,128)(2,1)S(1)}, bf16[128,512]{1,0:T(8,128)(2,1)S(1)}, u32[]{:S(2)}, u32[]{:S(2)}) collective-permute-start(bf16[128,512]{1,0:T(8,128)(2,1)S(1)} %get-tuple-element.25), channel_id=1, source_target_pairs={{12,0},{8,4},{4,8},{0,12},{28,16},{24,20},{20,24},{16,28},{13,1},{... | collective-permute-start | bytes 393224 | tf_op jit(solution)/shard_map/ppermute | solution.py:33

commit v3 on v2

v3 whole, which is shorter than its diff:
```python
import functools
import math

import jax
import jax.numpy as jnp
from jax import lax
from jax.experimental import pallas as pl
from jax.experimental.pallas import tpu as pltpu
from jax.sharding import PartitionSpec as P

epsilon = 1e-06
LOG2E = math.log2(math.e)
F32 = jnp.float32
BF16 = jnp.bfloat16
VMEM = pl.BlockSpec(memory_space=pltpu.VMEM)
SMEM = pl.BlockSpec(memory_space=pltpu.SMEM)
HBM = pl.BlockSpec(memory_space=pltpu.HBM)
PARAMS = pltpu.CompilerParams(vmem_limit_bytes=40 * 1024 * 1024)


def mm(left, right, left_dim=1, right_dim=0):
    return lax.dot_general(
        left, right, (((left_dim,), (right_dim,)), ((), ())), preferred_element_type=F32
    )


def in_hbm(array):
    return pltpu.with_memory_space_constraint(array, pltpu.HBM)


def swap(block, offset):
    count = lax.axis_size("blk")
    return lax.ppermute(block, "blk", [(i ^ offset, i) for i in range(count)])


def merge_kernel(count, offset, own_ref, other_ref, sum_ref):
    sum_ref[...] = own_ref[...]
    for k in range(count):
        sum_ref[pl.ds(k, 1), :] = own_ref[pl.ds(k, 1), :] + other_ref[pl.ds(k ^ offset, 1), :]


def total_sums(sums, count, stride):
    offset = 1
    while True:
        other = swap(sums, offset * stride)
        if 2 * offset >= count:
            return sums, other, offset
        sums = pl.pallas_call(
            functools.partial(merge_kernel, count, offset),
            out_shape=jax.ShapeDtypeStruct(sums.shape, F32),
            in_specs=[VMEM, VMEM],
            out_specs=VMEM,
            compiler_params=PARAMS,
        )(sums, other)
        offset *= 2


def blocks_of(refs, order, block):
    parts = [ref.at[pl.ds(at, block)] for ref in refs for at in range(0, ref.shape[0], block)]
    return [parts[order.index(k)] for k in range(len(parts))]


def unit_low(values):
    return values * lax.rsqrt(jnp.sum(values * values, axis=1, keepdims=True) + epsilon)


def text_kernel(captions_hbm, text_ref, captions_ref, sem):
    copy = pltpu.make_async_copy(captions_hbm, captions_ref, sem)
    copy.start()
    copy.wait()
    text_ref[...] = unit_low(captions_ref[...].astype(F32)).astype(BF16)


def frames_kernel(chunks, *refs):
    lengths_hbm, bias_hbm, first_hbm, second_hbm, frames_hbm, pooled_ref, audio_ref = refs[:7]
    lengths_ref, bias_ref, first_ref, second_ref, held, sems = refs[7:]
    copies = []
    at = 0
    for k, rows in enumerate(chunks):
        part = pl.ds(at, rows)
        copies.append(pltpu.make_async_copy(frames_hbm.at[part], held.at[part], sems.at[k]))
        at += rows
    extra = []
    for k, pair in enumerate(
        [
            (first_hbm, first_ref),
            (lengths_hbm, lengths_ref),
            (bias_hbm, bias_ref),
            (second_hbm, second_ref),
        ]
    ):
        extra.append(pltpu.make_async_copy(*pair, sems.at[len(chunks) + k]))
    first_copy, lengths_copy, bias_copy, second_copy = extra
    for copy in [lengths_copy, first_copy, copies[0], bias_copy, *copies[1:], second_copy]:
        copy.start()
    clips = lengths_ref.shape[1]
    lengths_copy.wait()
    lengths = lengths_ref[...].astype(F32)
    row_id = lax.broadcasted_iota(jnp.int32, (clips, clips), 0)
    col_id = lax.broadcasted_iota(jnp.int32, (clips, clips), 1)
    ends = jnp.sum(jnp.where(col_id <= row_id, lengths, 0.0), axis=1, keepdims=True)
    sizes = jnp.sum(jnp.where(col_id == row_id, lengths, 0.0), axis=1, keepdims=True)
    starts = ends - sizes
    live = jnp.sum(lengths_ref[...])
    bias_copy.wait()
    first_copy.wait()
    root = math.sqrt(2.0 / math.pi)

    def pooled_chunk(at, rows):
        before = mm(held[pl.ds(at, rows), :], first_ref[...]) + bias_ref[...]
        half = before * 0.5
        inner = before * (root + (root * 0.044715) * (before * before))
        active = (half + half * jnp.tanh(inner)).astype(BF16)
        place = lax.broadcasted_iota(jnp.int32, (clips, rows), 1).astype(F32) + float(at)
        onehot = jnp.where((place >= starts) & (place < ends), 1.0, 0.0).astype(BF16)
        return mm(onehot, active)

    at = 0
    for k, rows in enumerate(chunks):
        copies[k].wait()
        if k == 0:
            pooled_ref[...] = pooled_chunk(at, rows)
        else:

            @pl.when(live > at)
            def _():
                pooled_ref[...] += pooled_chunk(at, rows)

        at += rows
    second_copy.wait()
    total = pooled_ref[...]
    high = total.astype(BF16)
    rest = (total - high.astype(F32)).astype(BF16)
    second = second_ref[...]
    pooled = (mm(high, second) + mm(rest, second)) / sizes
    pooled_ref[...] = pooled
    audio_ref[...] = unit_low(pooled).astype(BF16)


def tile_kernel(row_blocks, order, scale_ref, *refs):
    audio = refs[:row_blocks]
    col_blocks = len(order)
    text = blocks_of(refs[row_blocks:-3], order, audio[0].shape[0])
    grown_ref, row_ref, col_ref = refs[-3:]
    block = audio[0].shape[0]
    factor = scale_ref[0, 0] * LOG2E
    row_ref[...] = jnp.zeros(row_ref.shape, F32)
    col_sums = [None] * col_blocks
    for r in range(row_blocks):
        rows = audio[r][...]
        partial = None
        for c in range(col_blocks):
            grown = jnp.exp2(mm(rows, text[c][...], 1, 1) * factor)
            grown_ref[pl.ds(r * block, block), pl.ds(c * block, block)] = grown
            down = jnp.sum(grown, axis=0, keepdims=True)
            col_sums[c] = down if r == 0 else col_sums[c] + down
            partial = grown if c == 0 else partial + grown
        row_ref[pl.ds(r, 1), :] = jnp.sum(partial.T, axis=0, keepdims=True)
    for c in range(col_blocks):
        col_ref[pl.ds(c, 1), :] = col_sums[c]


def grad_kernel(row_blocks, order, row_offset, col_offset, *refs):
    grown_ref, row_ref, row_other, col_ref, col_other = refs[:5]
    col_blocks = len(order)
    outs = refs[len(refs) - row_blocks - col_blocks :]
    audio_outs, text_outs = outs[:row_blocks], outs[row_blocks:]
    audio = refs[5 : 5 + row_blocks]
    block = audio[0].shape[0]
    text = blocks_of(refs[5 + row_blocks : len(refs) - len(outs)], order, block)

    def inverses(own, other, count, offset):
        return [
            1.0 / (own[pl.ds(k, 1), :] + other[pl.ds(k ^ offset, 1), :])
            for k in range(count)
        ]

    row_inverse = [
        jnp.broadcast_to(row, (block, block)).T for row in inverses(row_ref, row_other, row_blocks, row_offset)
    ]
    col_inverse = inverses(col_ref, col_other, col_blocks, col_offset)
    weights = [
        [
            (
                grown_ref[pl.ds(r * block, block), pl.ds(c * block, block)]
                * (row_inverse[r] + col_inverse[c])
            ).astype(BF16)
            for c in range(col_blocks)
        ]
        for r in range(row_blocks)
    ]
    for r in reversed(range(row_blocks)):
        total = sum(mm(weights[r][c], text[c][...]) for c in range(col_blocks))
        audio_outs[r][...] = total.astype(audio_outs[r].dtype)
    for c in reversed(range(col_blocks)):
        total = sum(mm(weights[r][c], audio[r][...], 0, 0) for r in range(row_blocks))
        text_outs[c][...] = total.astype(text_outs[c].dtype)


def final_kernel(pair_count, scale_ref, values_ref, partner_ref, *refs):
    parts, out_ref = refs[:-1], refs[-1]
    values = values_ref[...].astype(F32)
    total = parts[0][...] - 2.0 * partner_ref[...].astype(F32)
    for part in parts[1:]:
        total = total + part[...].astype(F32)
    total = total * (scale_ref[0, 0] / (2.0 * pair_count))
    inverse = lax.rsqrt(jnp.sum(values * values, axis=1, keepdims=True) + epsilon)
    unit = values * inverse
    along = jnp.sum(unit * total, axis=1, keepdims=True)
    out_ref[...] = (total - unit * along) * inverse


def local(frames, lengths, routes, w_first, b_first, w_second, captions, logit_scale):
    clips = lengths.shape[0]
    width = w_second.shape[1]
    group = lax.axis_size("blk")
    pair_count = clips * group * lax.axis_size("dp")
    col_blocks = min(4, group)
    row_blocks = group // col_blocks
    live_rows = min(routes.shape[1] * routes.shape[2], frames.shape[0])
    chunks = [live_rows // 2, live_rows // 4]
    chunks.append(live_rows - sum(chunks))
    scale = logit_scale.reshape(1, 1)
    block_low = jax.ShapeDtypeStruct((clips, width), BF16)
    block_full = jax.ShapeDtypeStruct((clips, width), F32)

    text_low = pl.pallas_call(
        text_kernel,
        out_shape=block_low,
        in_specs=[HBM],
        out_specs=VMEM,
        scratch_shapes=[pltpu.VMEM((clips, width), BF16), pltpu.SemaphoreType.DMA],
        compiler_params=PARAMS,
    )(in_hbm(captions))
    pooled, audio_low = pl.pallas_call(
        functools.partial(frames_kernel, chunks),
        out_shape=(block_full, block_low),
        in_specs=[HBM] * 5,
        out_specs=(VMEM, VMEM),
        scratch_shapes=[
            pltpu.VMEM((1, clips), lengths.dtype),
            pltpu.VMEM((1, width), F32),
            pltpu.VMEM(w_first.shape, BF16),
            pltpu.VMEM(w_second.shape, BF16),
            pltpu.VMEM((live_rows, frames.shape[1]), BF16),
            pltpu.SemaphoreType.DMA((len(chunks) + 4,)),
        ],
        compiler_params=PARAMS,
    )(
        *map(
            in_hbm,
            (lengths.reshape(1, clips), b_first.reshape(1, width), w_first, w_second, frames),
        )
    )
    text, order = [text_low], [0]
    offset = col_blocks // 2
    while offset:
        held = text_low
        if len(text) > 1:
            held, audio_low = lax.optimization_barrier((text, audio_low))
            held = jnp.concatenate(held, axis=0)
        text.append(swap(held, offset))
        order += [k ^ offset for k in order]
        offset //= 2
    audio = [audio_low] + [swap(audio_low, col_blocks * r) for r in range(1, row_blocks)]
    grown, row_sum, col_sum = pl.pallas_call(
        functools.partial(tile_kernel, row_blocks, order),
        out_shape=(
            jax.ShapeDtypeStruct((row_blocks * clips, col_blocks * clips), F32),
            jax.ShapeDtypeStruct((max(row_blocks, 8), clips), F32),
            jax.ShapeDtypeStruct((col_blocks, clips), F32),
        ),
        in_specs=[SMEM] + [VMEM] * (len(audio) + len(text)),
        out_specs=(VMEM, VMEM, VMEM),
        compiler_params=PARAMS,
    )(scale, *audio, *text)
    col_own, col_other, col_offset = total_sums(col_sum, col_blocks, 1)
    row_own, row_other, row_offset = total_sums(row_sum, row_blocks, col_blocks)
    parts = pl.pallas_call(
        functools.partial(grad_kernel, row_blocks, order, row_offset, col_offset),
        out_shape=[block_full if r == 0 else block_low for r in range(row_blocks)]
        + [block_full if c == 0 else block_low for c in range(col_blocks)],
        in_specs=[VMEM] * (5 + len(audio) + len(text)),
        out_specs=[VMEM] * (row_blocks + col_blocks),
        compiler_params=PARAMS,
    )(grown, row_own, row_other, col_own, col_other, *audio, *text)
    audio_parts = [parts[0]] + [swap(parts[r], col_blocks * r) for r in range(1, row_blocks)]
    text_parts = [parts[row_blocks]] + [
        swap(parts[row_blocks + c], c) for c in range(1, col_blocks)
    ]

    def final(values, partner, pieces):
        return pl.pallas_call(
            functools.partial(final_kernel, pair_count),
            out_shape=block_full,
            in_specs=[SMEM] + [VMEM] * (2 + len(pieces)),
            out_specs=VMEM,
            compiler_params=PARAMS,
        )(scale, values, partner, *pieces)

    return final(pooled, text_low, audio_parts), final(captions, audio_low, text_parts)


def solution(mesh):
    rows = P(("blk", "dp"))
    return jax.shard_map(
        local,
        mesh=mesh,
        in_specs=(rows, rows, rows, P(), P(), P(), rows, P()),
        out_specs=(rows, rows),
        check_vma=False,
    )
```

time: 39.6 us -> 38.9 us (0.982)
  starting transfers between devices: 16.8 us -> 14.3 us
  Pallas kernels: 6.76 us -> 8.94 us
  waiting for transfers between devices: 14.6 us -> 13.9 us
    ppermute x12 -> x10, starting transfers between devices: 16.8 us -> 14.3 us  [swap(): return lax.ppermute(block, 'blk', [(i ^ offset, i) for i in range(count)])]
    pallas_call x3 -> x6, Pallas kernels: 2.39 us -> 4.19 us  [the longest x2 1.82 us: final(): pl.pallas_call(functools.partial(final_kernel, pair_count), out_shape=blo...]
    ppermute x12 -> x10, waiting for transfers between devices: 14.6 us -> 13.9 us  [swap(): return lax.ppermute(block, 'blk', [(i ^ offset, i) for i in range(count)])]
  transfers between devices with their start and end apart: 12 -> 10, of which waited for: 7 -> 6; matrix products, arithmetic and copies ran while one was open for 0% -> 0% of each run, Pallas kernels for 0% -> 15%
where the time goes in v3:
time: 38.9 us; the launch traced here: 38.5 us
  starting transfers between devices  14.3 us (37%)
  waiting for transfers between devices  13.9 us (36%)
  Pallas kernels  8.94 us (23%)
  between operations  1.34 us (3%)
    ppermute x10, starting transfers between devices, swap(): return lax.ppermute(block, 'blk', [(i ^ offset, i) for i in range(count)])  14.3 us
    ppermute x10, waiting for transfers between devices, swap(): return lax.ppermute(block, 'blk', [(i ^ offset, i) for i in range(count)])  13.9 us
    pallas_call x1, Pallas kernels, local(): pl.pallas_call(functools.partial(frames_kernel, chunks), out_shape=(block...  4.75 us
    pallas_call x2, Pallas kernels, final(): pl.pallas_call(functools.partial(final_kernel, pair_count), out_shape=blo...  1.82 us
    pallas_call x1, Pallas kernels, local(): pl.pallas_call(text_kernel, out_shape=block_low, in_specs=[HBM], out_spec...  1.09 us
  transfers between devices with their start and end apart: 10, of which 6 were waited for; matrix products, arithmetic and copies ran while one was open for 0% of the time, Pallas kernels for 15%

profile of v3, /device:TPU:0, one launch (start us, length us, event | category | flops | bytes accessed | tf_op | source)
XLA Modules:
  0.0 38.5 jit_solution(3272032041328926407)
XLA Ops:
  0.6 1.1 %shard_map.87.refs_2_.refs_7_.partner_ref = bf16[128,512]{1,0:T(8,128)(2,1)S(1)} custom-call(bf16[128,512]{1,0:T(8,128)(2,1)} %values_ref.1), custom_call_target="tpu_custom_call" | custom-call | tf_op jit(solution)/shard_map/pallas_call | solution.py:227
  1.7 3.1 %collective-permute-start = (bf16[128,512]{1,0:T(8,128)(2,1)S(1)}, bf16[128,512]{1,0:T(8,128)(2,1)S(1)}, u32[]{:S(2)}, u32[]{:S(2)}) collective-permute-start(bf16[128,512]{1,0:T(8,128)(2,1)S(1)} %shard_map.87.refs_2_.refs_7_.partner_ref), channel_id=1, source_target_pairs={{8,0},{12,4},{0,8},{4,12},{24,16},{28,20},{16,24},{20,28},{9,1},{1... | collective-permute-start | bytes 393224 | tf_op jit(solution)/shard_map/ppermute | solution.py:33
  4.8 4.7 %shard_map.86 = (f32[128,512]{1,0:T(8,128)S(1)}, bf16[128,512]{1,0:T(8,128)(2,1)S(1)}) custom-call(s32[1,128]{1,0:T(1,128)} %bitcast.7, f32[1,512]{1,0:T(1,128)} %bitcast.6, bf16[768,512]{1,0:T(8,128)(2,1)} %refs_2_.1, bf16[512,512]{1,0:T(8,128)(2,1)} %refs_3_.1, bf16[4096,768]{1,0:T(8,128)(2,1)} %refs_4_.1), custom_call_target="tpu_custom_call" | custom-call | tf_op jit(solution)/shard_map/pallas_call | solution.py:235
  9.6 0.0 collective-permute-done.refs_3_.refs_8_
  9.6 0.6 %collective-permute-start.2 = (bf16[256,512]{1,0:T(8,128)(2,1)S(1)}, bf16[256,512]{1,0:T(8,128)(2,1)S(1)}, u32[]{:S(2)}, u32[]{:S(2)}) collective-permute-start(bf16[256,512]{1,0:T(8,128)(2,1)S(1)} %pad_maximum_fusion), channel_id=1, source_target_pairs={{4,0},{0,4},{12,8},{8,12},{20,16},{16,20},{28,24},{24,28},{5,1},{1... | collective-permute-start | bytes 786440 | tf_op jit(solution)/shard_map/ppermute | solution.py:33
  10.2 2.6 %collective-permute-start.1 = (bf16[128,512]{1,0:T(8,128)(2,1)S(1)}, bf16[128,512]{1,0:T(8,128)(2,1)S(1)}, u32[]{:S(2)}, u32[]{:S(2)}) collective-permute-start(bf16[128,512]{1,0:T(8,128)(2,1)S(1)} %get-tuple-element.18.refs_0_.refs_5_.partner_ref), channel_id=1, source_target_pairs={{16,0},{20,4},{24,8},{28,12},{0,16},{4,20},{8,24},{12,28},{17,1},{... | collective-permute-start | bytes 393224 | tf_op jit(solution)/shard_map/ppermute | solution.py:33
  13.5 5.1 %collective-permute-done.1.refs_1_.refs_6_ = bf16[128,512]{1,0:T(8,128)(2,1)S(1)} collective-permute-done((bf16[128,512]{1,0:T(8,128)(2,1)S(1)}, bf16[128,512]{1,0:T(8,128)(2,1)S(1)}, u32[]{:S(2)}, u32[]{:S(2)}) %collective-permute-start.1) | collective-permute-done | bytes 131104 | tf_op jit(solution)/shard_map/ppermute | solution.py:33
  18.6 0.5 %shard_map.88 = (f32[256,512]{1,0:T(8,128)S(1)}, f32[8,128]{1,0:T(8,128)S(1)}, f32[4,128]{1,0:T(4,128)S(1)}) custom-call(f32[1,1]{1,0:T(1,128)} %bitcast.3.scale_ref, bf16[128,512]{1,0:T(8,128)(2,1)S(1)} %get-tuple-element.18.refs_0_.refs_5_.partner_ref, bf16[128,512]{1,0:T(8,128)(2,1)S(1)} %collective-permute-done.1.refs_1_.refs_6_, ...), custom_call_target="tpu_custom_call" | custom-call | tf_op jit(solution)/shard_map/pallas_call | solution.py:266
  19.1 0.6 %collective-permute-start.4 = (f32[4,128]{1,0:T(4,128)S(1)}, f32[4,128]{1,0:T(4,128)S(1)}, u32[]{:S(2)}, u32[]{:S(2)}) collective-permute-start(f32[4,128]{1,0:T(4,128)S(1)} %get-tuple-element.23.own_ref), channel_id=1, source_target_pairs={{4,0},{0,4},{12,8},{8,12},{20,16},{16,20},{28,24},{24,28},{5,1},{1... | collective-permute-start | bytes 6152 | tf_op jit(solution)/shard_map/ppermute | solution.py:33
  19.7 1.5 %collective-permute-start.3 = (f32[8,128]{1,0:T(8,128)S(1)}, f32[8,128]{1,0:T(8,128)S(1)}, u32[]{:S(2)}, u32[]{:S(2)}) collective-permute-start(f32[8,128]{1,0:T(8,128)S(1)} %get-tuple-element.22.refs_1_), channel_id=1, source_target_pairs={{16,0},{20,4},{24,8},{28,12},{0,16},{4,20},{8,24},{12,28},{17,1},{... | collective-permute-start | bytes 12296 | tf_op jit(solution)/shard_map/ppermute | solution.py:33
  21.1 1.6 %collective-permute-done.4.other_ref = f32[4,128]{1,0:T(4,128)S(1)} collective-permute-done((f32[4,128]{1,0:T(4,128)S(1)}, f32[4,128]{1,0:T(4,128)S(1)}, u32[]{:S(2)}, u32[]{:S(2)}) %collective-permute-start.4) | collective-permute-done | bytes 2080 | tf_op jit(solution)/shard_map/ppermute | solution.py:33
  22.8 1.0 %collective-permute-start.5 = (f32[4,128]{1,0:T(4,128)S(1)}, f32[4,128]{1,0:T(4,128)S(1)}, u32[]{:S(2)}, u32[]{:S(2)}) collective-permute-start(f32[4,128]{1,0:T(4,128)S(1)} %shard_map.89.refs_3_), channel_id=1, source_target_pairs={{8,0},{12,4},{0,8},{4,12},{24,16},{28,20},{16,24},{20,28},{9,1},{1... | collective-permute-start | bytes 6152 | tf_op jit(solution)/shard_map/ppermute | solution.py:33
  23.8 2.6 %collective-permute-done.5.refs_4_ = f32[4,128]{1,0:T(4,128)S(1)} collective-permute-done((f32[4,128]{1,0:T(4,128)S(1)}, f32[4,128]{1,0:T(4,128)S(1)}, u32[]{:S(2)}, u32[]{:S(2)}) %collective-permute-start.5) | collective-permute-done | bytes 2080 | tf_op jit(solution)/shard_map/ppermute | solution.py:33
  26.4 0.0 collective-permute-done.3.refs_2_
  26.4 0.8 %shard_map.90 = (f32[128,512]{1,0:T(8,128)S(1)}, bf16[128,512]{1,0:T(8,128)(2,1)S(1)}, f32[128,512]{1,0:T(8,128)S(1)}, bf16[128,512]{1,0:T(8,128)(2,1)S(1)}, bf1...) custom-call(f32[256,512]{1,0:T(8,128)S(1)} %get-tuple-element.21.refs_0_, ...), custom_call_target="tpu_custom_call" | custom-call | tf_op jit(solution)/shard_map/pallas_call | solution.py:279
  27.1 1.5 %collective-permute-start.6 = (bf16[128,512]{1,0:T(8,128)(2,1)S(1)}, bf16[128,512]{1,0:T(8,128)(2,1)S(1)}, u32[]{:S(2)}, u32[]{:S(2)}) collective-permute-start(bf16[128,512]{1,0:T(8,128)(2,1)S(1)} %get-tuple-element.25), channel_id=1, source_target_pairs={{16,0},{20,4},{24,8},{28,12},{0,16},{4,20},{8,24},{12,28},{17,1},{... | collective-permute-start | bytes 393224 | tf_op jit(solution)/shard_map/ppermute | solution.py:33
  28.6 1.1 %collective-permute-start.7 = (bf16[128,512]{1,0:T(8,128)(2,1)S(1)}, bf16[128,512]{1,0:T(8,128)(2,1)S(1)}, u32[]{:S(2)}, u32[]{:S(2)}) collective-permute-start(bf16[128,512]{1,0:T(8,128)(2,1)S(1)} %get-tuple-element.27), channel_id=1, source_target_pairs={{4,0},{0,4},{12,8},{8,12},{20,16},{16,20},{28,24},{24,28},{5,1},{1... | collective-permute-start | bytes 393224 | tf_op jit(solution)/shard_map/ppermute | solution.py:33
  29.7 2.0 %collective-permute-start.8 = (bf16[128,512]{1,0:T(8,128)(2,1)S(1)}, bf16[128,512]{1,0:T(8,128)(2,1)S(1)}, u32[]{:S(2)}, u32[]{:S(2)}) collective-permute-start(bf16[128,512]{1,0:T(8,128)(2,1)S(1)} %get-tuple-element.28), channel_id=1, source_target_pairs={{8,0},{12,4},{0,8},{4,12},{24,16},{28,20},{16,24},{20,28},{9,1},{1... | collective-permute-start | bytes 393224 | tf_op jit(solution)/shard_map/ppermute | solution.py:33
  31.7 0.4 %collective-permute-start.9 = (bf16[128,512]{1,0:T(8,128)(2,1)S(1)}, bf16[128,512]{1,0:T(8,128)(2,1)S(1)}, u32[]{:S(2)}, u32[]{:S(2)}) collective-permute-start(bf16[128,512]{1,0:T(8,128)(2,1)S(1)} %get-tuple-element.29), channel_id=1, source_target_pairs={{12,0},{8,4},{4,8},{0,12},{28,16},{24,20},{20,24},{16,28},{13,1},{... | collective-permute-start | bytes 393224 | tf_op jit(solution)/shard_map/ppermute | solution.py:33
  32.1 1.8 %collective-permute-done.6.refs_1_ = bf16[128,512]{1,0:T(8,128)(2,1)S(1)} collective-permute-done((bf16[128,512]{1,0:T(8,128)(2,1)S(1)}, bf16[128,512]{1,0:T(8,128)(2,1)S(1)}, u32[]{:S(2)}, u32[]{:S(2)}) %collective-permute-start.6) | collective-permute-done | bytes 131104 | tf_op jit(solution)/shard_map/ppermute | solution.py:33
  34.0 0.9 %shard_map.91 = f32[128,512]{1,0:T(8,128)} custom-call(f32[1,1]{1,0:T(1,128)} %bitcast.4.scale_ref, f32[128,512]{1,0:T(8,128)S(1)} %get-tuple-element.16.values_ref, bf16[128,512]{1,0:T(8,128)(2,1)S(1)} %shard_map.87.refs_2_.refs_7_.partner_ref, f32[128,512]{1,0:T(8,128)S(1)} %get-tuple-element.24.refs_0_, bf16[128,512]{1,0:T(8,128)(2,1)S(1)} %collective-permute-done.6.refs_1_), custom_call_target="tpu_custom_call" | custom-call | tf_op jit(solution)/shard_map/pallas_call | solution.py:293
  34.9 0.7 %collective-permute-done.8.refs_2_ = bf16[128,512]{1,0:T(8,128)(2,1)S(1)} collective-permute-done((bf16[128,512]{1,0:T(8,128)(2,1)S(1)}, bf16[128,512]{1,0:T(8,128)(2,1)S(1)}, u32[]{:S(2)}, u32[]{:S(2)}) %collective-permute-start.8) | collective-permute-done | bytes 131104 | tf_op jit(solution)/shard_map/ppermute | solution.py:33
  35.5 2.0 %collective-permute-done.9.refs_3_ = bf16[128,512]{1,0:T(8,128)(2,1)S(1)} collective-permute-done((bf16[128,512]{1,0:T(8,128)(2,1)S(1)}, bf16[128,512]{1,0:T(8,128)(2,1)S(1)}, u32[]{:S(2)}, u32[]{:S(2)}) %collective-permute-start.9) | collective-permute-done | bytes 131104 | tf_op jit(solution)/shard_map/ppermute | solution.py:33
  37.6 0.9 %shard_map.92 = f32[128,512]{1,0:T(8,128)} custom-call(f32[1,1]{1,0:T(1,128)} %bitcast.5.scale_ref, bf16[128,512]{1,0:T(8,128)(2,1)S(1)} %copy-done, bf16[128,512]{1,0:T(8,128)(2,1)S(1)} %get-tuple-element.18.refs_0_.refs_5_.partner_ref, f32[128,512]{1,0:T(8,128)S(1)} %get-tuple-element.26.refs_0_, bf16[128,512]{1,0:T(8,128)(2,1)S(1)} %collective-permute-done.7.refs_1_, ...), custom_call_target="tpu_custom_call" | custom-call | tf_op jit(solution)/shard_map/pallas_call | solution.py:293
  (6 shorter events, 0.0 us)
Async XLA Ops:
  0.6 37.0 %copy-start = (bf16[128,512]{1,0:T(8,128)(2,1)S(1)}, bf16[128,512]{1,0:T(8,128)(2,1)}, u32[]{:S(2)}) copy-start(bf16[128,512]{1,0:T(8,128)(2,1)} %values_ref.1) | copy-start | bytes 393220
  1.7 7.8 %collective-permute-start = (bf16[128,512]{1,0:T(8,128)(2,1)S(1)}, bf16[128,512]{1,0:T(8,128)(2,1)S(1)}, u32[]{:S(2)}, u32[]{:S(2)}) collective-permute-start(bf16[128,512]{1,0:T(8,128)(2,1)S(1)} %shard_map.87.refs_2_.refs_7_.partner_ref), channel_id=1, source_target_pairs={{8,0},{12,4},{0,8},{4,12},{24,16},{28,20},{16,24},{20,28},{9,1},{1... | collective-permute-start | bytes 393224 | tf_op jit(solution)/shard_map/ppermute | solution.py:33
  9.6 9.0 %collective-permute-start.2 = (bf16[256,512]{1,0:T(8,128)(2,1)S(1)}, bf16[256,512]{1,0:T(8,128)(2,1)S(1)}, u32[]{:S(2)}, u32[]{:S(2)}) collective-permute-start(bf16[256,512]{1,0:T(8,128)(2,1)S(1)} %pad_maximum_fusion), channel_id=1, source_target_pairs={{4,0},{0,4},{12,8},{8,12},{20,16},{16,20},{28,24},{24,28},{5,1},{1... | collective-permute-start | bytes 786440 | tf_op jit(solution)/shard_map/ppermute | solution.py:33
  10.2 8.4 %collective-permute-start.1 = (bf16[128,512]{1,0:T(8,128)(2,1)S(1)}, bf16[128,512]{1,0:T(8,128)(2,1)S(1)}, u32[]{:S(2)}, u32[]{:S(2)}) collective-permute-start(bf16[128,512]{1,0:T(8,128)(2,1)S(1)} %get-tuple-element.18.refs_0_.refs_5_.partner_ref), channel_id=1, source_target_pairs={{16,0},{20,4},{24,8},{28,12},{0,16},{4,20},{8,24},{12,28},{17,1},{... | collective-permute-start | bytes 393224 | tf_op jit(solution)/shard_map/ppermute | solution.py:33
  19.1 3.7 %collective-permute-start.4 = (f32[4,128]{1,0:T(4,128)S(1)}, f32[4,128]{1,0:T(4,128)S(1)}, u32[]{:S(2)}, u32[]{:S(2)}) collective-permute-start(f32[4,128]{1,0:T(4,128)S(1)} %get-tuple-element.23.own_ref), channel_id=1, source_target_pairs={{4,0},{0,4},{12,8},{8,12},{20,16},{16,20},{28,24},{24,28},{5,1},{1... | collective-permute-start | bytes 6152 | tf_op jit(solution)/shard_map/ppermute | solution.py:33
  19.7 6.7 %collective-permute-start.3 = (f32[8,128]{1,0:T(8,128)S(1)}, f32[8,128]{1,0:T(8,128)S(1)}, u32[]{:S(2)}, u32[]{:S(2)}) collective-permute-start(f32[8,128]{1,0:T(8,128)S(1)} %get-tuple-element.22.refs_1_), channel_id=1, source_target_pairs={{16,0},{20,4},{24,8},{28,12},{0,16},{4,20},{8,24},{12,28},{17,1},{... | collective-permute-start | bytes 12296 | tf_op jit(solution)/shard_map/ppermute | solution.py:33
  22.8 3.6 %collective-permute-start.5 = (f32[4,128]{1,0:T(4,128)S(1)}, f32[4,128]{1,0:T(4,128)S(1)}, u32[]{:S(2)}, u32[]{:S(2)}) collective-permute-start(f32[4,128]{1,0:T(4,128)S(1)} %shard_map.89.refs_3_), channel_id=1, source_target_pairs={{8,0},{12,4},{0,8},{4,12},{24,16},{28,20},{16,24},{20,28},{9,1},{1... | collective-permute-start | bytes 6152 | tf_op jit(solution)/shard_map/ppermute | solution.py:33
  27.1 6.8 %collective-permute-start.6 = (bf16[128,512]{1,0:T(8,128)(2,1)S(1)}, bf16[128,512]{1,0:T(8,128)(2,1)S(1)}, u32[]{:S(2)}, u32[]{:S(2)}) collective-permute-start(bf16[128,512]{1,0:T(8,128)(2,1)S(1)} %get-tuple-element.25), channel_id=1, source_target_pairs={{16,0},{20,4},{24,8},{28,12},{0,16},{4,20},{8,24},{12,28},{17,1},{... | collective-permute-start | bytes 393224 | tf_op jit(solution)/shard_map/ppermute | solution.py:33
  28.6 6.2 %collective-permute-start.7 = (bf16[128,512]{1,0:T(8,128)(2,1)S(1)}, bf16[128,512]{1,0:T(8,128)(2,1)S(1)}, u32[]{:S(2)}, u32[]{:S(2)}) collective-permute-start(bf16[128,512]{1,0:T(8,128)(2,1)S(1)} %get-tuple-element.27), channel_id=1, source_target_pairs={{4,0},{0,4},{12,8},{8,12},{20,16},{16,20},{28,24},{24,28},{5,1},{1... | collective-permute-start | bytes 393224 | tf_op jit(solution)/shard_map/ppermute | solution.py:33
  29.7 5.8 %collective-permute-start.8 = (bf16[128,512]{1,0:T(8,128)(2,1)S(1)}, bf16[128,512]{1,0:T(8,128)(2,1)S(1)}, u32[]{:S(2)}, u32[]{:S(2)}) collective-permute-start(bf16[128,512]{1,0:T(8,128)(2,1)S(1)} %get-tuple-element.28), channel_id=1, source_target_pairs={{8,0},{12,4},{0,8},{4,12},{24,16},{28,20},{16,24},{20,28},{9,1},{1... | collective-permute-start | bytes 393224 | tf_op jit(solution)/shard_map/ppermute | solution.py:33
  31.7 5.9 %collective-permute-start.9 = (bf16[128,512]{1,0:T(8,128)(2,1)S(1)}, bf16[128,512]{1,0:T(8,128)(2,1)S(1)}, u32[]{:S(2)}, u32[]{:S(2)}) collective-permute-start(bf16[128,512]{1,0:T(8,128)(2,1)S(1)} %get-tuple-element.29), channel_id=1, source_target_pairs={{12,0},{8,4},{4,8},{0,12},{28,16},{24,20},{20,24},{16,28},{13,1},{... | collective-permute-start | bytes 393224 | tf_op jit(solution)/shard_map/ppermute | solution.py:33

commit v4 on v3

--- a/solution.py
+++ b/solution.py
@@ -33,31 +33,9 @@
     return lax.ppermute(block, "blk", [(i ^ offset, i) for i in range(count)])
 
 
-def merge_kernel(count, offset, own_ref, other_ref, sum_ref):
-    sum_ref[...] = own_ref[...]
-    for k in range(count):
-        sum_ref[pl.ds(k, 1), :] = own_ref[pl.ds(k, 1), :] + other_ref[pl.ds(k ^ offset, 1), :]
-
-
-def total_sums(sums, count, stride):
-    offset = 1
-    while True:
-        other = swap(sums, offset * stride)
-        if 2 * offset >= count:
-            return sums, other, offset
-        sums = pl.pallas_call(
-            functools.partial(merge_kernel, count, offset),
-            out_shape=jax.ShapeDtypeStruct(sums.shape, F32),
-            in_specs=[VMEM, VMEM],
-            out_specs=VMEM,
-            compiler_params=PARAMS,
-        )(sums, other)
-        offset *= 2
-
-
-def blocks_of(refs, order, block):
+def blocks_of(refs, offsets, block):
     parts = [ref.at[pl.ds(at, block)] for ref in refs for at in range(0, ref.shape[0], block)]
-    return [parts[order.index(k)] for k in range(len(parts))]
+    return dict(zip(offsets, parts, strict=True))
 
 
 def unit_low(values):
@@ -137,64 +115,77 @@
     audio_ref[...] = unit_low(pooled).astype(BF16)
 
 
-def tile_kernel(row_blocks, order, scale_ref, *refs):
-    audio = refs[:row_blocks]
-    col_blocks = len(order)
-    text = blocks_of(refs[row_blocks:-3], order, audio[0].shape[0])
-    grown_ref, row_ref, col_ref = refs[-3:]
-    block = audio[0].shape[0]
+def tile_kernel(rows, columns, scale_ref, *refs):
+    first_refs, last_refs = refs[: len(refs) - 3], refs[len(refs) - 3 :]
+    grown_ref, row_ref, col_ref = last_refs
+    block = row_ref.shape[1]
+    held, at = [], 0
+    for offsets in (rows, columns):
+        taken, count = [], 0
+        while count < len(offsets):
+            taken.append(first_refs[at])
+            count += first_refs[at].shape[0] // block
+            at += 1
+        held.append(blocks_of(taken, offsets, block))
+    audio, text = held
+    col_sums = [first_refs[at][pl.ds(c, 1), :] for c in range(len(columns))] if at < len(first_refs) else None
     factor = scale_ref[0, 0] * LOG2E
-    row_ref[...] = jnp.zeros(row_ref.shape, F32)
-    col_sums = [None] * col_blocks
-    for r in range(row_blocks):
-        rows = audio[r][...]
+    for r, row in enumerate(rows):
+        values = audio[row][...]
         partial = None
-        for c in range(col_blocks):
-            grown = jnp.exp2(mm(rows, text[c][...], 1, 1) * factor)
+        downs = []
+        for c, column in enumerate(columns):
+            grown = jnp.exp2(mm(values, text[column][...], 1, 1) * factor)
             grown_ref[pl.ds(r * block, block), pl.ds(c * block, block)] = grown
-            down = jnp.sum(grown, axis=0, keepdims=True)
-            col_sums[c] = down if r == 0 else col_sums[c] + down
+            downs.append(jnp.sum(grown, axis=0, keepdims=True))
             partial = grown if c == 0 else partial + grown
+        col_sums = downs if col_sums is None else [x + y for x, y in zip(col_sums, downs, strict=True)]
         row_ref[pl.ds(r, 1), :] = jnp.sum(partial.T, axis=0, keepdims=True)
-    for c in range(col_blocks):
+    for c in range(len(columns)):
         col_ref[pl.ds(c, 1), :] = col_sums[c]
 
 
-def grad_kernel(row_blocks, order, row_offset, col_offset, *refs):
-    grown_ref, row_ref, row_other, col_ref, col_other = refs[:5]
-    col_blocks = len(order)
-    outs = refs[len(refs) - row_blocks - col_blocks :]
-    audio_outs, text_outs = outs[:row_blocks], outs[row_blocks:]
-    audio = refs[5 : 5 + row_blocks]
-    block = audio[0].shape[0]
-    text = blocks_of(refs[5 + row_blocks : len(refs) - len(outs)], order, block)
-
-    def inverses(own, other, count, offset):
-        return [
-            1.0 / (own[pl.ds(k, 1), :] + other[pl.ds(k ^ offset, 1), :])
-            for k in range(count)
-        ]
-
-    row_inverse = [
-        jnp.broadcast_to(row, (block, block)).T for row in inverses(row_ref, row_other, row_blocks, row_offset)
-    ]
-    col_inverse = inverses(col_ref, col_other, col_blocks, col_offset)
-    weights = [
-        [
-            (
-                grown_ref[pl.ds(r * block, block), pl.ds(c * block, block)]
-                * (row_inverse[r] + col_inverse[c])
-            ).astype(BF16)
-            for c in range(col_blocks)
-        ]
-        for r in range(row_blocks)
-    ]
-    for r in reversed(range(row_blocks)):
-        total = sum(mm(weights[r][c], text[c][...]) for c in range(col_blocks))
-        audio_outs[r][...] = total.astype(audio_outs[r].dtype)
-    for c in reversed(range(col_blocks)):
-        total = sum(mm(weights[r][c], audio[r][...], 0, 0) for r in range(row_blocks))
-        text_outs[c][...] = total.astype(text_outs[c].dtype)
+def grad_kernel(rows, columns, pick, *refs):
+    block = refs[-1].shape[0]
+    count = len(rows)
+    grown, near = {}, 0
+    held = 0
+    while held < count:
+        for k in range(refs[near].shape[0] // block):
+            for c, column in enumerate(columns):
+                grown[rows[held], column] = (near, k, c)
+            held += 1
+        near += 1
+    row_ref, row_other, col_ref, col_other = refs[near : near + 4]
+    audio_refs, text_refs, at = [], [], near + 4
+    for store, wanted in ((audio_refs, len(rows)), (text_refs, len(columns))):
+        total = 0
+        while total < wanted:
+            store.append(refs[at])
+            total += refs[at].shape[0] // block
+            at += 1
+    audio, text = blocks_of(audio_refs, rows, block), blocks_of(text_refs, columns, block)
+    audio_out, text_out = refs[at:]
+
+    def inverse(offsets, offset, bit, own, other):
+        here, there = (pl.ds(offsets.index(k), 1) for k in (offset, offset ^ bit))
+        return 1.0 / (own[here, :] + other[there, :])
+
+    def row_inverse(row):
+        return jnp.broadcast_to(inverse(rows, row, 1, row_ref, row_other), (block, block)).T
+
+    row_scale = {row: row_inverse(row) for row in rows}
+    col_scale = {column: inverse(columns, column, 2, col_ref, col_other) for column in columns}
+
+    def weights(row, column):
+        index, k, c = grown[row, column]
+        values = refs[index][pl.ds(k * block, block), pl.ds(c * block, block)]
+        return (values * (row_scale[row] + col_scale[column])).astype(BF16)
+
+    total = sum(mm(weights(pick[0], column), text[column][...]) for column in columns)
+    audio_out[...] = total.astype(audio_out.dtype)
+    total = sum(mm(weights(row, pick[1]), audio[row][...], 0, 0) for row in rows)
+    text_out[...] = total.astype(text_out.dtype)
 
 
 def final_kernel(pair_count, scale_ref, values_ref, partner_ref, *refs):
@@ -215,8 +206,7 @@
     width = w_second.shape[1]
     group = lax.axis_size("blk")
     pair_count = clips * group * lax.axis_size("dp")
-    col_blocks = min(4, group)
-    row_blocks = group // col_blocks
+    shared_bits = [1 << k for k in range(2, group.bit_length() - 1)]
     live_rows = min(routes.shape[1] * routes.shape[2], frames.shape[0])
     chunks = [live_rows // 2, live_rows // 4]
     chunks.append(live_rows - sum(chunks))
@@ -252,42 +242,62 @@
             (lengths.reshape(1, clips), b_first.reshape(1, width), w_first, w_second, frames),
         )
     )
-    text, order = [text_low], [0]
-    offset = col_blocks // 2
-    while offset:
-        held = text_low
-        if len(text) > 1:
-            held, audio_low = lax.optimization_barrier((text, audio_low))
-            held = jnp.concatenate(held, axis=0)
-        text.append(swap(held, offset))
-        order += [k ^ offset for k in order]
-        offset //= 2
-    audio = [audio_low] + [swap(audio_low, col_blocks * r) for r in range(1, row_blocks)]
-    grown, row_sum, col_sum = pl.pallas_call(
-        functools.partial(tile_kernel, row_blocks, order),
-        out_shape=(
-            jax.ShapeDtypeStruct((row_blocks * clips, col_blocks * clips), F32),
-            jax.ShapeDtypeStruct((max(row_blocks, 8), clips), F32),
-            jax.ShapeDtypeStruct((col_blocks, clips), F32),
-        ),
-        in_specs=[SMEM] + [VMEM] * (len(audio) + len(text)),
-        out_specs=(VMEM, VMEM, VMEM),
-        compiler_params=PARAMS,
-    )(scale, *audio, *text)
-    col_own, col_other, col_offset = total_sums(col_sum, col_blocks, 1)
-    row_own, row_other, row_offset = total_sums(row_sum, row_blocks, col_blocks)
-    parts = pl.pallas_call(
-        functools.partial(grad_kernel, row_blocks, order, row_offset, col_offset),
-        out_shape=[block_full if r == 0 else block_low for r in range(row_blocks)]
-        + [block_full if c == 0 else block_low for c in range(col_blocks)],
-        in_specs=[VMEM] * (5 + len(audio) + len(text)),
-        out_specs=[VMEM] * (row_blocks + col_blocks),
-        compiler_params=PARAMS,
-    )(grown, row_own, row_other, col_own, col_other, *audio, *text)
-    audio_parts = [parts[0]] + [swap(parts[r], col_blocks * r) for r in range(1, row_blocks)]
-    text_parts = [parts[row_blocks]] + [
-        swap(parts[row_blocks + c], c) for c in range(1, col_blocks)
-    ]
+    def joined(arrays):
+        return arrays[0] if len(arrays) == 1 else jnp.concatenate(arrays, axis=0)
+
+    def gathered(block):
+        arrays, offsets = [block], [0]
+        for bit in shared_bits:
+            arrays.append(swap(joined(arrays), bit))
+            offsets += [k ^ bit for k in offsets]
+        return arrays, offsets
+
+    text, columns = gathered(text_low)
+    shared_text, _ = lax.optimization_barrier((text, audio_low))
+    text += [swap(shared_text[0], 2), swap(joined(shared_text[1:]), 2)]
+    columns += [k ^ 2 for k in columns]
+    audio, rows = gathered(audio_low)
+    audio.append(swap(audio_low, 1))
+    early_rows = rows + [1]
+    early_audio = list(audio)
+    late_rows = [k ^ 1 for k in rows[1:]]
+    late_audio = [swap(joined(audio[1:-1]), 1)]
+
+    def tile(row_offsets, held, *sums):
+        count = len(row_offsets)
+        return pl.pallas_call(
+            functools.partial(tile_kernel, row_offsets, columns),
+            out_shape=(
+                jax.ShapeDtypeStruct((count * clips, len(columns) * clips), F32),
+                jax.ShapeDtypeStruct((count, clips), F32),
+                jax.ShapeDtypeStruct((len(columns), clips), F32),
+            ),
+            in_specs=[SMEM] + [VMEM] * (len(held) + len(text) + len(sums)),
+            out_specs=(VMEM, VMEM, VMEM),
+            compiler_params=PARAMS,
+        )(scale, *held, *text, *sums)
+
+    early_grown, early_sum, col_sum = tile(early_rows, early_audio)
+    late_grown, late_sum, col_sum = tile(late_rows, late_audio, col_sum)
+    row_sum = jnp.concatenate([early_sum, late_sum], axis=0)
+    row_other, col_other = swap(row_sum, 1), swap(col_sum, 2)
+    rows, audio = early_rows + late_rows, early_audio + late_audio
+    operands = [early_grown, late_grown, row_sum, row_other, col_sum, col_other, *audio, *text]
+
+    def grads(pick, kind):
+        return pl.pallas_call(
+            functools.partial(grad_kernel, rows, columns, pick),
+            out_shape=[kind, kind],
+            in_specs=[VMEM] * len(operands),
+            out_specs=[VMEM, VMEM],
+            compiler_params=PARAMS,
+        )(*operands)
+
+    audio_sent, text_sent = grads((1, 2), block_low)
+    text_parts, audio_parts = [swap(text_sent, 2)], [swap(audio_sent, 1)]
+    audio_own, text_own = grads((0, 0), block_full)
+    text_parts.insert(0, text_own)
+    audio_parts.insert(0, audio_own)
 
     def final(values, partner, pieces):
         return pl.pallas_call(

time: 38.9 us -> 37.1 us (0.954)
  waiting for transfers between devices: 13.9 us -> 12.6 us
  starting transfers between devices: 14.3 us -> 13.9 us
    ppermute x10, waiting for transfers between devices: 13.9 us -> 12.6 us  [swap(): return lax.ppermute(block, 'blk', [(i ^ offset, i) for i in range(count)])]
    pallas_call x1, Pallas kernels: 4.75 us -> 3.79 us  [local(): pl.pallas_call(functools.partial(frames_kernel, chunks), out_shape=(block...]
    pallas_call x3 -> x4, Pallas kernels: 1.28 us -> 1.99 us  [the longest x2 1.02 us: tile(): pl.pallas_call(functools.partial(tile_kernel, row_offsets, columns), out_...]
  transfers between devices with their start and end apart: 10 -> 10, of which waited for: 6 -> 8; matrix products, arithmetic and copies ran while one was open for 0% -> 0% of each run, Pallas kernels for 15% -> 16%
where the time goes in v4:
time: 37.1 us; the launch traced here: 36.5 us
  starting transfers between devices  13.9 us (37%)
  waiting for transfers between devices  12.6 us (34%)
  Pallas kernels  8.61 us (23%)
  between operations  1.35 us (4%)
    ppermute x10, starting transfers between devices, swap(): return lax.ppermute(block, 'blk', [(i ^ offset, i) for i in range(count)])  13.9 us
    ppermute x10, waiting for transfers between devices, swap(): return lax.ppermute(block, 'blk', [(i ^ offset, i) for i in range(count)])  12.6 us
    pallas_call x1, Pallas kernels, local(): pl.pallas_call(functools.partial(frames_kernel, chunks), out_shape=(block...  3.79 us
    pallas_call x2, Pallas kernels, final(): pl.pallas_call(functools.partial(final_kernel, pair_count), out_shape=blo...  1.8 us
    pallas_call x1, Pallas kernels, local(): pl.pallas_call(text_kernel, out_shape=block_low, in_specs=[HBM], out_spec...  1.03 us
    pallas_call x2, Pallas kernels, tile(): pl.pallas_call(functools.partial(tile_kernel, row_offsets, columns), out_...  1.02 us
    pallas_call x2, Pallas kernels, grads(): pl.pallas_call(functools.partial(grad_kernel, rows, columns, pick), out_s...  0.97 us
  transfers between devices with their start and end apart: 10, of which 8 were waited for; matrix products, arithmetic and copies ran while one was open for 0% of the time, Pallas kernels for 16%

profile of v4, /device:TPU:0, one launch (start us, length us, event | category | flops | bytes accessed | tf_op | source)
XLA Modules:
  0.0 36.5 jit_solution(9716312985052302733)
XLA Ops:
  0.6 1.0 %shard_map.87.refs_3_.refs_1_.refs_10_.partner_ref = bf16[128,512]{1,0:T(8,128)(2,1)S(1)} custom-call(bf16[128,512]{1,0:T(8,128)(2,1)} %values_ref.1), custom_call_target="tpu_custom_call" | custom-call | tf_op jit(solution)/shard_map/pallas_call | solution.py:217
  1.7 4.1 %collective-permute-start.2 = (bf16[128,512]{1,0:T(8,128)(2,1)S(1)}, bf16[128,512]{1,0:T(8,128)(2,1)S(1)}, u32[]{:S(2)}, u32[]{:S(2)}) collective-permute-start(bf16[128,512]{1,0:T(8,128)(2,1)S(1)} %shard_map.87.refs_3_.refs_1_.refs_10_.partner_ref), channel_id=1, source_target_pairs={{16,0},{20,4},{24,8},{28,12},{0,16},{4,20},{8,24},{12,28},{17,1},{... | collective-permute-start | bytes 393224 | tf_op jit(solution)/shard_map/ppermute | solution.py:33
  5.8 3.8 %shard_map.86 = (f32[128,512]{1,0:T(8,128)S(1)}, bf16[128,512]{1,0:T(8,128)(2,1)S(1)}) custom-call(s32[1,128]{1,0:T(1,128)} %bitcast.8, f32[1,512]{1,0:T(1,128)} %bitcast.7, bf16[768,512]{1,0:T(8,128)(2,1)} %refs_2_.1, bf16[512,512]{1,0:T(8,128)(2,1)} %refs_3_.1, bf16[4096,768]{1,0:T(8,128)(2,1)} %refs_4_.1), custom_call_target="tpu_custom_call" | custom-call | tf_op jit(solution)/shard_map/pallas_call | solution.py:225
  9.6 2.1 %collective-permute-start = (bf16[128,512]{1,0:T(8,128)(2,1)S(1)}, bf16[128,512]{1,0:T(8,128)(2,1)S(1)}, u32[]{:S(2)}, u32[]{:S(2)}) collective-permute-start(bf16[128,512]{1,0:T(8,128)(2,1)S(1)} %get-tuple-element.17.refs_0_.refs_6_.partner_ref), channel_id=1, source_target_pairs={{16,0},{20,4},{24,8},{28,12},{0,16},{4,20},{8,24},{12,28},{17,1},{... | collective-permute-start | bytes 393224 | tf_op jit(solution)/shard_map/ppermute | solution.py:33
  11.6 0.4 %collective-permute-done.2.refs_4_.refs_2_.refs_11_ = bf16[128,512]{1,0:T(8,128)(2,1)S(1)} collective-permute-done((bf16[128,512]{1,0:T(8,128)(2,1)S(1)}, bf16[128,512]{1,0:T(8,128)(2,1)S(1)}, u32[]{:S(2)}, u32[]{:S(2)}) %collective-permute-start.2) | collective-permute-done | bytes 131104 | tf_op jit(solution)/shard_map/ppermute | solution.py:33
  12.1 2.3 %collective-permute-start.3 = (bf16[128,512]{1,0:T(8,128)(2,1)S(1)}, bf16[128,512]{1,0:T(8,128)(2,1)S(1)}, u32[]{:S(2)}, u32[]{:S(2)}) collective-permute-start(bf16[128,512]{1,0:T(8,128)(2,1)S(1)} %shard_map.87.refs_3_.refs_1_.refs_10_.partner_ref), channel_id=1, source_target_pairs={{8,0},{12,4},{0,8},{4,12},{24,16},{28,20},{16,24},{20,28},{9,1},{1... | collective-permute-start | bytes 393224 | tf_op jit(solution)/shard_map/ppermute | solution.py:33
  14.4 4.0 %collective-permute-done.refs_1_.refs_7_ = bf16[128,512]{1,0:T(8,128)(2,1)S(1)} collective-permute-done((bf16[128,512]{1,0:T(8,128)(2,1)S(1)}, bf16[128,512]{1,0:T(8,128)(2,1)S(1)}, u32[]{:S(2)}, u32[]{:S(2)}) %collective-permute-start) | collective-permute-done | bytes 131104 | tf_op jit(solution)/shard_map/ppermute | solution.py:33
  18.4 1.5 %collective-permute-start.5 = (bf16[128,512]{1,0:T(8,128)(2,1)S(1)}, bf16[128,512]{1,0:T(8,128)(2,1)S(1)}, u32[]{:S(2)}, u32[]{:S(2)}) collective-permute-start(bf16[128,512]{1,0:T(8,128)(2,1)S(1)} %collective-permute-done.refs_1_.refs_7_), channel_id=1, source_target_pairs={{4,0},{0,4},{12,8},{8,12},{20,16},{16,20},{28,24},{24,28},{5,1},{1... | collective-permute-start | bytes 393224 | tf_op jit(solution)/shard_map/ppermute | solution.py:33
  20.6 1.8 %collective-permute-done.4.refs_6_.refs_4_.refs_13_ = bf16[128,512]{1,0:T(8,128)(2,1)S(1)} collective-permute-done((bf16[128,512]{1,0:T(8,128)(2,1)S(1)}, bf16[128,512]{1,0:T(8,128)(2,1)S(1)}, u32[]{:S(2)}, u32[]{:S(2)}) %collective-permute-start.4) | collective-permute-done | bytes 131104 | tf_op jit(solution)/shard_map/ppermute | solution.py:33
  22.4 0.7 %shard_map.88 = (f32[384,512]{1,0:T(8,128)S(1)}, f32[3,128]{1,0:T(4,128)S(1)}, f32[4,128]{1,0:T(4,128)S(1)}) custom-call(f32[1,1]{1,0:T(1,128)} %bitcast.3.scale_ref, bf16[128,512]{1,0:T(8,128)(2,1)S(1)} %get-tuple-element.17.refs_0_.refs_6_.partner_ref, bf16[128,512]{1,0:T(8,128)(2,1)S(1)} %collective-permute-done.refs_1_.refs_7_, ...), custom_call_target="tpu_custom_call" | custom-call | tf_op jit(solution)/shard_map/pallas_call | solution.py:268
  23.0 0.3 collective-permute-done.5.refs_0_.refs_9_
  23.4 0.4 %shard_map.89 = (f32[128,512]{1,0:T(8,128)S(1)}, f32[1,128]{1,0:T(1,128)S(1)}, f32[4,128]{1,0:T(4,128)S(1)}) custom-call(f32[1,1]{1,0:T(1,128)} %bitcast.4.scale_ref, bf16[128,512]{1,0:T(8,128)(2,1)S(1)} %collective-permute-done.5.refs_0_.refs_9_, bf16[128,512]{1,0:T(8,128)(2,1)S(1)} %shard_map.87.refs_3_.refs_1_.refs_10_.partner_ref, ...), custom_call_target="tpu_custom_call" | custom-call | tf_op jit(solution)/shard_map/pallas_call | solution.py:268
  23.8 1.7 %collective-permute-start.6 = (f32[4,128]{1,0:T(4,128)S(1)}, f32[4,128]{1,0:T(4,128)S(1)}, u32[]{:S(2)}, u32[]{:S(2)}) collective-permute-start(f32[4,128]{1,0:T(4,128)S(1)} %pad_maximum_fusion.refs_2_), channel_id=1, source_target_pairs={{4,0},{0,4},{12,8},{8,12},{20,16},{16,20},{28,24},{24,28},{5,1},{1... | collective-permute-start | bytes 6152 | tf_op jit(solution)/shard_map/ppermute | solution.py:33
  25.4 1.0 %collective-permute-start.7 = (f32[4,128]{1,0:T(4,128)S(1)}, f32[4,128]{1,0:T(4,128)S(1)}, u32[]{:S(2)}, u32[]{:S(2)}) collective-permute-start(f32[4,128]{1,0:T(4,128)S(1)} %get-tuple-element.25.refs_4_), channel_id=1, source_target_pairs={{8,0},{12,4},{0,8},{4,12},{24,16},{28,20},{16,24},{20,28},{9,1},{1... | collective-permute-start | bytes 6152 | tf_op jit(solution)/shard_map/ppermute | solution.py:33
  26.5 0.9 %collective-permute-done.6.refs_3_ = f32[4,128]{1,0:T(4,128)S(1)} collective-permute-done((f32[4,128]{1,0:T(4,128)S(1)}, f32[4,128]{1,0:T(4,128)S(1)}, u32[]{:S(2)}, u32[]{:S(2)}) %collective-permute-start.6) | collective-permute-done | bytes 2080 | tf_op jit(solution)/shard_map/ppermute | solution.py:33
  27.4 1.6 %collective-permute-done.7.refs_5_ = f32[4,128]{1,0:T(4,128)S(1)} collective-permute-done((f32[4,128]{1,0:T(4,128)S(1)}, f32[4,128]{1,0:T(4,128)S(1)}, u32[]{:S(2)}, u32[]{:S(2)}) %collective-permute-start.7) | collective-permute-done | bytes 2080 | tf_op jit(solution)/shard_map/ppermute | solution.py:33
  29.0 0.5 %shard_map.91 = (bf16[128,512]{1,0:T(8,128)(2,1)S(1)}, bf16[128,512]{1,0:T(8,128)(2,1)S(1)}) custom-call(f32[384,512]{1,0:T(8,128)S(1)} %get-tuple-element.20.refs_0_, f32[128,512]{1,0:T(8,128)S(1)} %get-tuple-element.22.refs_1_, f32[4,128]{1,0:T(4,128)S(1)} %pad_maximum_fusion.refs_2_, f32[4,128]{1,0:T(4,128)S(1)} %collective-permute-done.6.refs_3_, ...), custom_call_target="tpu_custom_call" | custom-call | tf_op jit(solution)/shard_map/pallas_call | solution.py:288
  29.5 1.1 %collective-permute-start.9 = (bf16[128,512]{1,0:T(8,128)(2,1)S(1)}, bf16[128,512]{1,0:T(8,128)(2,1)S(1)}, u32[]{:S(2)}, u32[]{:S(2)}) collective-permute-start(bf16[128,512]{1,0:T(8,128)(2,1)S(1)} %get-tuple-element.29), channel_id=1, source_target_pairs={{8,0},{12,4},{0,8},{4,12},{24,16},{28,20},{16,24},{20,28},{9,1},{1... | collective-permute-start | bytes 393224 | tf_op jit(solution)/shard_map/ppermute | solution.py:33
  30.6 0.1 collective-permute-start.8
  30.7 0.5 %shard_map.90 = (f32[128,512]{1,0:T(8,128)S(1)}, f32[128,512]{1,0:T(8,128)S(1)}) custom-call(f32[384,512]{1,0:T(8,128)S(1)} %get-tuple-element.20.refs_0_, f32[128,512]{1,0:T(8,128)S(1)} %get-tuple-element.22.refs_1_, f32[4,128]{1,0:T(4,128)S(1)} %pad_maximum_fusion.refs_2_, f32[4,128]{1,0:T(4,128)S(1)} %collective-permute-done.6.refs_3_, ...), custom_call_target="tpu_custom_call" | custom-call | tf_op jit(solution)/shard_map/pallas_call | solution.py:288
  31.2 3.4 %collective-permute-done.9.refs_1_ = bf16[128,512]{1,0:T(8,128)(2,1)S(1)} collective-permute-done((bf16[128,512]{1,0:T(8,128)(2,1)S(1)}, bf16[128,512]{1,0:T(8,128)(2,1)S(1)}, u32[]{:S(2)}, u32[]{:S(2)}) %collective-permute-start.9) | collective-permute-done | bytes 131104 | tf_op jit(solution)/shard_map/ppermute | solution.py:33
  34.5 0.9 %shard_map.93 = f32[128,512]{1,0:T(8,128)} custom-call(f32[1,1]{1,0:T(1,128)} %bitcast.6.scale_ref, bf16[128,512]{1,0:T(8,128)(2,1)S(1)} %copy-done, bf16[128,512]{1,0:T(8,128)(2,1)S(1)} %get-tuple-element.17.refs_0_.refs_6_.partner_ref, f32[128,512]{1,0:T(8,128)S(1)} %get-tuple-element.28.refs_0_, bf16[128,512]{1,0:T(8,128)(2,1)S(1)} %collective-permute-done.9.refs_1_), custom_call_target="tpu_custom_call" | custom-call | tf_op jit(solution)/shard_map/pallas_call | solution.py:303
  35.5 0.1 collective-permute-done.8.refs_1_
  35.6 0.9 %shard_map.92 = f32[128,512]{1,0:T(8,128)} custom-call(f32[1,1]{1,0:T(1,128)} %bitcast.5.scale_ref, f32[128,512]{1,0:T(8,128)S(1)} %get-tuple-element.16.values_ref, bf16[128,512]{1,0:T(8,128)(2,1)S(1)} %shard_map.87.refs_3_.refs_1_.refs_10_.partner_ref, f32[128,512]{1,0:T(8,128)S(1)} %get-tuple-element.26.refs_0_, ...), custom_call_target="tpu_custom_call" | custom-call | tf_op jit(solution)/shard_map/pallas_call | solution.py:303
  (7 shorter events, 0.1 us)
Async XLA Ops:
  1.7 10.4 %collective-permute-start.2 = (bf16[128,512]{1,0:T(8,128)(2,1)S(1)}, bf16[128,512]{1,0:T(8,128)(2,1)S(1)}, u32[]{:S(2)}, u32[]{:S(2)}) collective-permute-start(bf16[128,512]{1,0:T(8,128)(2,1)S(1)} %shard_map.87.refs_3_.refs_1_.refs_10_.partner_ref), channel_id=1, source_target_pairs={{16,0},{20,4},{24,8},{28,12},{0,16},{4,20},{8,24},{12,28},{17,1},{... | collective-permute-start | bytes 393224 | tf_op jit(solution)/shard_map/ppermute | solution.py:33
  5.8 28.8 %copy-start = (bf16[128,512]{1,0:T(8,128)(2,1)S(1)}, bf16[128,512]{1,0:T(8,128)(2,1)}, u32[]{:S(2)}) copy-start(bf16[128,512]{1,0:T(8,128)(2,1)} %values_ref.1) | copy-start | bytes 393220
  9.6 8.8 %collective-permute-start = (bf16[128,512]{1,0:T(8,128)(2,1)S(1)}, bf16[128,512]{1,0:T(8,128)(2,1)S(1)}, u32[]{:S(2)}, u32[]{:S(2)}) collective-permute-start(bf16[128,512]{1,0:T(8,128)(2,1)S(1)} %get-tuple-element.17.refs_0_.refs_6_.partner_ref), channel_id=1, source_target_pairs={{16,0},{20,4},{24,8},{28,12},{0,16},{4,20},{8,24},{12,28},{17,1},{... | collective-permute-start | bytes 393224 | tf_op jit(solution)/shard_map/ppermute | solution.py:33
  11.6 9.0 %collective-permute-start.1 = (bf16[128,512]{1,0:T(8,128)(2,1)S(1)}, bf16[128,512]{1,0:T(8,128)(2,1)S(1)}, u32[]{:S(2)}, u32[]{:S(2)}) collective-permute-start(bf16[128,512]{1,0:T(8,128)(2,1)S(1)} %get-tuple-element.17.refs_0_.refs_6_.partner_ref), channel_id=1, source_target_pairs={{4,0},{0,4},{12,8},{8,12},{20,16},{16,20},{28,24},{24,28},{5,1},{1... | collective-permute-start | bytes 393224 | tf_op jit(solution)/shard_map/ppermute | solution.py:33
  12.1 8.5 %collective-permute-start.3 = (bf16[128,512]{1,0:T(8,128)(2,1)S(1)}, bf16[128,512]{1,0:T(8,128)(2,1)S(1)}, u32[]{:S(2)}, u32[]{:S(2)}) collective-permute-start(bf16[128,512]{1,0:T(8,128)(2,1)S(1)} %shard_map.87.refs_3_.refs_1_.refs_10_.partner_ref), channel_id=1, source_target_pairs={{8,0},{12,4},{0,8},{4,12},{24,16},{28,20},{16,24},{20,28},{9,1},{1... | collective-permute-start | bytes 393224 | tf_op jit(solution)/shard_map/ppermute | solution.py:33
  14.4 8.0 %collective-permute-start.4 = (bf16[128,512]{1,0:T(8,128)(2,1)S(1)}, bf16[128,512]{1,0:T(8,128)(2,1)S(1)}, u32[]{:S(2)}, u32[]{:S(2)}) collective-permute-start(bf16[128,512]{1,0:T(8,128)(2,1)S(1)} %collective-permute-done.2.refs_4_.refs_2_.refs_11_), channel_id=1, source_target_pairs={{8,0},{12,4},{0,8},{4,12},{24,16},{28,20},{16,24},{20,28},{9,1},{1... | collective-permute-start | bytes 393224 | tf_op jit(solution)/shard_map/ppermute | solution.py:33
  18.4 5.0 %collective-permute-start.5 = (bf16[128,512]{1,0:T(8,128)(2,1)S(1)}, bf16[128,512]{1,0:T(8,128)(2,1)S(1)}, u32[]{:S(2)}, u32[]{:S(2)}) collective-permute-start(bf16[128,512]{1,0:T(8,128)(2,1)S(1)} %collective-permute-done.refs_1_.refs_7_), channel_id=1, source_target_pairs={{4,0},{0,4},{12,8},{8,12},{20,16},{16,20},{28,24},{24,28},{5,1},{1... | collective-permute-start | bytes 393224 | tf_op jit(solution)/shard_map/ppermute | solution.py:33
  23.8 3.7 %collective-permute-start.6 = (f32[4,128]{1,0:T(4,128)S(1)}, f32[4,128]{1,0:T(4,128)S(1)}, u32[]{:S(2)}, u32[]{:S(2)}) collective-permute-start(f32[4,128]{1,0:T(4,128)S(1)} %pad_maximum_fusion.refs_2_), channel_id=1, source_target_pairs={{4,0},{0,4},{12,8},{8,12},{20,16},{16,20},{28,24},{24,28},{5,1},{1... | collective-permute-start | bytes 6152 | tf_op jit(solution)/shard_map/ppermute | solution.py:33
  25.4 3.6 %collective-permute-start.7 = (f32[4,128]{1,0:T(4,128)S(1)}, f32[4,128]{1,0:T(4,128)S(1)}, u32[]{:S(2)}, u32[]{:S(2)}) collective-permute-start(f32[4,128]{1,0:T(4,128)S(1)} %get-tuple-element.25.refs_4_), channel_id=1, source_target_pairs={{8,0},{12,4},{0,8},{4,12},{24,16},{28,20},{16,24},{20,28},{9,1},{1... | collective-permute-start | bytes 6152 | tf_op jit(solution)/shard_map/ppermute | solution.py:33
  29.5 5.0 %collective-permute-start.9 = (bf16[128,512]{1,0:T(8,128)(2,1)S(1)}, bf16[128,512]{1,0:T(8,128)(2,1)S(1)}, u32[]{:S(2)}, u32[]{:S(2)}) collective-permute-start(bf16[128,512]{1,0:T(8,128)(2,1)S(1)} %get-tuple-element.29), channel_id=1, source_target_pairs={{8,0},{12,4},{0,8},{4,12},{24,16},{28,20},{16,24},{20,28},{9,1},{1... | collective-permute-start | bytes 393224 | tf_op jit(solution)/shard_map/ppermute | solution.py:33
  30.6 5.0 %collective-permute-start.8 = (bf16[128,512]{1,0:T(8,128)(2,1)S(1)}, bf16[128,512]{1,0:T(8,128)(2,1)S(1)}, u32[]{:S(2)}, u32[]{:S(2)}) collective-permute-start(bf16[128,512]{1,0:T(8,128)(2,1)S(1)} %get-tuple-element.27), channel_id=1, source_target_pairs={{4,0},{0,4},{12,8},{8,12},{20,16},{16,20},{28,24},{24,28},{5,1},{1... | collective-permute-start | bytes 393224 | tf_op jit(solution)/shard_map/ppermute | solution.py:33

commit v5 on v4

--- a/solution.py
+++ b/solution.py
@@ -188,17 +188,25 @@
     text_out[...] = total.astype(text_out.dtype)
 
 
-def final_kernel(pair_count, scale_ref, values_ref, partner_ref, *refs):
-    parts, out_ref = refs[:-1], refs[-1]
-    values = values_ref[...].astype(F32)
-    total = parts[0][...] - 2.0 * partner_ref[...].astype(F32)
-    for part in parts[1:]:
-        total = total + part[...].astype(F32)
-    total = total * (scale_ref[0, 0] / (2.0 * pair_count))
-    inverse = lax.rsqrt(jnp.sum(values * values, axis=1, keepdims=True) + epsilon)
-    unit = values * inverse
-    along = jnp.sum(unit * total, axis=1, keepdims=True)
-    out_ref[...] = (total - unit * along) * inverse
+def final_kernel(pair_count, count, scale_ref, *refs):
+    factor = scale_ref[0, 0] / (2.0 * pair_count)
+    copies = []
+    outs, stages, sems = refs[2 * count :][:2], refs[2 * count + 2 :][:2], refs[-1]
+    for side in range(2):
+        values_ref, partner_ref, *parts = refs[side * count : (side + 1) * count]
+        values = values_ref[...].astype(F32)
+        total = parts[0][...] - 2.0 * partner_ref[...].astype(F32)
+        for part in parts[1:]:
+            total = total + part[...].astype(F32)
+        total = total * factor
+        inverse = lax.rsqrt(jnp.sum(values * values, axis=1, keepdims=True) + epsilon)
+        unit = values * inverse
+        along = jnp.sum(unit * total, axis=1, keepdims=True)
+        stages[side][...] = (total - unit * along) * inverse
+        copies.append(pltpu.make_async_copy(stages[side], outs[side], sems.at[side]))
+        copies[-1].start()
+    for copy in copies:
+        copy.wait()
 
 
 def local(frames, lengths, routes, w_first, b_first, w_second, captions, logit_scale):
@@ -254,7 +262,7 @@
 
     text, columns = gathered(text_low)
     shared_text, _ = lax.optimization_barrier((text, audio_low))
-    text += [swap(shared_text[0], 2), swap(joined(shared_text[1:]), 2)]
+    text += [swap(text_low, 2), swap(joined(shared_text[1:]), 2)]
     columns += [k ^ 2 for k in columns]
     audio, rows = gathered(audio_low)
     audio.append(swap(audio_low, 1))
@@ -299,16 +307,19 @@
     text_parts.insert(0, text_own)
     audio_parts.insert(0, audio_own)
 
-    def final(values, partner, pieces):
-        return pl.pallas_call(
-            functools.partial(final_kernel, pair_count),
-            out_shape=block_full,
-            in_specs=[SMEM] + [VMEM] * (2 + len(pieces)),
-            out_specs=VMEM,
-            compiler_params=PARAMS,
-        )(scale, values, partner, *pieces)
-
-    return final(pooled, text_low, audio_parts), final(captions, audio_low, text_parts)
+    sides = [pooled, text_low, *audio_parts, captions, audio_low, *text_parts]
+    return pl.pallas_call(
+        functools.partial(final_kernel, pair_count, len(sides) // 2),
+        out_shape=(block_full, block_full),
+        in_specs=[SMEM] + [VMEM] * len(sides),
+        out_specs=(HBM, HBM),
+        scratch_shapes=[
+            pltpu.VMEM((clips, width), F32),
+            pltpu.VMEM((clips, width), F32),
+            pltpu.SemaphoreType.DMA((2,)),
+        ],
+        compiler_params=PARAMS,
+    )(scale, *sides)
 
 
 def solution(mesh):

time: 37.1 us -> 37 us (level); the launches traced: 36.5 us -> 37.7 us
  waiting for transfers between devices: 12.6 us -> 15.8 us
  starting transfers between devices: 13.9 us -> 12.6 us
  Pallas kernels: 8.61 us -> 7.85 us
    ppermute x10, waiting for transfers between devices: 12.6 us -> 15.8 us  [swap(): return lax.ppermute(block, 'blk', [(i ^ offset, i) for i in range(count)])]
    ppermute x10, starting transfers between devices: 13.9 us -> 12.6 us  [swap(): return lax.ppermute(block, 'blk', [(i ^ offset, i) for i in range(count)])]
    pallas_call x2 -> x1, Pallas kernels: 1.8 us -> 1.04 us  [local(): pl.pallas_call(functools.partial(final_kernel, pair_count, len(sides) //...]
  transfers between devices with their start and end apart: 10 -> 10, of which waited for: 8 -> 7; matrix products, arithmetic and copies ran while one was open for 0% -> 0% of each run, Pallas kernels for 16% -> 13%
where the time goes in v5:
time: 37 us; the launch traced here: 37.7 us
  waiting for transfers between devices  15.8 us (43%)
  starting transfers between devices  12.6 us (34%)
  Pallas kernels  7.85 us (21%)
  between operations  1.34 us (4%)
    ppermute x10, waiting for transfers between devices, swap(): return lax.ppermute(block, 'blk', [(i ^ offset, i) for i in range(count)])  15.8 us
    ppermute x10, starting transfers between devices, swap(): return lax.ppermute(block, 'blk', [(i ^ offset, i) for i in range(count)])  12.6 us
    pallas_call x1, Pallas kernels, local(): pl.pallas_call(functools.partial(frames_kernel, chunks), out_shape=(block...  3.79 us
    pallas_call x1, Pallas kernels, local(): pl.pallas_call(functools.partial(final_kernel, pair_count, len(sides) //...  1.04 us
    pallas_call x1, Pallas kernels, local(): pl.pallas_call(text_kernel, out_shape=block_low, in_specs=[HBM], out_spec...  1.03 us
    pallas_call x2, Pallas kernels, tile(): pl.pallas_call(functools.partial(tile_kernel, row_offsets, columns), out_...  1.02 us
    pallas_call x2, Pallas kernels, grads(): pl.pallas_call(functools.partial(grad_kernel, rows, columns, pick), out_s...  0.98 us
  transfers between devices with their start and end apart: 10, of which 7 were waited for; matrix products, arithmetic and copies ran while one was open for 0% of the time, Pallas kernels for 13%

profile of v5, /device:TPU:0, one launch (start us, length us, event | category | flops | bytes accessed | tf_op | source)
XLA Modules:
  0.0 37.7 jit_solution(10840081052340555663)
XLA Ops:
  0.6 1.0 %shard_map.87.refs_3_.refs_1_.refs_10_ = bf16[128,512]{1,0:T(8,128)(2,1)S(1)} custom-call(bf16[128,512]{1,0:T(8,128)(2,1)} %refs_4_.3), custom_call_target="tpu_custom_call" | custom-call | tf_op jit(solution)/shard_map/pallas_call | solution.py:225
  1.7 4.1 %collective-permute-start.2 = (bf16[128,512]{1,0:T(8,128)(2,1)S(1)}, bf16[128,512]{1,0:T(8,128)(2,1)S(1)}, u32[]{:S(2)}, u32[]{:S(2)}) collective-permute-start(bf16[128,512]{1,0:T(8,128)(2,1)S(1)} %shard_map.87.refs_3_.refs_1_.refs_10_), channel_id=1, source_target_pairs={{16,0},{20,4},{24,8},{28,12},{0,16},{4,20},{8,24},{12,28},{17,1},{... | collective-permute-start | bytes 393224 | tf_op jit(solution)/shard_map/ppermute | solution.py:33
  5.8 3.8 %shard_map.86 = (f32[128,512]{1,0:T(8,128)S(1)}, bf16[128,512]{1,0:T(8,128)(2,1)S(1)}) custom-call(s32[1,128]{1,0:T(1,128)} %bitcast.7, f32[1,512]{1,0:T(1,128)} %bitcast.6, bf16[768,512]{1,0:T(8,128)(2,1)} %refs_2_.1, bf16[512,512]{1,0:T(8,128)(2,1)} %refs_3_.1, bf16[4096,768]{1,0:T(8,128)(2,1)} %refs_4_.2), custom_call_target="tpu_custom_call" | custom-call | tf_op jit(solution)/shard_map/pallas_call | solution.py:233
  9.6 0.1 collective-permute-start
  9.7 1.9 %collective-permute-start.3 = (bf16[128,512]{1,0:T(8,128)(2,1)S(1)}, bf16[128,512]{1,0:T(8,128)(2,1)S(1)}, u32[]{:S(2)}, u32[]{:S(2)}) collective-permute-start(bf16[128,512]{1,0:T(8,128)(2,1)S(1)} %shard_map.87.refs_3_.refs_1_.refs_10_), channel_id=1, source_target_pairs={{8,0},{12,4},{0,8},{4,12},{24,16},{28,20},{16,24},{20,28},{9,1},{1... | collective-permute-start | bytes 393224 | tf_op jit(solution)/shard_map/ppermute | solution.py:33
  11.5 1.5 %collective-permute-start.1 = (bf16[128,512]{1,0:T(8,128)(2,1)S(1)}, bf16[128,512]{1,0:T(8,128)(2,1)S(1)}, u32[]{:S(2)}, u32[]{:S(2)}) collective-permute-start(bf16[128,512]{1,0:T(8,128)(2,1)S(1)} %get-tuple-element.16.refs_0_.refs_6_.refs_5_), channel_id=1, source_target_pairs={{4,0},{0,4},{12,8},{8,12},{20,16},{16,20},{28,24},{24,28},{5,1},{1... | collective-permute-start | bytes 393224 | tf_op jit(solution)/shard_map/ppermute | solution.py:33
  13.1 2.1 %collective-permute-start.4 = (bf16[128,512]{1,0:T(8,128)(2,1)S(1)}, bf16[128,512]{1,0:T(8,128)(2,1)S(1)}, u32[]{:S(2)}, u32[]{:S(2)}) collective-permute-start(bf16[128,512]{1,0:T(8,128)(2,1)S(1)} %collective-permute-done.2.refs_4_.refs_2_.refs_11_), channel_id=1, source_target_pairs={{8,0},{12,4},{0,8},{4,12},{24,16},{28,20},{16,24},{20,28},{9,1},{1... | collective-permute-start | bytes 393224 | tf_op jit(solution)/shard_map/ppermute | solution.py:33
  15.2 4.1 %collective-permute-done.refs_1_.refs_7_ = bf16[128,512]{1,0:T(8,128)(2,1)S(1)} collective-permute-done((bf16[128,512]{1,0:T(8,128)(2,1)S(1)}, bf16[128,512]{1,0:T(8,128)(2,1)S(1)}, u32[]{:S(2)}, u32[]{:S(2)}) %collective-permute-start) | collective-permute-done | bytes 131104 | tf_op jit(solution)/shard_map/ppermute | solution.py:33
  19.3 0.6 %collective-permute-start.5 = (bf16[128,512]{1,0:T(8,128)(2,1)S(1)}, bf16[128,512]{1,0:T(8,128)(2,1)S(1)}, u32[]{:S(2)}, u32[]{:S(2)}) collective-permute-start(bf16[128,512]{1,0:T(8,128)(2,1)S(1)} %collective-permute-done.refs_1_.refs_7_), channel_id=1, source_target_pairs={{4,0},{0,4},{12,8},{8,12},{20,16},{16,20},{28,24},{24,28},{5,1},{1... | collective-permute-start | bytes 393224 | tf_op jit(solution)/shard_map/ppermute | solution.py:33
  20.6 0.0 collective-permute-done.3.refs_5_.refs_3_.refs_12_
  20.6 1.1 %collective-permute-done.4.refs_6_.refs_4_.refs_13_ = bf16[128,512]{1,0:T(8,128)(2,1)S(1)} collective-permute-done((bf16[128,512]{1,0:T(8,128)(2,1)S(1)}, bf16[128,512]{1,0:T(8,128)(2,1)S(1)}, u32[]{:S(2)}, u32[]{:S(2)}) %collective-permute-start.4) | collective-permute-done | bytes 131104 | tf_op jit(solution)/shard_map/ppermute | solution.py:33
  21.7 0.7 %shard_map.88 = (f32[384,512]{1,0:T(8,128)S(1)}, f32[3,128]{1,0:T(4,128)S(1)}, f32[4,128]{1,0:T(4,128)S(1)}) custom-call(f32[1,1]{1,0:T(1,128)} %bitcast.3.scale_ref, bf16[128,512]{1,0:T(8,128)(2,1)S(1)} %get-tuple-element.16.refs_0_.refs_6_.refs_5_, bf16[128,512]{1,0:T(8,128)(2,1)S(1)} %collective-permute-done.refs_1_.refs_7_, ...), custom_call_target="tpu_custom_call" | custom-call | tf_op jit(solution)/shard_map/pallas_call | solution.py:276
  22.4 2.7 %collective-permute-done.5.refs_0_.refs_9_ = bf16[128,512]{1,0:T(8,128)(2,1)S(1)} collective-permute-done((bf16[128,512]{1,0:T(8,128)(2,1)S(1)}, bf16[128,512]{1,0:T(8,128)(2,1)S(1)}, u32[]{:S(2)}, u32[]{:S(2)}) %collective-permute-start.5) | collective-permute-done | bytes 131104 | tf_op jit(solution)/shard_map/ppermute | solution.py:33
  25.0 0.4 shard_map.89
  25.4 0.4 collective-permute-start.6
  25.8 0.1 collective-permute-start.7
  25.9 3.2 %collective-permute-done.6.refs_3_ = f32[4,128]{1,0:T(4,128)S(1)} collective-permute-done((f32[4,128]{1,0:T(4,128)S(1)}, f32[4,128]{1,0:T(4,128)S(1)}, u32[]{:S(2)}, u32[]{:S(2)}) %collective-permute-start.6) | collective-permute-done | bytes 2080 | tf_op jit(solution)/shard_map/ppermute | solution.py:33
  29.1 0.3 collective-permute-done.7.refs_5_
  29.4 0.5 %shard_map.91 = (bf16[128,512]{1,0:T(8,128)(2,1)S(1)}, bf16[128,512]{1,0:T(8,128)(2,1)S(1)}) custom-call(f32[384,512]{1,0:T(8,128)S(1)} %get-tuple-element.18.refs_0_, f32[128,512]{1,0:T(8,128)S(1)} %get-tuple-element.20.refs_1_, f32[4,128]{1,0:T(4,128)S(1)} %pad_maximum_fusion.refs_2_, f32[4,128]{1,0:T(4,128)S(1)} %collective-permute-done.6.refs_3_, ...), custom_call_target="tpu_custom_call" | custom-call | tf_op jit(solution)/shard_map/pallas_call | solution.py:296
  29.9 1.8 %collective-permute-start.8 = (bf16[128,512]{1,0:T(8,128)(2,1)S(1)}, bf16[128,512]{1,0:T(8,128)(2,1)S(1)}, u32[]{:S(2)}, u32[]{:S(2)}) collective-permute-start(bf16[128,512]{1,0:T(8,128)(2,1)S(1)} %get-tuple-element.25), channel_id=1, source_target_pairs={{4,0},{0,4},{12,8},{8,12},{20,16},{16,20},{28,24},{24,28},{5,1},{1... | collective-permute-start | bytes 393224 | tf_op jit(solution)/shard_map/ppermute | solution.py:33
  31.7 0.5 %shard_map.90 = (f32[128,512]{1,0:T(8,128)S(1)}, f32[128,512]{1,0:T(8,128)S(1)}) custom-call(f32[384,512]{1,0:T(8,128)S(1)} %get-tuple-element.18.refs_0_, f32[128,512]{1,0:T(8,128)S(1)} %get-tuple-element.20.refs_1_, f32[4,128]{1,0:T(4,128)S(1)} %pad_maximum_fusion.refs_2_, f32[4,128]{1,0:T(4,128)S(1)} %collective-permute-done.6.refs_3_, ...), custom_call_target="tpu_custom_call" | custom-call | tf_op jit(solution)/shard_map/pallas_call | solution.py:296
  32.2 2.7 %collective-permute-done.8.refs_3_ = bf16[128,512]{1,0:T(8,128)(2,1)S(1)} collective-permute-done((bf16[128,512]{1,0:T(8,128)(2,1)S(1)}, bf16[128,512]{1,0:T(8,128)(2,1)S(1)}, u32[]{:S(2)}, u32[]{:S(2)}) %collective-permute-start.8) | collective-permute-done | bytes 131104 | tf_op jit(solution)/shard_map/ppermute | solution.py:33
  34.9 1.7 %collective-permute-done.9.refs_7_ = bf16[128,512]{1,0:T(8,128)(2,1)S(1)} collective-permute-done((bf16[128,512]{1,0:T(8,128)(2,1)S(1)}, bf16[128,512]{1,0:T(8,128)(2,1)S(1)}, u32[]{:S(2)}, u32[]{:S(2)}) %collective-permute-start.9) | collective-permute-done | bytes 131104 | tf_op jit(solution)/shard_map/ppermute | solution.py:33
  36.6 1.0 %shard_map.92 = (f32[128,512]{1,0:T(8,128)}, f32[128,512]{1,0:T(8,128)}) custom-call(f32[1,1]{1,0:T(1,128)} %bitcast.5.scale_ref, f32[128,512]{1,0:T(8,128)S(1)} %get-tuple-element.15.refs_0_, bf16[128,512]{1,0:T(8,128)(2,1)S(1)} %shard_map.87.refs_3_.refs_1_.refs_10_, f32[128,512]{1,0:T(8,128)S(1)} %get-tuple-element.24.refs_2_, ...), custom_call_target="tpu_custom_call" | custom-call | tf_op jit(solution)/shard_map/pallas_call | solution.py:311
  (6 shorter events, 0.0 us)
Async XLA Ops:
  1.7 11.4 %collective-permute-start.2 = (bf16[128,512]{1,0:T(8,128)(2,1)S(1)}, bf16[128,512]{1,0:T(8,128)(2,1)S(1)}, u32[]{:S(2)}, u32[]{:S(2)}) collective-permute-start(bf16[128,512]{1,0:T(8,128)(2,1)S(1)} %shard_map.87.refs_3_.refs_1_.refs_10_), channel_id=1, source_target_pairs={{16,0},{20,4},{24,8},{28,12},{0,16},{4,20},{8,24},{12,28},{17,1},{... | collective-permute-start | bytes 393224 | tf_op jit(solution)/shard_map/ppermute | solution.py:33
  5.8 30.9 %copy-start = (bf16[128,512]{1,0:T(8,128)(2,1)S(1)}, bf16[128,512]{1,0:T(8,128)(2,1)}, u32[]{:S(2)}) copy-start(bf16[128,512]{1,0:T(8,128)(2,1)} %refs_4_.3) | copy-start | bytes 393220
  9.6 9.8 %collective-permute-start = (bf16[128,512]{1,0:T(8,128)(2,1)S(1)}, bf16[128,512]{1,0:T(8,128)(2,1)S(1)}, u32[]{:S(2)}, u32[]{:S(2)}) collective-permute-start(bf16[128,512]{1,0:T(8,128)(2,1)S(1)} %get-tuple-element.16.refs_0_.refs_6_.refs_5_), channel_id=1, source_target_pairs={{16,0},{20,4},{24,8},{28,12},{0,16},{4,20},{8,24},{12,28},{17,1},{... | collective-permute-start | bytes 393224 | tf_op jit(solution)/shard_map/ppermute | solution.py:33
  9.7 11.0 %collective-permute-start.3 = (bf16[128,512]{1,0:T(8,128)(2,1)S(1)}, bf16[128,512]{1,0:T(8,128)(2,1)S(1)}, u32[]{:S(2)}, u32[]{:S(2)}) collective-permute-start(bf16[128,512]{1,0:T(8,128)(2,1)S(1)} %shard_map.87.refs_3_.refs_1_.refs_10_), channel_id=1, source_target_pairs={{8,0},{12,4},{0,8},{4,12},{24,16},{28,20},{16,24},{20,28},{9,1},{1... | collective-permute-start | bytes 393224 | tf_op jit(solution)/shard_map/ppermute | solution.py:33
  11.5 9.1 %collective-permute-start.1 = (bf16[128,512]{1,0:T(8,128)(2,1)S(1)}, bf16[128,512]{1,0:T(8,128)(2,1)S(1)}, u32[]{:S(2)}, u32[]{:S(2)}) collective-permute-start(bf16[128,512]{1,0:T(8,128)(2,1)S(1)} %get-tuple-element.16.refs_0_.refs_6_.refs_5_), channel_id=1, source_target_pairs={{4,0},{0,4},{12,8},{8,12},{20,16},{16,20},{28,24},{24,28},{5,1},{1... | collective-permute-start | bytes 393224 | tf_op jit(solution)/shard_map/ppermute | solution.py:33
  13.1 8.6 %collective-permute-start.4 = (bf16[128,512]{1,0:T(8,128)(2,1)S(1)}, bf16[128,512]{1,0:T(8,128)(2,1)S(1)}, u32[]{:S(2)}, u32[]{:S(2)}) collective-permute-start(bf16[128,512]{1,0:T(8,128)(2,1)S(1)} %collective-permute-done.2.refs_4_.refs_2_.refs_11_), channel_id=1, source_target_pairs={{8,0},{12,4},{0,8},{4,12},{24,16},{28,20},{16,24},{20,28},{9,1},{1... | collective-permute-start | bytes 393224 | tf_op jit(solution)/shard_map/ppermute | solution.py:33
  19.3 5.7 %collective-permute-start.5 = (bf16[128,512]{1,0:T(8,128)(2,1)S(1)}, bf16[128,512]{1,0:T(8,128)(2,1)S(1)}, u32[]{:S(2)}, u32[]{:S(2)}) collective-permute-start(bf16[128,512]{1,0:T(8,128)(2,1)S(1)} %collective-permute-done.refs_1_.refs_7_), channel_id=1, source_target_pairs={{4,0},{0,4},{12,8},{8,12},{20,16},{16,20},{28,24},{24,28},{5,1},{1... | collective-permute-start | bytes 393224 | tf_op jit(solution)/shard_map/ppermute | solution.py:33
  25.4 3.7 %collective-permute-start.6 = (f32[4,128]{1,0:T(4,128)S(1)}, f32[4,128]{1,0:T(4,128)S(1)}, u32[]{:S(2)}, u32[]{:S(2)}) collective-permute-start(f32[4,128]{1,0:T(4,128)S(1)} %pad_maximum_fusion.refs_2_), channel_id=1, source_target_pairs={{4,0},{0,4},{12,8},{8,12},{20,16},{16,20},{28,24},{24,28},{5,1},{1... | collective-permute-start | bytes 6152 | tf_op jit(solution)/shard_map/ppermute | solution.py:33
  25.8 3.6 %collective-permute-start.7 = (f32[4,128]{1,0:T(4,128)S(1)}, f32[4,128]{1,0:T(4,128)S(1)}, u32[]{:S(2)}, u32[]{:S(2)}) collective-permute-start(f32[4,128]{1,0:T(4,128)S(1)} %get-tuple-element.23.refs_4_), channel_id=1, source_target_pairs={{8,0},{12,4},{0,8},{4,12},{24,16},{28,20},{16,24},{20,28},{9,1},{1... | collective-permute-start | bytes 6152 | tf_op jit(solution)/shard_map/ppermute | solution.py:33
  29.9 5.0 %collective-permute-start.8 = (bf16[128,512]{1,0:T(8,128)(2,1)S(1)}, bf16[128,512]{1,0:T(8,128)(2,1)S(1)}, u32[]{:S(2)}, u32[]{:S(2)}) collective-permute-start(bf16[128,512]{1,0:T(8,128)(2,1)S(1)} %get-tuple-element.25), channel_id=1, source_target_pairs={{4,0},{0,4},{12,8},{8,12},{20,16},{16,20},{28,24},{24,28},{5,1},{1... | collective-permute-start | bytes 393224 | tf_op jit(solution)/shard_map/ppermute | solution.py:33
  31.7 5.0 %collective-permute-start.9 = (bf16[128,512]{1,0:T(8,128)(2,1)S(1)}, bf16[128,512]{1,0:T(8,128)(2,1)S(1)}, u32[]{:S(2)}, u32[]{:S(2)}) collective-permute-start(bf16[128,512]{1,0:T(8,128)(2,1)S(1)} %get-tuple-element.27), channel_id=1, source_target_pairs={{8,0},{12,4},{0,8},{4,12},{24,16},{28,20},{16,24},{20,28},{9,1},{1... | collective-permute-start | bytes 393224 | tf_op jit(solution)/shard_map/ppermute | solution.py:33

commit v6 on v5

--- a/solution.py
+++ b/solution.py
@@ -40,13 +40,6 @@
 
 def unit_low(values):
     return values * lax.rsqrt(jnp.sum(values * values, axis=1, keepdims=True) + epsilon)
-
-
-def text_kernel(captions_hbm, text_ref, captions_ref, sem):
-    copy = pltpu.make_async_copy(captions_hbm, captions_ref, sem)
-    copy.start()
-    copy.wait()
-    text_ref[...] = unit_low(captions_ref[...].astype(F32)).astype(BF16)
 
 
 def frames_kernel(chunks, *refs):
@@ -115,27 +108,15 @@
     audio_ref[...] = unit_low(pooled).astype(BF16)
 
 
-def tile_kernel(rows, columns, scale_ref, *refs):
-    first_refs, last_refs = refs[: len(refs) - 3], refs[len(refs) - 3 :]
-    grown_ref, row_ref, col_ref = last_refs
+def tile_kernel(rows, columns, audio_refs, text, col_sums, scale, grown_ref, row_ref, col_ref):
     block = row_ref.shape[1]
-    held, at = [], 0
-    for offsets in (rows, columns):
-        taken, count = [], 0
-        while count < len(offsets):
-            taken.append(first_refs[at])
-            count += first_refs[at].shape[0] // block
-            at += 1
-        held.append(blocks_of(taken, offsets, block))
-    audio, text = held
-    col_sums = [first_refs[at][pl.ds(c, 1), :] for c in range(len(columns))] if at < len(first_refs) else None
-    factor = scale_ref[0, 0] * LOG2E
+    audio = blocks_of(audio_refs, rows, block)
     for r, row in enumerate(rows):
         values = audio[row][...]
         partial = None
         downs = []
-        for c, column in enumerate(columns):
-            grown = jnp.exp2(mm(values, text[column][...], 1, 1) * factor)
+        for c in range(len(columns)):
+            grown = jnp.exp2(mm(values, text[c], 1, 1) * (scale * LOG2E))
             grown_ref[pl.ds(r * block, block), pl.ds(c * block, block)] = grown
             downs.append(jnp.sum(grown, axis=0, keepdims=True))
             partial = grown if c == 0 else partial + grown
@@ -145,8 +126,29 @@
         col_ref[pl.ds(c, 1), :] = col_sums[c]
 
 
-def grad_kernel(rows, columns, pick, *refs):
-    block = refs[-1].shape[0]
+def early_tile_kernel(rows, columns, audio_count, scale_ref, *refs):
+    grown_ref, row_ref, col_ref, low_ref = refs[len(refs) - 4 :]
+    block = row_ref.shape[1]
+    raw = blocks_of(refs[audio_count : len(refs) - 4], columns, block)
+    text = []
+    for c, column in enumerate(columns):
+        text.append(unit_low(raw[column][...].astype(F32)).astype(BF16))
+        low_ref[pl.ds(c * block, block), :] = text[c]
+    audio = refs[:audio_count]
+    tile_kernel(rows, columns, audio, text, None, scale_ref[0, 0], grown_ref, row_ref, col_ref)
+
+
+def late_tile_kernel(rows, columns, scale_ref, *refs):
+    low_ref, sums_ref, grown_ref, row_ref, col_ref = refs[len(refs) - 5 :]
+    block = row_ref.shape[1]
+    text = [low_ref[pl.ds(c * block, block), :] for c in range(len(columns))]
+    sums = [sums_ref[pl.ds(c, 1), :] for c in range(len(columns))]
+    audio = refs[: len(refs) - 5]
+    tile_kernel(rows, columns, audio, text, sums, scale_ref[0, 0], grown_ref, row_ref, col_ref)
+
+
+def grad_kernel(rows, columns, row_bit, col_bit, pick, *refs):
+    block = refs[len(refs) - 1].shape[0]
     count = len(rows)
     grown, near = {}, 0
     held = 0
@@ -172,10 +174,10 @@
         return 1.0 / (own[here, :] + other[there, :])
 
     def row_inverse(row):
-        return jnp.broadcast_to(inverse(rows, row, 1, row_ref, row_other), (block, block)).T
+        return jnp.broadcast_to(inverse(rows, row, row_bit, row_ref, row_other), (block, block)).T
 
     row_scale = {row: row_inverse(row) for row in rows}
-    col_scale = {column: inverse(columns, column, 2, col_ref, col_other) for column in columns}
+    col_scale = {column: inverse(columns, column, col_bit, col_ref, col_other) for column in columns}
 
     def weights(row, column):
         index, k, c = grown[row, column]
@@ -195,7 +197,7 @@
     for side in range(2):
         values_ref, partner_ref, *parts = refs[side * count : (side + 1) * count]
         values = values_ref[...].astype(F32)
-        total = parts[0][...] - 2.0 * partner_ref[...].astype(F32)
+        total = parts[0][...] - 2.0 * partner_ref[pl.ds(0, values.shape[0]), :].astype(F32)
         for part in parts[1:]:
             total = total + part[...].astype(F32)
         total = total * factor
@@ -214,7 +216,9 @@
     width = w_second.shape[1]
     group = lax.axis_size("blk")
     pair_count = clips * group * lax.axis_size("dp")
-    shared_bits = [1 << k for k in range(2, group.bit_length() - 1)]
+    bits = [1 << k for k in range(group.bit_length() - 1)]
+    row_bit, col_bit = bits[1], bits[0]
+    shared_bits = [bit for bit in bits if bit not in (row_bit, col_bit)]
     live_rows = min(routes.shape[1] * routes.shape[2], frames.shape[0])
     chunks = [live_rows // 2, live_rows // 4]
     chunks.append(live_rows - sum(chunks))
@@ -222,14 +226,6 @@
     block_low = jax.ShapeDtypeStruct((clips, width), BF16)
     block_full = jax.ShapeDtypeStruct((clips, width), F32)
 
-    text_low = pl.pallas_call(
-        text_kernel,
-        out_shape=block_low,
-        in_specs=[HBM],
-        out_specs=VMEM,
-        scratch_shapes=[pltpu.VMEM((clips, width), BF16), pltpu.SemaphoreType.DMA],
-        compiler_params=PARAMS,
-    )(in_hbm(captions))
     pooled, audio_low = pl.pallas_call(
         functools.partial(frames_kernel, chunks),
         out_shape=(block_full, block_low),
@@ -260,49 +256,58 @@
             offsets += [k ^ bit for k in offsets]
         return arrays, offsets
 
-    text, columns = gathered(text_low)
+    text, columns = gathered(captions)
     shared_text, _ = lax.optimization_barrier((text, audio_low))
-    text += [swap(text_low, 2), swap(joined(shared_text[1:]), 2)]
-    columns += [k ^ 2 for k in columns]
+    text += [swap(captions, col_bit), swap(joined(shared_text[1:]), col_bit)]
+    columns += [k ^ col_bit for k in columns]
     audio, rows = gathered(audio_low)
-    audio.append(swap(audio_low, 1))
-    early_rows = rows + [1]
+    audio.append(swap(audio_low, row_bit))
+    early_rows = rows + [row_bit]
     early_audio = list(audio)
-    late_rows = [k ^ 1 for k in rows[1:]]
-    late_audio = [swap(joined(audio[1:-1]), 1)]
-
-    def tile(row_offsets, held, *sums):
+    late_rows = [k ^ row_bit for k in rows[1:]]
+    late_audio = [swap(joined(audio[1:-1]), row_bit)]
+
+    def tile_shapes(row_offsets):
         count = len(row_offsets)
-        return pl.pallas_call(
-            functools.partial(tile_kernel, row_offsets, columns),
-            out_shape=(
-                jax.ShapeDtypeStruct((count * clips, len(columns) * clips), F32),
-                jax.ShapeDtypeStruct((count, clips), F32),
-                jax.ShapeDtypeStruct((len(columns), clips), F32),
-            ),
-            in_specs=[SMEM] + [VMEM] * (len(held) + len(text) + len(sums)),
-            out_specs=(VMEM, VMEM, VMEM),
-            compiler_params=PARAMS,
-        )(scale, *held, *text, *sums)
-
-    early_grown, early_sum, col_sum = tile(early_rows, early_audio)
-    late_grown, late_sum, col_sum = tile(late_rows, late_audio, col_sum)
+        return (
+            jax.ShapeDtypeStruct((count * clips, len(columns) * clips), F32),
+            jax.ShapeDtypeStruct((count, clips), F32),
+            jax.ShapeDtypeStruct((len(columns), clips), F32),
+        )
+
+    early_grown, early_sum, col_sum, text_low = pl.pallas_call(
+        functools.partial(early_tile_kernel, early_rows, columns, len(early_audio)),
+        out_shape=(
+            *tile_shapes(early_rows),
+            jax.ShapeDtypeStruct((len(columns) * clips, width), BF16),
+        ),
+        in_specs=[SMEM] + [VMEM] * (len(early_audio) + len(text)),
+        out_specs=[VMEM] * 4,
+        compiler_params=PARAMS,
+    )(scale, *early_audio, *text)
+    late_grown, late_sum, col_sum = pl.pallas_call(
+        functools.partial(late_tile_kernel, late_rows, columns),
+        out_shape=tile_shapes(late_rows),
+        in_specs=[SMEM] + [VMEM] * (len(late_audio) + 2),
+        out_specs=[VMEM] * 3,
+        compiler_params=PARAMS,
+    )(scale, *late_audio, text_low, col_sum)
     row_sum = jnp.concatenate([early_sum, late_sum], axis=0)
-    row_other, col_other = swap(row_sum, 1), swap(col_sum, 2)
+    row_other, col_other = swap(row_sum, row_bit), swap(col_sum, col_bit)
     rows, audio = early_rows + late_rows, early_audio + late_audio
-    operands = [early_grown, late_grown, row_sum, row_other, col_sum, col_other, *audio, *text]
+    operands = [early_grown, late_grown, row_sum, row_other, col_sum, col_other, *audio, text_low]
 
     def grads(pick, kind):
         return pl.pallas_call(
-            functools.partial(grad_kernel, rows, columns, pick),
+            functools.partial(grad_kernel, rows, columns, row_bit, col_bit, pick),
             out_shape=[kind, kind],
             in_specs=[VMEM] * len(operands),
             out_specs=[VMEM, VMEM],
             compiler_params=PARAMS,
         )(*operands)
 
-    audio_sent, text_sent = grads((1, 2), block_low)
-    text_parts, audio_parts = [swap(text_sent, 2)], [swap(audio_sent, 1)]
+    audio_sent, text_sent = grads((row_bit, col_bit), block_low)
+    text_parts, audio_parts = [swap(text_sent, col_bit)], [swap(audio_sent, row_bit)]
     audio_own, text_own = grads((0, 0), block_full)
     text_parts.insert(0, text_own)
     audio_parts.insert(0, audio_own)

time: 37 us -> 35.5 us (0.959); the launches traced: 37.7 us -> 35.7 us
  waiting for transfers between devices: 15.8 us -> 9.03 us
  starting transfers between devices: 12.6 us -> 18.4 us
  Pallas kernels: 7.85 us -> 6.9 us
    ppermute x10, waiting for transfers between devices: 15.8 us -> 9.03 us  [swap(): return lax.ppermute(block, 'blk', [(i ^ offset, i) for i in range(count)])]
    ppermute x10, starting transfers between devices: 12.6 us -> 18.4 us  [swap(): return lax.ppermute(block, 'blk', [(i ^ offset, i) for i in range(count)])]
    pallas_call x5 -> x4, Pallas kernels: 3.03 us -> 2.12 us  [the longest x2 0.97 us: grads(): pl.pallas_call(functools.partial(grad_kernel, rows, columns, row_bit, col...]
  transfers between devices with their start and end apart: 10 -> 10, of which waited for: 7 -> 5; matrix products, arithmetic and copies ran while one was open for 0% -> 0% of each run, Pallas kernels for 13% -> 14%
where the time goes in v6:
time: 35.5 us; the launch traced here: 35.7 us
  starting transfers between devices  18.4 us (52%)
  waiting for transfers between devices  9.03 us (25%)
  Pallas kernels  6.9 us (19%)
  between operations  1.35 us (4%)
    ppermute x10, starting transfers between devices, swap(): return lax.ppermute(block, 'blk', [(i ^ offset, i) for i in range(count)])  18.4 us
    ppermute x10, waiting for transfers between devices, swap(): return lax.ppermute(block, 'blk', [(i ^ offset, i) for i in range(count)])  9.03 us
    pallas_call x1, Pallas kernels, local(): pl.pallas_call(functools.partial(frames_kernel, chunks), out_shape=(block...  3.75 us
    pallas_call x1, Pallas kernels, local(): pl.pallas_call(functools.partial(final_kernel, pair_count, len(sides) //...  1.03 us
    pallas_call x2, Pallas kernels, grads(): pl.pallas_call(functools.partial(grad_kernel, rows, columns, row_bit, col...  0.97 us
    pallas_call x1, Pallas kernels, local(): pl.pallas_call(functools.partial(early_tile_kernel, early_rows, columns,...  0.77 us
  transfers between devices with their start and end apart: 10, of which 5 were waited for; matrix products, arithmetic and copies ran while one was open for 0% of the time, Pallas kernels for 14%

profile of v6, /device:TPU:0, one launch (start us, length us, event | category | flops | bytes accessed | tf_op | source)
XLA Modules:
  0.0 35.7 jit_solution(13505621104383305874)
XLA Ops:
  0.6 4.1 %collective-permute-start.2 = (bf16[128,512]{1,0:T(8,128)(2,1)}, bf16[128,512]{1,0:T(8,128)(2,1)S(1)}, u32[]{:S(2)}, u32[]{:S(2)}) collective-permute-start(bf16[128,512]{1,0:T(8,128)(2,1)} %refs_4_.3), channel_id=1, source_target_pairs={{16,0},{20,4},{24,8},{28,12},{0,16},{4,20},{8,24},{12,28},{17,1},{... | collective-permute-start | bytes 393224 | tf_op jit(solution)/shard_map/ppermute | solution.py:33
  4.7 3.8 %shard_map.86 = (f32[128,512]{1,0:T(8,128)S(1)}, bf16[128,512]{1,0:T(8,128)(2,1)S(1)}) custom-call(s32[1,128]{1,0:T(1,128)} %bitcast.7, f32[1,512]{1,0:T(1,128)} %bitcast.6, bf16[768,512]{1,0:T(8,128)(2,1)} %refs_2_.1, bf16[512,512]{1,0:T(8,128)(2,1)} %refs_3_.2, bf16[4096,768]{1,0:T(8,128)(2,1)} %refs_4_.2), custom_call_target="tpu_custom_call" | custom-call | tf_op jit(solution)/shard_map/pallas_call | solution.py:229
  8.5 0.1 collective-permute-start
  8.6 2.8 %collective-permute-start.3 = (bf16[128,512]{1,0:T(8,128)(2,1)S(1)}, bf16[128,512]{1,0:T(8,128)(2,1)S(1)}, u32[]{:S(2)}, u32[]{:S(2)}) collective-permute-start(bf16[128,512]{1,0:T(8,128)(2,1)S(1)} %copy-done), channel_id=1, source_target_pairs={{4,0},{0,4},{12,8},{8,12},{20,16},{16,20},{28,24},{24,28},{5,1},{1... | collective-permute-start | bytes 393224 | tf_op jit(solution)/shard_map/ppermute | solution.py:33
  11.4 0.6 %collective-permute-start.1 = (bf16[128,512]{1,0:T(8,128)(2,1)S(1)}, bf16[128,512]{1,0:T(8,128)(2,1)S(1)}, u32[]{:S(2)}, u32[]{:S(2)}) collective-permute-start(bf16[128,512]{1,0:T(8,128)(2,1)S(1)} %get-tuple-element.17.refs_0_.refs_6_.refs_5_), channel_id=1, source_target_pairs={{8,0},{12,4},{0,8},{4,12},{24,16},{28,20},{16,24},{20,28},{9,1},{1... | collective-permute-start | bytes 393224 | tf_op jit(solution)/shard_map/ppermute | solution.py:33
  12.0 0.0 collective-permute-done.2.refs_4_
  12.0 1.2 %collective-permute-start.4 = (bf16[128,512]{1,0:T(8,128)(2,1)S(1)}, bf16[128,512]{1,0:T(8,128)(2,1)S(1)}, u32[]{:S(2)}, u32[]{:S(2)}) collective-permute-start(bf16[128,512]{1,0:T(8,128)(2,1)S(1)} %collective-permute-done.2.refs_4_), channel_id=1, source_target_pairs={{4,0},{0,4},{12,8},{8,12},{20,16},{16,20},{28,24},{24,28},{5,1},{1... | collective-permute-start | bytes 393224 | tf_op jit(solution)/shard_map/ppermute | solution.py:33
  13.3 3.3 %collective-permute-done.refs_1_.refs_7_ = bf16[128,512]{1,0:T(8,128)(2,1)S(1)} collective-permute-done((bf16[128,512]{1,0:T(8,128)(2,1)S(1)}, bf16[128,512]{1,0:T(8,128)(2,1)S(1)}, u32[]{:S(2)}, u32[]{:S(2)}) %collective-permute-start) | collective-permute-done | bytes 131104 | tf_op jit(solution)/shard_map/ppermute | solution.py:33
  16.6 1.9 %collective-permute-start.5 = (bf16[128,512]{1,0:T(8,128)(2,1)S(1)}, bf16[128,512]{1,0:T(8,128)(2,1)S(1)}, u32[]{:S(2)}, u32[]{:S(2)}) collective-permute-start(bf16[128,512]{1,0:T(8,128)(2,1)S(1)} %collective-permute-done.refs_1_.refs_7_), channel_id=1, source_target_pairs={{8,0},{12,4},{0,8},{4,12},{24,16},{28,20},{16,24},{20,28},{9,1},{1... | collective-permute-start | bytes 393224 | tf_op jit(solution)/shard_map/ppermute | solution.py:33
  19.1 0.0 collective-permute-done.3.refs_5_
  19.1 0.0 collective-permute-done.1.refs_2_.refs_8_
  19.1 0.8 %shard_map.87 = (f32[384,512]{1,0:T(8,128)S(1)}, f32[3,128]{1,0:T(4,128)S(1)}, f32[4,128]{1,0:T(4,128)S(1)}, bf16[512,512]{1,0:T(8,128)(2,1)S(1)}) custom-call(f32[1,1]{1,0:T(1,128)} %bitcast.3.scale_ref, bf16[128,512]{1,0:T(8,128)(2,1)S(1)} %get-tuple-element.17.refs_0_.refs_6_.refs_5_, bf16[128,512]{1,0:T(8,128)(2,1)S(1)} %collective-permute-done.refs_1_.refs_7_, ...), custom_call_target="tpu_custom_call" | custom-call | tf_op jit(solution)/shard_map/pallas_call | solution.py:278
  19.9 1.7 %collective-permute-done.5.refs_0_.refs_9_ = bf16[128,512]{1,0:T(8,128)(2,1)S(1)} collective-permute-done((bf16[128,512]{1,0:T(8,128)(2,1)S(1)}, bf16[128,512]{1,0:T(8,128)(2,1)S(1)}, u32[]{:S(2)}, u32[]{:S(2)}) %collective-permute-start.5) | collective-permute-done | bytes 131104 | tf_op jit(solution)/shard_map/ppermute | solution.py:33
  21.6 0.4 %shard_map.88 = (f32[128,512]{1,0:T(8,128)S(1)}, f32[1,128]{1,0:T(1,128)S(1)}, f32[4,128]{1,0:T(4,128)S(1)}) custom-call(f32[1,1]{1,0:T(1,128)} %bitcast.4.scale_ref, bf16[128,512]{1,0:T(8,128)(2,1)S(1)} %collective-permute-done.5.refs_0_.refs_9_, bf16[512,512]{1,0:T(8,128)(2,1)S(1)} %get-tuple-element.19.refs_1_.refs_10_, ...), custom_call_target="tpu_custom_call" | custom-call | tf_op jit(solution)/shard_map/pallas_call | solution.py:288
  21.9 1.9 %collective-permute-start.6 = (f32[4,128]{1,0:T(4,128)S(1)}, f32[4,128]{1,0:T(4,128)S(1)}, u32[]{:S(2)}, u32[]{:S(2)}) collective-permute-start(f32[4,128]{1,0:T(4,128)S(1)} %pad_maximum_fusion.refs_2_), channel_id=1, source_target_pairs={{8,0},{12,4},{0,8},{4,12},{24,16},{28,20},{16,24},{20,28},{9,1},{1... | collective-permute-start | bytes 6152 | tf_op jit(solution)/shard_map/ppermute | solution.py:33
  23.9 2.0 %collective-permute-start.7 = (f32[4,128]{1,0:T(4,128)S(1)}, f32[4,128]{1,0:T(4,128)S(1)}, u32[]{:S(2)}, u32[]{:S(2)}) collective-permute-start(f32[4,128]{1,0:T(4,128)S(1)} %get-tuple-element.25.refs_4_), channel_id=1, source_target_pairs={{4,0},{0,4},{12,8},{8,12},{20,16},{16,20},{28,24},{24,28},{5,1},{1... | collective-permute-start | bytes 6152 | tf_op jit(solution)/shard_map/ppermute | solution.py:33
  25.9 1.6 %collective-permute-done.7.refs_5_ = f32[4,128]{1,0:T(4,128)S(1)} collective-permute-done((f32[4,128]{1,0:T(4,128)S(1)}, f32[4,128]{1,0:T(4,128)S(1)}, u32[]{:S(2)}, u32[]{:S(2)}) %collective-permute-start.7) | collective-permute-done | bytes 2080 | tf_op jit(solution)/shard_map/ppermute | solution.py:33
  27.5 0.5 %shard_map.90 = (bf16[128,512]{1,0:T(8,128)(2,1)S(1)}, bf16[128,512]{1,0:T(8,128)(2,1)S(1)}) custom-call(f32[384,512]{1,0:T(8,128)S(1)} %get-tuple-element.20.refs_0_, f32[128,512]{1,0:T(8,128)S(1)} %get-tuple-element.22.refs_1_, f32[4,128]{1,0:T(4,128)S(1)} %pad_maximum_fusion.refs_2_, f32[4,128]{1,0:T(4,128)S(1)} %collective-permute-done.6.refs_3_, ...), custom_call_target="tpu_custom_call" | custom-call | tf_op jit(solution)/shard_map/pallas_call | solution.py:301
  28.0 1.8 %collective-permute-start.8 = (bf16[128,512]{1,0:T(8,128)(2,1)S(1)}, bf16[128,512]{1,0:T(8,128)(2,1)S(1)}, u32[]{:S(2)}, u32[]{:S(2)}) collective-permute-start(bf16[128,512]{1,0:T(8,128)(2,1)S(1)} %get-tuple-element.27), channel_id=1, source_target_pairs={{8,0},{12,4},{0,8},{4,12},{24,16},{28,20},{16,24},{20,28},{9,1},{1... | collective-permute-start | bytes 393224 | tf_op jit(solution)/shard_map/ppermute | solution.py:33
  29.7 2.0 %collective-permute-start.9 = (bf16[128,512]{1,0:T(8,128)(2,1)S(1)}, bf16[128,512]{1,0:T(8,128)(2,1)S(1)}, u32[]{:S(2)}, u32[]{:S(2)}) collective-permute-start(bf16[128,512]{1,0:T(8,128)(2,1)S(1)} %get-tuple-element.29), channel_id=1, source_target_pairs={{4,0},{0,4},{12,8},{8,12},{20,16},{16,20},{28,24},{24,28},{5,1},{1... | collective-permute-start | bytes 393224 | tf_op jit(solution)/shard_map/ppermute | solution.py:33
  31.8 0.5 %shard_map.89 = (f32[128,512]{1,0:T(8,128)S(1)}, f32[128,512]{1,0:T(8,128)S(1)}) custom-call(f32[384,512]{1,0:T(8,128)S(1)} %get-tuple-element.20.refs_0_, f32[128,512]{1,0:T(8,128)S(1)} %get-tuple-element.22.refs_1_, f32[4,128]{1,0:T(4,128)S(1)} %pad_maximum_fusion.refs_2_, f32[4,128]{1,0:T(4,128)S(1)} %collective-permute-done.6.refs_3_, ...), custom_call_target="tpu_custom_call" | custom-call | tf_op jit(solution)/shard_map/pallas_call | solution.py:301
  32.3 0.7 %collective-permute-done.8.refs_3_ = bf16[128,512]{1,0:T(8,128)(2,1)S(1)} collective-permute-done((bf16[128,512]{1,0:T(8,128)(2,1)S(1)}, bf16[128,512]{1,0:T(8,128)(2,1)S(1)}, u32[]{:S(2)}, u32[]{:S(2)}) %collective-permute-start.8) | collective-permute-done | bytes 131104 | tf_op jit(solution)/shard_map/ppermute | solution.py:33
  33.0 1.7 %collective-permute-done.9.refs_7_ = bf16[128,512]{1,0:T(8,128)(2,1)S(1)} collective-permute-done((bf16[128,512]{1,0:T(8,128)(2,1)S(1)}, bf16[128,512]{1,0:T(8,128)(2,1)S(1)}, u32[]{:S(2)}, u32[]{:S(2)}) %collective-permute-start.9) | collective-permute-done | bytes 131104 | tf_op jit(solution)/shard_map/ppermute | solution.py:33
  34.7 1.0 %shard_map.91 = (f32[128,512]{1,0:T(8,128)}, f32[128,512]{1,0:T(8,128)}) custom-call(f32[1,1]{1,0:T(1,128)} %bitcast.5.scale_ref, f32[128,512]{1,0:T(8,128)S(1)} %get-tuple-element.16.refs_0_, bf16[512,512]{1,0:T(8,128)(2,1)S(1)} %get-tuple-element.19.refs_1_.refs_10_, f32[128,512]{1,0:T(8,128)S(1)} %get-tuple-element.26.refs_2_, ...), custom_call_target="tpu_custom_call" | custom-call | tf_op jit(solution)/shard_map/pallas_call | solution.py:316
  (5 shorter events, 0.0 us)
Async XLA Ops:
  0.6 8.0 %copy-start = (bf16[128,512]{1,0:T(8,128)(2,1)S(1)}, bf16[128,512]{1,0:T(8,128)(2,1)}, u32[]{:S(2)}) copy-start(bf16[128,512]{1,0:T(8,128)(2,1)} %refs_4_.3) | copy-start | bytes 393220
  0.6 11.4 %collective-permute-start.2 = (bf16[128,512]{1,0:T(8,128)(2,1)}, bf16[128,512]{1,0:T(8,128)(2,1)S(1)}, u32[]{:S(2)}, u32[]{:S(2)}) collective-permute-start(bf16[128,512]{1,0:T(8,128)(2,1)} %refs_4_.3), channel_id=1, source_target_pairs={{16,0},{20,4},{24,8},{28,12},{0,16},{4,20},{8,24},{12,28},{17,1},{... | collective-permute-start | bytes 393224 | tf_op jit(solution)/shard_map/ppermute | solution.py:33
  8.5 8.1 %collective-permute-start = (bf16[128,512]{1,0:T(8,128)(2,1)S(1)}, bf16[128,512]{1,0:T(8,128)(2,1)S(1)}, u32[]{:S(2)}, u32[]{:S(2)}) collective-permute-start(bf16[128,512]{1,0:T(8,128)(2,1)S(1)} %get-tuple-element.17.refs_0_.refs_6_.refs_5_), channel_id=1, source_target_pairs={{16,0},{20,4},{24,8},{28,12},{0,16},{4,20},{8,24},{12,28},{17,1},{... | collective-permute-start | bytes 393224 | tf_op jit(solution)/shard_map/ppermute | solution.py:33
  8.6 10.5 %collective-permute-start.3 = (bf16[128,512]{1,0:T(8,128)(2,1)S(1)}, bf16[128,512]{1,0:T(8,128)(2,1)S(1)}, u32[]{:S(2)}, u32[]{:S(2)}) collective-permute-start(bf16[128,512]{1,0:T(8,128)(2,1)S(1)} %copy-done), channel_id=1, source_target_pairs={{4,0},{0,4},{12,8},{8,12},{20,16},{16,20},{28,24},{24,28},{5,1},{1... | collective-permute-start | bytes 393224 | tf_op jit(solution)/shard_map/ppermute | solution.py:33
  11.4 7.7 %collective-permute-start.1 = (bf16[128,512]{1,0:T(8,128)(2,1)S(1)}, bf16[128,512]{1,0:T(8,128)(2,1)S(1)}, u32[]{:S(2)}, u32[]{:S(2)}) collective-permute-start(bf16[128,512]{1,0:T(8,128)(2,1)S(1)} %get-tuple-element.17.refs_0_.refs_6_.refs_5_), channel_id=1, source_target_pairs={{8,0},{12,4},{0,8},{4,12},{24,16},{28,20},{16,24},{20,28},{9,1},{1... | collective-permute-start | bytes 393224 | tf_op jit(solution)/shard_map/ppermute | solution.py:33
  12.0 7.1 %collective-permute-start.4 = (bf16[128,512]{1,0:T(8,128)(2,1)S(1)}, bf16[128,512]{1,0:T(8,128)(2,1)S(1)}, u32[]{:S(2)}, u32[]{:S(2)}) collective-permute-start(bf16[128,512]{1,0:T(8,128)(2,1)S(1)} %collective-permute-done.2.refs_4_), channel_id=1, source_target_pairs={{4,0},{0,4},{12,8},{8,12},{20,16},{16,20},{28,24},{24,28},{5,1},{1... | collective-permute-start | bytes 393224 | tf_op jit(solution)/shard_map/ppermute | solution.py:33
  16.6 5.0 %collective-permute-start.5 = (bf16[128,512]{1,0:T(8,128)(2,1)S(1)}, bf16[128,512]{1,0:T(8,128)(2,1)S(1)}, u32[]{:S(2)}, u32[]{:S(2)}) collective-permute-start(bf16[128,512]{1,0:T(8,128)(2,1)S(1)} %collective-permute-done.refs_1_.refs_7_), channel_id=1, source_target_pairs={{8,0},{12,4},{0,8},{4,12},{24,16},{28,20},{16,24},{20,28},{9,1},{1... | collective-permute-start | bytes 393224 | tf_op jit(solution)/shard_map/ppermute | solution.py:33
  21.9 3.9 %collective-permute-start.6 = (f32[4,128]{1,0:T(4,128)S(1)}, f32[4,128]{1,0:T(4,128)S(1)}, u32[]{:S(2)}, u32[]{:S(2)}) collective-permute-start(f32[4,128]{1,0:T(4,128)S(1)} %pad_maximum_fusion.refs_2_), channel_id=1, source_target_pairs={{8,0},{12,4},{0,8},{4,12},{24,16},{28,20},{16,24},{20,28},{9,1},{1... | collective-permute-start | bytes 6152 | tf_op jit(solution)/shard_map/ppermute | solution.py:33
  23.9 3.6 %collective-permute-start.7 = (f32[4,128]{1,0:T(4,128)S(1)}, f32[4,128]{1,0:T(4,128)S(1)}, u32[]{:S(2)}, u32[]{:S(2)}) collective-permute-start(f32[4,128]{1,0:T(4,128)S(1)} %get-tuple-element.25.refs_4_), channel_id=1, source_target_pairs={{4,0},{0,4},{12,8},{8,12},{20,16},{16,20},{28,24},{24,28},{5,1},{1... | collective-permute-start | bytes 6152 | tf_op jit(solution)/shard_map/ppermute | solution.py:33
  28.0 5.0 %collective-permute-start.8 = (bf16[128,512]{1,0:T(8,128)(2,1)S(1)}, bf16[128,512]{1,0:T(8,128)(2,1)S(1)}, u32[]{:S(2)}, u32[]{:S(2)}) collective-permute-start(bf16[128,512]{1,0:T(8,128)(2,1)S(1)} %get-tuple-element.27), channel_id=1, source_target_pairs={{8,0},{12,4},{0,8},{4,12},{24,16},{28,20},{16,24},{20,28},{9,1},{1... | collective-permute-start | bytes 393224 | tf_op jit(solution)/shard_map/ppermute | solution.py:33
  29.7 5.0 %collective-permute-start.9 = (bf16[128,512]{1,0:T(8,128)(2,1)S(1)}, bf16[128,512]{1,0:T(8,128)(2,1)S(1)}, u32[]{:S(2)}, u32[]{:S(2)}) collective-permute-start(bf16[128,512]{1,0:T(8,128)(2,1)S(1)} %get-tuple-element.29), channel_id=1, source_target_pairs={{4,0},{0,4},{12,8},{8,12},{20,16},{16,20},{28,24},{24,28},{5,1},{1... | collective-permute-start | bytes 393224 | tf_op jit(solution)/shard_map/ppermute | solution.py:33

commit v7 on v6

--- a/solution.py
+++ b/solution.py
@@ -147,8 +147,8 @@
     tile_kernel(rows, columns, audio, text, sums, scale_ref[0, 0], grown_ref, row_ref, col_ref)
 
 
-def grad_kernel(rows, columns, row_bit, col_bit, pick, *refs):
-    block = refs[len(refs) - 1].shape[0]
+def grad_kernel(rows, columns, row_bit, col_bit, pick, pair_count, scale_ref, *refs):
+    block = refs[1].shape[1] // len(columns)
     count = len(rows)
     grown, near = {}, 0
     held = 0
@@ -167,7 +167,7 @@
             total += refs[at].shape[0] // block
             at += 1
     audio, text = blocks_of(audio_refs, rows, block), blocks_of(text_refs, columns, block)
-    audio_out, text_out = refs[at:]
+    sources, outs = ([], refs[at:]) if pair_count is None else (refs[at : at + 2], refs[at + 2 :])
 
     def inverse(offsets, offset, bit, own, other):
         here, there = (pl.ds(offsets.index(k), 1) for k in (offset, offset ^ bit))
@@ -184,27 +184,36 @@
         values = refs[index][pl.ds(k * block, block), pl.ds(c * block, block)]
         return (values * (row_scale[row] + col_scale[column])).astype(BF16)
 
-    total = sum(mm(weights(pick[0], column), text[column][...]) for column in columns)
-    audio_out[...] = total.astype(audio_out.dtype)
-    total = sum(mm(weights(row, pick[1]), audio[row][...], 0, 0) for row in rows)
-    text_out[...] = total.astype(text_out.dtype)
-
-
-def final_kernel(pair_count, count, scale_ref, *refs):
+    def audio_total():
+        return sum(mm(weights(pick[0], column), text[column][...]) for column in columns)
+
+    def text_total():
+        return sum(mm(weights(row, pick[1]), audio[row][...], 0, 0) for row in rows)
+
+    if pair_count is None:
+        outs[0][...] = audio_total().astype(BF16)
+        outs[1][...] = text_total().astype(BF16)
+        return
     factor = scale_ref[0, 0] / (2.0 * pair_count)
+    for side, (total, partner) in enumerate(((audio_total, text), (text_total, audio))):
+        base_ref, unit_ref, inverse_ref = outs[3 * side : 3 * side + 3]
+        values = sources[side][...].astype(F32)
+        base_ref[...] = (total() - 2.0 * partner[0][...].astype(F32)) * factor
+        scaled = lax.rsqrt(jnp.sum(values * values, axis=1, keepdims=True) + epsilon)
+        unit_ref[...] = values * scaled
+        inverse_ref[...] = jnp.broadcast_to(scaled, inverse_ref.shape)
+
+
+def final_kernel(pair_count, sides, scale_ref, *refs):
+    factor = scale_ref[0, 0] / (2.0 * pair_count)
+    outs, stages, sems = refs[4 * sides : 5 * sides], refs[5 * sides : 6 * sides], refs[-1]
     copies = []
-    outs, stages, sems = refs[2 * count :][:2], refs[2 * count + 2 :][:2], refs[-1]
-    for side in range(2):
-        values_ref, partner_ref, *parts = refs[side * count : (side + 1) * count]
-        values = values_ref[...].astype(F32)
-        total = parts[0][...] - 2.0 * partner_ref[pl.ds(0, values.shape[0]), :].astype(F32)
-        for part in parts[1:]:
-            total = total + part[...].astype(F32)
-        total = total * factor
-        inverse = lax.rsqrt(jnp.sum(values * values, axis=1, keepdims=True) + epsilon)
-        unit = values * inverse
+    for side in range(sides):
+        base_ref, unit_ref, inverse_ref, other_ref = refs[4 * side : 4 * side + 4]
+        total = base_ref[...] + other_ref[...].astype(F32) * factor
+        unit = unit_ref[...]
         along = jnp.sum(unit * total, axis=1, keepdims=True)
-        stages[side][...] = (total - unit * along) * inverse
+        stages[side][...] = (total - unit * along) * inverse_ref[:, :1]
         copies.append(pltpu.make_async_copy(stages[side], outs[side], sems.at[side]))
         copies[-1].start()
     for copy in copies:
@@ -297,34 +306,35 @@
     rows, audio = early_rows + late_rows, early_audio + late_audio
     operands = [early_grown, late_grown, row_sum, row_other, col_sum, col_other, *audio, text_low]
 
-    def grads(pick, kind):
+    def grads(pick, extra, pairs, kinds):
         return pl.pallas_call(
-            functools.partial(grad_kernel, rows, columns, row_bit, col_bit, pick),
-            out_shape=[kind, kind],
-            in_specs=[VMEM] * len(operands),
-            out_specs=[VMEM, VMEM],
+            functools.partial(grad_kernel, rows, columns, row_bit, col_bit, pick, pairs),
+            out_shape=kinds,
+            in_specs=[SMEM] + [VMEM] * (len(operands) + len(extra)),
+            out_specs=[VMEM] * len(kinds),
             compiler_params=PARAMS,
-        )(*operands)
-
-    audio_sent, text_sent = grads((row_bit, col_bit), block_low)
-    text_parts, audio_parts = [swap(text_sent, col_bit)], [swap(audio_sent, row_bit)]
-    audio_own, text_own = grads((0, 0), block_full)
-    text_parts.insert(0, text_own)
-    audio_parts.insert(0, audio_own)
-
-    sides = [pooled, text_low, *audio_parts, captions, audio_low, *text_parts]
-    return pl.pallas_call(
-        functools.partial(final_kernel, pair_count, len(sides) // 2),
-        out_shape=(block_full, block_full),
-        in_specs=[SMEM] + [VMEM] * len(sides),
-        out_specs=(HBM, HBM),
-        scratch_shapes=[
-            pltpu.VMEM((clips, width), F32),
-            pltpu.VMEM((clips, width), F32),
-            pltpu.SemaphoreType.DMA((2,)),
-        ],
-        compiler_params=PARAMS,
-    )(scale, *sides)
+        )(scale, *operands, *extra)
+
+    audio_sent, text_sent = grads((row_bit, col_bit), [], None, [block_low] * 2)
+    text_other, audio_other = swap(text_sent, col_bit), swap(audio_sent, row_bit)
+    narrow = jax.ShapeDtypeStruct((clips, 128), F32)
+    prepared = grads((0, 0), [pooled, captions], pair_count, [block_full, block_full, narrow] * 2)
+
+    def final(*inputs):
+        sides = len(inputs) // 4
+        return pl.pallas_call(
+            functools.partial(final_kernel, pair_count, sides),
+            out_shape=[block_full] * sides,
+            in_specs=[SMEM] + [VMEM] * len(inputs),
+            out_specs=[HBM] * sides,
+            scratch_shapes=[pltpu.VMEM((clips, width), F32)] * sides
+            + [pltpu.SemaphoreType.DMA((sides,))],
+            compiler_params=PARAMS,
+        )(scale, *inputs)
+
+    (audio_grad,) = final(*prepared[:3], audio_other)
+    (text_grad,) = final(*prepared[3:], text_other)
+    return audio_grad, text_grad
 
 
 def solution(mesh):

time: 35.5 us -> 34.9 us (0.983); the launches traced: 35.7 us -> 34.7 us
  starting transfers between devices: 18.4 us -> 14 us
  waiting for transfers between devices: 9.03 us -> 11.7 us
  Pallas kernels: 6.9 us -> 7.63 us
    ppermute x10, starting transfers between devices: 18.4 us -> 14 us  [swap(): return lax.ppermute(block, 'blk', [(i ^ offset, i) for i in range(count)])]
    ppermute x10, waiting for transfers between devices: 9.03 us -> 11.7 us  [swap(): return lax.ppermute(block, 'blk', [(i ^ offset, i) for i in range(count)])]
    pallas_call x1 -> x2, Pallas kernels: 1.03 us -> 1.74 us  [final(): pl.pallas_call(functools.partial(final_kernel, pair_count, sides), out_sh...]
  transfers between devices with their start and end apart: 10 -> 10, of which waited for: 5 -> 6; matrix products, arithmetic and copies ran while one was open for 0% -> 0% of each run, Pallas kernels for 14% -> 17%
where the time goes in v7:
time: 34.9 us; the launch traced here: 34.7 us
  starting transfers between devices  14 us (40%)
  waiting for transfers between devices  11.7 us (34%)
  Pallas kernels  7.63 us (22%)
  between operations  1.36 us (4%)
    ppermute x10, starting transfers between devices, swap(): return lax.ppermute(block, 'blk', [(i ^ offset, i) for i in range(count)])  14 us
    ppermute x10, waiting for transfers between devices, swap(): return lax.ppermute(block, 'blk', [(i ^ offset, i) for i in range(count)])  11.7 us
    pallas_call x1, Pallas kernels, local(): pl.pallas_call(functools.partial(frames_kernel, chunks), out_shape=(block...  3.75 us
    pallas_call x2, Pallas kernels, final(): pl.pallas_call(functools.partial(final_kernel, pair_count, sides), out_sh...  1.74 us
    pallas_call x2, Pallas kernels, grads(): pl.pallas_call(functools.partial(grad_kernel, rows, columns, row_bit, col...  1 us
    pallas_call x1, Pallas kernels, local(): pl.pallas_call(functools.partial(early_tile_kernel, early_rows, columns,...  0.77 us
  transfers between devices with their start and end apart: 10, of which 6 were waited for; matrix products, arithmetic and copies ran while one was open for 0% of the time, Pallas kernels for 17%

profile of v7, /device:TPU:0, one launch (start us, length us, event | category | flops | bytes accessed | tf_op | source)
XLA Modules:
  0.0 34.7 jit_solution(6081362056557324509)
XLA Ops:
  0.6 4.1 %collective-permute-start.2 = (bf16[128,512]{1,0:T(8,128)(2,1)}, bf16[128,512]{1,0:T(8,128)(2,1)S(1)}, u32[]{:S(2)}, u32[]{:S(2)}) collective-permute-start(bf16[128,512]{1,0:T(8,128)(2,1)} %refs_12_.1), channel_id=1, source_target_pairs={{16,0},{20,4},{24,8},{28,12},{0,16},{4,20},{8,24},{12,28},{17,1},{... | collective-permute-start | bytes 393224 | tf_op jit(solution)/shard_map/ppermute | solution.py:33
  4.7 3.8 %shard_map.86 = (f32[128,512]{1,0:T(8,128)S(1)}, bf16[128,512]{1,0:T(8,128)(2,1)S(1)}) custom-call(s32[1,128]{1,0:T(1,128)} %bitcast.10, f32[1,512]{1,0:T(1,128)} %bitcast.9, bf16[768,512]{1,0:T(8,128)(2,1)} %refs_2_.1, bf16[512,512]{1,0:T(8,128)(2,1)} %refs_3_.2, bf16[4096,768]{1,0:T(8,128)(2,1)} %refs_4_.1), custom_call_target="tpu_custom_call" | custom-call | tf_op jit(solution)/shard_map/pallas_call | solution.py:238
  8.5 0.1 collective-permute-start
  8.6 1.9 %collective-permute-start.1 = (bf16[128,512]{1,0:T(8,128)(2,1)S(1)}, bf16[128,512]{1,0:T(8,128)(2,1)S(1)}, u32[]{:S(2)}, u32[]{:S(2)}) collective-permute-start(bf16[128,512]{1,0:T(8,128)(2,1)S(1)} %get-tuple-element.20.refs_0_.refs_6_), channel_id=1, source_target_pairs={{8,0},{12,4},{0,8},{4,12},{24,16},{28,20},{16,24},{20,28},{9,1},{1... | collective-permute-start | bytes 393224 | tf_op jit(solution)/shard_map/ppermute | solution.py:33
  10.5 1.5 %collective-permute-start.3 = (bf16[128,512]{1,0:T(8,128)(2,1)S(1)}, bf16[128,512]{1,0:T(8,128)(2,1)S(1)}, u32[]{:S(2)}, u32[]{:S(2)}) collective-permute-start(bf16[128,512]{1,0:T(8,128)(2,1)S(1)} %copy-done), channel_id=1, source_target_pairs={{4,0},{0,4},{12,8},{8,12},{20,16},{16,20},{28,24},{24,28},{5,1},{1... | collective-permute-start | bytes 393224 | tf_op jit(solution)/shard_map/ppermute | solution.py:33
  12.0 0.0 collective-permute-done.2.refs_4_
  12.0 0.8 %collective-permute-start.4 = (bf16[128,512]{1,0:T(8,128)(2,1)S(1)}, bf16[128,512]{1,0:T(8,128)(2,1)S(1)}, u32[]{:S(2)}, u32[]{:S(2)}) collective-permute-start(bf16[128,512]{1,0:T(8,128)(2,1)S(1)} %collective-permute-done.2.refs_4_), channel_id=1, source_target_pairs={{4,0},{0,4},{12,8},{8,12},{20,16},{16,20},{28,24},{24,28},{5,1},{1... | collective-permute-start | bytes 393224 | tf_op jit(solution)/shard_map/ppermute | solution.py:33
  12.8 4.4 %collective-permute-done.refs_1_.refs_7_ = bf16[128,512]{1,0:T(8,128)(2,1)S(1)} collective-permute-done((bf16[128,512]{1,0:T(8,128)(2,1)S(1)}, bf16[128,512]{1,0:T(8,128)(2,1)S(1)}, u32[]{:S(2)}, u32[]{:S(2)}) %collective-permute-start) | collective-permute-done | bytes 131104 | tf_op jit(solution)/shard_map/ppermute | solution.py:33
  17.2 0.4 %collective-permute-start.5 = (bf16[128,512]{1,0:T(8,128)(2,1)S(1)}, bf16[128,512]{1,0:T(8,128)(2,1)S(1)}, u32[]{:S(2)}, u32[]{:S(2)}) collective-permute-start(bf16[128,512]{1,0:T(8,128)(2,1)S(1)} %collective-permute-done.refs_1_.refs_7_), channel_id=1, source_target_pairs={{8,0},{12,4},{0,8},{4,12},{24,16},{28,20},{16,24},{20,28},{9,1},{1... | collective-permute-start | bytes 393224 | tf_op jit(solution)/shard_map/ppermute | solution.py:33
  18.3 0.8 %shard_map.87 = (f32[384,512]{1,0:T(8,128)S(1)}, f32[3,128]{1,0:T(4,128)S(1)}, f32[4,128]{1,0:T(4,128)S(1)}, bf16[512,512]{1,0:T(8,128)(2,1)S(1)}) custom-call(f32[1,1]{1,0:T(1,128)} %bitcast.3.scale_ref, bf16[128,512]{1,0:T(8,128)(2,1)S(1)} %get-tuple-element.20.refs_0_.refs_6_, bf16[128,512]{1,0:T(8,128)(2,1)S(1)} %collective-permute-done.refs_1_.refs_7_, ...), custom_call_target="tpu_custom_call" | custom-call | tf_op jit(solution)/shard_map/pallas_call | solution.py:287
  19.1 3.1 %collective-permute-done.5.refs_0_.refs_9_ = bf16[128,512]{1,0:T(8,128)(2,1)S(1)} collective-permute-done((bf16[128,512]{1,0:T(8,128)(2,1)S(1)}, bf16[128,512]{1,0:T(8,128)(2,1)S(1)}, u32[]{:S(2)}, u32[]{:S(2)}) %collective-permute-start.5) | collective-permute-done | bytes 131104 | tf_op jit(solution)/shard_map/ppermute | solution.py:33
  22.2 0.4 %shard_map.88 = (f32[128,512]{1,0:T(8,128)S(1)}, f32[1,128]{1,0:T(1,128)S(1)}, f32[4,128]{1,0:T(4,128)S(1)}) custom-call(f32[1,1]{1,0:T(1,128)} %bitcast.4.scale_ref, bf16[128,512]{1,0:T(8,128)(2,1)S(1)} %collective-permute-done.5.refs_0_.refs_9_, bf16[512,512]{1,0:T(8,128)(2,1)S(1)} %get-tuple-element.23.refs_1_.refs_10_, ...), custom_call_target="tpu_custom_call" | custom-call | tf_op jit(solution)/shard_map/pallas_call | solution.py:297
  22.6 0.9 %collective-permute-start.6 = (f32[4,128]{1,0:T(4,128)S(1)}, f32[4,128]{1,0:T(4,128)S(1)}, u32[]{:S(2)}, u32[]{:S(2)}) collective-permute-start(f32[4,128]{1,0:T(4,128)S(1)} %pad_maximum_fusion.refs_2_), channel_id=1, source_target_pairs={{8,0},{12,4},{0,8},{4,12},{24,16},{28,20},{16,24},{20,28},{9,1},{1... | collective-permute-start | bytes 6152 | tf_op jit(solution)/shard_map/ppermute | solution.py:33
  23.5 1.5 %collective-permute-start.7 = (f32[4,128]{1,0:T(4,128)S(1)}, f32[4,128]{1,0:T(4,128)S(1)}, u32[]{:S(2)}, u32[]{:S(2)}) collective-permute-start(f32[4,128]{1,0:T(4,128)S(1)} %get-tuple-element.28.refs_4_), channel_id=1, source_target_pairs={{4,0},{0,4},{12,8},{8,12},{20,16},{16,20},{28,24},{24,28},{5,1},{1... | collective-permute-start | bytes 6152 | tf_op jit(solution)/shard_map/ppermute | solution.py:33
  25.0 1.2 %collective-permute-done.6.refs_3_ = f32[4,128]{1,0:T(4,128)S(1)} collective-permute-done((f32[4,128]{1,0:T(4,128)S(1)}, f32[4,128]{1,0:T(4,128)S(1)}, u32[]{:S(2)}, u32[]{:S(2)}) %collective-permute-start.6) | collective-permute-done | bytes 2080 | tf_op jit(solution)/shard_map/ppermute | solution.py:33
  26.3 0.9 %collective-permute-done.7.refs_5_ = f32[4,128]{1,0:T(4,128)S(1)} collective-permute-done((f32[4,128]{1,0:T(4,128)S(1)}, f32[4,128]{1,0:T(4,128)S(1)}, u32[]{:S(2)}, u32[]{:S(2)}) %collective-permute-start.7) | collective-permute-done | bytes 2080 | tf_op jit(solution)/shard_map/ppermute | solution.py:33
  27.1 0.5 %shard_map.90 = (bf16[128,512]{1,0:T(8,128)(2,1)S(1)}, bf16[128,512]{1,0:T(8,128)(2,1)S(1)}) custom-call(f32[1,1]{1,0:T(1,128)} %bitcast.6.scale_ref, f32[384,512]{1,0:T(8,128)S(1)} %get-tuple-element.22.refs_0_, f32[128,512]{1,0:T(8,128)S(1)} %get-tuple-element.25.refs_1_, f32[4,128]{1,0:T(4,128)S(1)} %pad_maximum_fusion.refs_2_, ...), custom_call_target="tpu_custom_call" | custom-call | tf_op jit(solution)/shard_map/pallas_call | solution.py:310
  27.6 1.2 %collective-permute-start.8 = (bf16[128,512]{1,0:T(8,128)(2,1)S(1)}, bf16[128,512]{1,0:T(8,128)(2,1)S(1)}, u32[]{:S(2)}, u32[]{:S(2)}) collective-permute-start(bf16[128,512]{1,0:T(8,128)(2,1)S(1)} %get-tuple-element.33), channel_id=1, source_target_pairs={{8,0},{12,4},{0,8},{4,12},{24,16},{28,20},{16,24},{20,28},{9,1},{1... | collective-permute-start | bytes 393224 | tf_op jit(solution)/shard_map/ppermute | solution.py:33
  28.8 1.5 %collective-permute-start.9 = (bf16[128,512]{1,0:T(8,128)(2,1)S(1)}, bf16[128,512]{1,0:T(8,128)(2,1)S(1)}, u32[]{:S(2)}, u32[]{:S(2)}) collective-permute-start(bf16[128,512]{1,0:T(8,128)(2,1)S(1)} %get-tuple-element.37), channel_id=1, source_target_pairs={{4,0},{0,4},{12,8},{8,12},{20,16},{16,20},{28,24},{24,28},{5,1},{1... | collective-permute-start | bytes 393224 | tf_op jit(solution)/shard_map/ppermute | solution.py:33
  30.4 0.5 %shard_map.89 = (f32[128,512]{1,0:T(8,128)S(1)}, f32[128,512]{1,0:T(8,128)S(1)}, f32[128,128]{1,0:T(8,128)S(1)}, f32[128,512]{1,0:T(8,128)S(1)}, f32[128,512]{1,0:T(8,128)S(1)}, /*index=5*/f32[128,128]{1,0:T(8,128)S(1)}) custom-call(f32[1,1]{1,0:T(1,128)} %bitcast.5.scale_ref, f32[384,512]{1,0:T(8,128)S(1)} %get-tuple-element.22.refs_0_, ...), custom_call_target="tpu_custom_call" | custom-call | tf_op jit(solution)/shard_map/pallas_call | solution.py:310
  30.9 1.8 %collective-permute-done.8.refs_3_ = bf16[128,512]{1,0:T(8,128)(2,1)S(1)} collective-permute-done((bf16[128,512]{1,0:T(8,128)(2,1)S(1)}, bf16[128,512]{1,0:T(8,128)(2,1)S(1)}, u32[]{:S(2)}, u32[]{:S(2)}) %collective-permute-start.8) | collective-permute-done | bytes 131104 | tf_op jit(solution)/shard_map/ppermute | solution.py:33
  32.6 0.9 %shard_map.91 = f32[128,512]{1,0:T(8,128)} custom-call(f32[1,1]{1,0:T(1,128)} %bitcast.7.scale_ref, f32[128,512]{1,0:T(8,128)S(1)} %get-tuple-element.30.refs_0_, f32[128,512]{1,0:T(8,128)S(1)} %get-tuple-element.31.refs_1_, f32[128,128]{1,0:T(8,128)S(1)} %get-tuple-element.32.refs_2_, bf16[128,512]{1,0:T(8,128)(2,1)S(1)} %collective-permute-done.8.refs_3_), custom_call_target="tpu_custom_call" | custom-call | tf_op jit(solution)/shard_map/pallas_call | solution.py:325
  33.5 0.3 collective-permute-done.9.refs_3_
  33.8 0.9 %shard_map.92 = f32[128,512]{1,0:T(8,128)} custom-call(f32[1,1]{1,0:T(1,128)} %bitcast.8.scale_ref, f32[128,512]{1,0:T(8,128)S(1)} %get-tuple-element.34.refs_0_, f32[128,512]{1,0:T(8,128)S(1)} %get-tuple-element.35.refs_1_, f32[128,128]{1,0:T(8,128)S(1)} %get-tuple-element.36.refs_2_, bf16[128,512]{1,0:T(8,128)(2,1)S(1)} %collective-permute-done.9.refs_3_), custom_call_target="tpu_custom_call" | custom-call | tf_op jit(solution)/shard_map/pallas_call | solution.py:325
  (6 shorter events, 0.0 us)
Async XLA Ops:
  0.6 9.9 %copy-start = (bf16[128,512]{1,0:T(8,128)(2,1)S(1)}, bf16[128,512]{1,0:T(8,128)(2,1)}, u32[]{:S(2)}) copy-start(bf16[128,512]{1,0:T(8,128)(2,1)} %refs_12_.1) | copy-start | bytes 393220
  0.6 11.4 %collective-permute-start.2 = (bf16[128,512]{1,0:T(8,128)(2,1)}, bf16[128,512]{1,0:T(8,128)(2,1)S(1)}, u32[]{:S(2)}, u32[]{:S(2)}) collective-permute-start(bf16[128,512]{1,0:T(8,128)(2,1)} %refs_12_.1), channel_id=1, source_target_pairs={{16,0},{20,4},{24,8},{28,12},{0,16},{4,20},{8,24},{12,28},{17,1},{... | collective-permute-start | bytes 393224 | tf_op jit(solution)/shard_map/ppermute | solution.py:33
  8.5 8.7 %collective-permute-start = (bf16[128,512]{1,0:T(8,128)(2,1)S(1)}, bf16[128,512]{1,0:T(8,128)(2,1)S(1)}, u32[]{:S(2)}, u32[]{:S(2)}) collective-permute-start(bf16[128,512]{1,0:T(8,128)(2,1)S(1)} %get-tuple-element.20.refs_0_.refs_6_), channel_id=1, source_target_pairs={{16,0},{20,4},{24,8},{28,12},{0,16},{4,20},{8,24},{12,28},{17,1},{... | collective-permute-start | bytes 393224 | tf_op jit(solution)/shard_map/ppermute | solution.py:33
  8.6 9.7 %collective-permute-start.1 = (bf16[128,512]{1,0:T(8,128)(2,1)S(1)}, bf16[128,512]{1,0:T(8,128)(2,1)S(1)}, u32[]{:S(2)}, u32[]{:S(2)}) collective-permute-start(bf16[128,512]{1,0:T(8,128)(2,1)S(1)} %get-tuple-element.20.refs_0_.refs_6_), channel_id=1, source_target_pairs={{8,0},{12,4},{0,8},{4,12},{24,16},{28,20},{16,24},{20,28},{9,1},{1... | collective-permute-start | bytes 393224 | tf_op jit(solution)/shard_map/ppermute | solution.py:33
  10.5 7.8 %collective-permute-start.3 = (bf16[128,512]{1,0:T(8,128)(2,1)S(1)}, bf16[128,512]{1,0:T(8,128)(2,1)S(1)}, u32[]{:S(2)}, u32[]{:S(2)}) collective-permute-start(bf16[128,512]{1,0:T(8,128)(2,1)S(1)} %copy-done), channel_id=1, source_target_pairs={{4,0},{0,4},{12,8},{8,12},{20,16},{16,20},{28,24},{24,28},{5,1},{1... | collective-permute-start | bytes 393224 | tf_op jit(solution)/shard_map/ppermute | solution.py:33
  12.0 6.3 %collective-permute-start.4 = (bf16[128,512]{1,0:T(8,128)(2,1)S(1)}, bf16[128,512]{1,0:T(8,128)(2,1)S(1)}, u32[]{:S(2)}, u32[]{:S(2)}) collective-permute-start(bf16[128,512]{1,0:T(8,128)(2,1)S(1)} %collective-permute-done.2.refs_4_), channel_id=1, source_target_pairs={{4,0},{0,4},{12,8},{8,12},{20,16},{16,20},{28,24},{24,28},{5,1},{1... | collective-permute-start | bytes 393224 | tf_op jit(solution)/shard_map/ppermute | solution.py:33
  17.2 5.0 %collective-permute-start.5 = (bf16[128,512]{1,0:T(8,128)(2,1)S(1)}, bf16[128,512]{1,0:T(8,128)(2,1)S(1)}, u32[]{:S(2)}, u32[]{:S(2)}) collective-permute-start(bf16[128,512]{1,0:T(8,128)(2,1)S(1)} %collective-permute-done.refs_1_.refs_7_), channel_id=1, source_target_pairs={{8,0},{12,4},{0,8},{4,12},{24,16},{28,20},{16,24},{20,28},{9,1},{1... | collective-permute-start | bytes 393224 | tf_op jit(solution)/shard_map/ppermute | solution.py:33
  22.6 3.7 %collective-permute-start.6 = (f32[4,128]{1,0:T(4,128)S(1)}, f32[4,128]{1,0:T(4,128)S(1)}, u32[]{:S(2)}, u32[]{:S(2)}) collective-permute-start(f32[4,128]{1,0:T(4,128)S(1)} %pad_maximum_fusion.refs_2_), channel_id=1, source_target_pairs={{8,0},{12,4},{0,8},{4,12},{24,16},{28,20},{16,24},{20,28},{9,1},{1... | collective-permute-start | bytes 6152 | tf_op jit(solution)/shard_map/ppermute | solution.py:33
  23.5 3.6 %collective-permute-start.7 = (f32[4,128]{1,0:T(4,128)S(1)}, f32[4,128]{1,0:T(4,128)S(1)}, u32[]{:S(2)}, u32[]{:S(2)}) collective-permute-start(f32[4,128]{1,0:T(4,128)S(1)} %get-tuple-element.28.refs_4_), channel_id=1, source_target_pairs={{4,0},{0,4},{12,8},{8,12},{20,16},{16,20},{28,24},{24,28},{5,1},{1... | collective-permute-start | bytes 6152 | tf_op jit(solution)/shard_map/ppermute | solution.py:33
  27.6 5.0 %collective-permute-start.8 = (bf16[128,512]{1,0:T(8,128)(2,1)S(1)}, bf16[128,512]{1,0:T(8,128)(2,1)S(1)}, u32[]{:S(2)}, u32[]{:S(2)}) collective-permute-start(bf16[128,512]{1,0:T(8,128)(2,1)S(1)} %get-tuple-element.33), channel_id=1, source_target_pairs={{8,0},{12,4},{0,8},{4,12},{24,16},{28,20},{16,24},{20,28},{9,1},{1... | collective-permute-start | bytes 393224 | tf_op jit(solution)/shard_map/ppermute | solution.py:33
  28.8 5.0 %collective-permute-start.9 = (bf16[128,512]{1,0:T(8,128)(2,1)S(1)}, bf16[128,512]{1,0:T(8,128)(2,1)S(1)}, u32[]{:S(2)}, u32[]{:S(2)}) collective-permute-start(bf16[128,512]{1,0:T(8,128)(2,1)S(1)} %get-tuple-element.37), channel_id=1, source_target_pairs={{4,0},{0,4},{12,8},{8,12},{20,16},{16,20},{28,24},{24,28},{5,1},{1... | collective-permute-start | bytes 393224 | tf_op jit(solution)/shard_map/ppermute | solution.py:33

commit v8 on v7

--- a/solution.py
+++ b/solution.py
@@ -62,7 +62,7 @@
     ):
         extra.append(pltpu.make_async_copy(*pair, sems.at[len(chunks) + k]))
     first_copy, lengths_copy, bias_copy, second_copy = extra
-    for copy in [lengths_copy, first_copy, copies[0], bias_copy, *copies[1:], second_copy]:
+    for copy in [copies[0], first_copy, lengths_copy, bias_copy, second_copy, *copies[1:]]:
         copy.start()
     clips = lengths_ref.shape[1]
     lengths_copy.wait()
@@ -74,28 +74,30 @@
     starts = ends - sizes
     live = jnp.sum(lengths_ref[...])
     bias_copy.wait()
-    first_copy.wait()
     root = math.sqrt(2.0 / math.pi)
 
-    def pooled_chunk(at, rows):
+    def place_of(at, rows):
+        place = lax.broadcasted_iota(jnp.int32, (clips, rows), 1).astype(F32) + float(at)
+        return jnp.where((place >= starts) & (place < ends), 1.0, 0.0).astype(BF16)
+
+    def pooled_chunk(at, rows, onehot):
         before = mm(held[pl.ds(at, rows), :], first_ref[...]) + bias_ref[...]
         half = before * 0.5
         inner = before * (root + (root * 0.044715) * (before * before))
         active = (half + half * jnp.tanh(inner)).astype(BF16)
-        place = lax.broadcasted_iota(jnp.int32, (clips, rows), 1).astype(F32) + float(at)
-        onehot = jnp.where((place >= starts) & (place < ends), 1.0, 0.0).astype(BF16)
         return mm(onehot, active)
 
-    at = 0
-    for k, rows in enumerate(chunks):
+    onehot = place_of(0, chunks[0])
+    first_copy.wait()
+    copies[0].wait()
+    pooled_ref[...] = pooled_chunk(0, chunks[0], onehot)
+    at = chunks[0]
+    for k, rows in enumerate(chunks[1:], 1):
         copies[k].wait()
-        if k == 0:
-            pooled_ref[...] = pooled_chunk(at, rows)
-        else:
-
-            @pl.when(live > at)
-            def _():
-                pooled_ref[...] += pooled_chunk(at, rows)
+
+        @pl.when(live > at)
+        def _():
+            pooled_ref[...] += pooled_chunk(at, rows, place_of(at, rows))
 
         at += rows
     second_copy.wait()
@@ -103,7 +105,8 @@
     high = total.astype(BF16)
     rest = (total - high.astype(F32)).astype(BF16)
     second = second_ref[...]
-    pooled = (mm(high, second) + mm(rest, second)) / sizes
+    both = mm(jnp.concatenate([high, rest], axis=0), second)
+    pooled = (both[:clips] + both[clips:]) / sizes
     pooled_ref[...] = pooled
     audio_ref[...] = unit_low(pooled).astype(BF16)
 
@@ -115,9 +118,10 @@
         values = audio[row][...]
         partial = None
         downs = []
+        whole = jnp.exp2(mm(values, text, 1, 1) * (scale * LOG2E))
+        grown_ref[pl.ds(r * block, block), :] = whole
         for c in range(len(columns)):
-            grown = jnp.exp2(mm(values, text[c], 1, 1) * (scale * LOG2E))
-            grown_ref[pl.ds(r * block, block), pl.ds(c * block, block)] = grown
+            grown = whole[:, c * block : (c + 1) * block]
             downs.append(jnp.sum(grown, axis=0, keepdims=True))
             partial = grown if c == 0 else partial + grown
         col_sums = downs if col_sums is None else [x + y for x, y in zip(col_sums, downs, strict=True)]
@@ -134,16 +138,20 @@
     for c, column in enumerate(columns):
         text.append(unit_low(raw[column][...].astype(F32)).astype(BF16))
         low_ref[pl.ds(c * block, block), :] = text[c]
+    text = jnp.concatenate(text, axis=0)
     audio = refs[:audio_count]
     tile_kernel(rows, columns, audio, text, None, scale_ref[0, 0], grown_ref, row_ref, col_ref)
 
 
 def late_tile_kernel(rows, columns, scale_ref, *refs):
-    low_ref, sums_ref, grown_ref, row_ref, col_ref = refs[len(refs) - 5 :]
+    low_ref, sums_ref, early_ref, grown_ref, row_ref, col_ref = refs[len(refs) - 6 :]
+    early = early_ref.shape[0]
+    row_ref[pl.ds(0, early), :] = early_ref[...]
+    row_ref = row_ref.at[pl.ds(early, len(rows))]
     block = row_ref.shape[1]
-    text = [low_ref[pl.ds(c * block, block), :] for c in range(len(columns))]
+    text = low_ref[...]
     sums = [sums_ref[pl.ds(c, 1), :] for c in range(len(columns))]
-    audio = refs[: len(refs) - 5]
+    audio = refs[: len(refs) - 6]
     tile_kernel(rows, columns, audio, text, sums, scale_ref[0, 0], grown_ref, row_ref, col_ref)
 
 
@@ -185,10 +193,12 @@
         return (values * (row_scale[row] + col_scale[column])).astype(BF16)
 
     def audio_total():
-        return sum(mm(weights(pick[0], column), text[column][...]) for column in columns)
+        row = jnp.concatenate([weights(pick[0], column) for column in columns], axis=1)
+        return mm(row, jnp.concatenate([text[column][...] for column in columns], axis=0))
 
     def text_total():
-        return sum(mm(weights(row, pick[1]), audio[row][...], 0, 0) for row in rows)
+        column = jnp.concatenate([weights(row, pick[1]) for row in rows], axis=0)
+        return mm(column, jnp.concatenate([audio[row][...] for row in rows], axis=0), 0, 0)
 
     if pair_count is None:
         outs[0][...] = audio_total().astype(BF16)
@@ -296,12 +306,16 @@
     )(scale, *early_audio, *text)
     late_grown, late_sum, col_sum = pl.pallas_call(
         functools.partial(late_tile_kernel, late_rows, columns),
-        out_shape=tile_shapes(late_rows),
-        in_specs=[SMEM] + [VMEM] * (len(late_audio) + 2),
+        out_shape=(
+            tile_shapes(late_rows)[0],
+            jax.ShapeDtypeStruct((len(early_rows + late_rows), clips), F32),
+            tile_shapes(late_rows)[2],
+        ),
+        in_specs=[SMEM] + [VMEM] * (len(late_audio) + 3),
         out_specs=[VMEM] * 3,
         compiler_params=PARAMS,
-    )(scale, *late_audio, text_low, col_sum)
-    row_sum = jnp.concatenate([early_sum, late_sum], axis=0)
+    )(scale, *late_audio, text_low, col_sum, early_sum)
+    row_sum = late_sum
     row_other, col_other = swap(row_sum, row_bit), swap(col_sum, col_bit)
     rows, audio = early_rows + late_rows, early_audio + late_audio
     operands = [early_grown, late_grown, row_sum, row_other, col_sum, col_other, *audio, text_low]

time: 34.9 us -> 35 us (level)
  starting transfers between devices: 14 us -> 14.5 us
  waiting for transfers between devices: 11.7 us -> 11.3 us
    ppermute x10, starting transfers between devices: 14 us -> 14.5 us  [swap(): return lax.ppermute(block, 'blk', [(i ^ offset, i) for i in range(count)])]
    ppermute x10, waiting for transfers between devices: 11.7 us -> 11.3 us  [swap(): return lax.ppermute(block, 'blk', [(i ^ offset, i) for i in range(count)])]
where the time goes in v8:
time: 35 us; the launch traced here: 34.5 us
  starting transfers between devices  14.5 us (41%)
  waiting for transfers between devices  11.3 us (32%)
  Pallas kernels  7.41 us (21%)
  between operations  1.35 us (4%)
    ppermute x10, starting transfers between devices, swap(): return lax.ppermute(block, 'blk', [(i ^ offset, i) for i in range(count)])  14.5 us
    ppermute x10, waiting for transfers between devices, swap(): return lax.ppermute(block, 'blk', [(i ^ offset, i) for i in range(count)])  11.3 us
    pallas_call x1, Pallas kernels, local(): pl.pallas_call(functools.partial(frames_kernel, chunks), out_shape=(block...  3.66 us
    pallas_call x2, Pallas kernels, final(): pl.pallas_call(functools.partial(final_kernel, pair_count, sides), out_sh...  1.74 us
    pallas_call x1, Pallas kernels, local(): pl.pallas_call(functools.partial(early_tile_kernel, early_rows, columns,...  0.85 us
    pallas_call x2, Pallas kernels, grads(): pl.pallas_call(functools.partial(grad_kernel, rows, columns, row_bit, col...  0.78 us
  transfers between devices with their start and end apart: 10, of which 6 were waited for; matrix products, arithmetic and copies ran while one was open for 0% of the time, Pallas kernels for 17%

profile of v8, /device:TPU:0, one launch (start us, length us, event | category | flops | bytes accessed | tf_op | source)
XLA Modules:
  0.0 34.5 jit_solution(2192920535264814317)
XLA Ops:
  0.6 4.1 %collective-permute-start.2 = (bf16[128,512]{1,0:T(8,128)(2,1)}, bf16[128,512]{1,0:T(8,128)(2,1)S(1)}, u32[]{:S(2)}, u32[]{:S(2)}) collective-permute-start(bf16[128,512]{1,0:T(8,128)(2,1)} %refs_12_.1), channel_id=1, source_target_pairs={{16,0},{20,4},{24,8},{28,12},{0,16},{4,20},{8,24},{12,28},{17,1},{... | collective-permute-start | bytes 393224 | tf_op jit(solution)/shard_map/ppermute | solution.py:33
  4.7 3.7 %shard_map.86 = (f32[128,512]{1,0:T(8,128)S(1)}, bf16[128,512]{1,0:T(8,128)(2,1)S(1)}) custom-call(s32[1,128]{1,0:T(1,128)} %bitcast.10, f32[1,512]{1,0:T(1,128)} %bitcast.9, bf16[768,512]{1,0:T(8,128)(2,1)} %refs_2_.1, bf16[512,512]{1,0:T(8,128)(2,1)} %refs_3_.2, bf16[4096,768]{1,0:T(8,128)(2,1)} %refs_4_.1), custom_call_target="tpu_custom_call" | custom-call | tf_op jit(solution)/shard_map/pallas_call | solution.py:248
  8.4 0.1 collective-permute-start
  8.5 2.6 %collective-permute-start.1 = (bf16[128,512]{1,0:T(8,128)(2,1)S(1)}, bf16[128,512]{1,0:T(8,128)(2,1)S(1)}, u32[]{:S(2)}, u32[]{:S(2)}) collective-permute-start(bf16[128,512]{1,0:T(8,128)(2,1)S(1)} %get-tuple-element.20.refs_0_.refs_6_), channel_id=1, source_target_pairs={{8,0},{12,4},{0,8},{4,12},{24,16},{28,20},{16,24},{20,28},{9,1},{1... | collective-permute-start | bytes 393224 | tf_op jit(solution)/shard_map/ppermute | solution.py:33
  11.1 1.8 %collective-permute-start.3 = (bf16[128,512]{1,0:T(8,128)(2,1)S(1)}, bf16[128,512]{1,0:T(8,128)(2,1)S(1)}, u32[]{:S(2)}, u32[]{:S(2)}) collective-permute-start(bf16[128,512]{1,0:T(8,128)(2,1)S(1)} %copy-done), channel_id=1, source_target_pairs={{4,0},{0,4},{12,8},{8,12},{20,16},{16,20},{28,24},{24,28},{5,1},{1... | collective-permute-start | bytes 393224 | tf_op jit(solution)/shard_map/ppermute | solution.py:33
  12.9 0.2 collective-permute-start.4
  13.1 4.0 %collective-permute-done.refs_1_.refs_7_ = bf16[128,512]{1,0:T(8,128)(2,1)S(1)} collective-permute-done((bf16[128,512]{1,0:T(8,128)(2,1)S(1)}, bf16[128,512]{1,0:T(8,128)(2,1)S(1)}, u32[]{:S(2)}, u32[]{:S(2)}) %collective-permute-start) | collective-permute-done | bytes 131104 | tf_op jit(solution)/shard_map/ppermute | solution.py:33
  17.2 0.5 %collective-permute-start.5 = (bf16[128,512]{1,0:T(8,128)(2,1)S(1)}, bf16[128,512]{1,0:T(8,128)(2,1)S(1)}, u32[]{:S(2)}, u32[]{:S(2)}) collective-permute-start(bf16[128,512]{1,0:T(8,128)(2,1)S(1)} %collective-permute-done.refs_1_.refs_7_), channel_id=1, source_target_pairs={{8,0},{12,4},{0,8},{4,12},{24,16},{28,20},{16,24},{20,28},{9,1},{1... | collective-permute-start | bytes 393224 | tf_op jit(solution)/shard_map/ppermute | solution.py:33
  18.3 0.0 collective-permute-done.3.refs_5_
  18.3 0.8 %shard_map.87 = (f32[384,512]{1,0:T(8,128)S(1)}, f32[3,128]{1,0:T(4,128)S(1)}, f32[4,128]{1,0:T(4,128)S(1)}, bf16[512,512]{1,0:T(8,128)(2,1)S(1)}) custom-call(f32[1,1]{1,0:T(1,128)} %bitcast.3.scale_ref, bf16[128,512]{1,0:T(8,128)(2,1)S(1)} %get-tuple-element.20.refs_0_.refs_6_, bf16[128,512]{1,0:T(8,128)(2,1)S(1)} %collective-permute-done.refs_1_.refs_7_, ...), custom_call_target="tpu_custom_call" | custom-call | tf_op jit(solution)/shard_map/pallas_call | solution.py:297
  19.2 2.9 %collective-permute-done.5.refs_0_.refs_9_ = bf16[128,512]{1,0:T(8,128)(2,1)S(1)} collective-permute-done((bf16[128,512]{1,0:T(8,128)(2,1)S(1)}, bf16[128,512]{1,0:T(8,128)(2,1)S(1)}, u32[]{:S(2)}, u32[]{:S(2)}) %collective-permute-start.5) | collective-permute-done | bytes 131104 | tf_op jit(solution)/shard_map/ppermute | solution.py:33
  22.1 0.4 %shard_map.88 = (f32[128,512]{1,0:T(8,128)S(1)}, f32[4,128]{1,0:T(4,128)S(1)}, f32[4,128]{1,0:T(4,128)S(1)}) custom-call(f32[1,1]{1,0:T(1,128)} %bitcast.4.scale_ref, bf16[128,512]{1,0:T(8,128)(2,1)S(1)} %collective-permute-done.5.refs_0_.refs_9_, bf16[512,512]{1,0:T(8,128)(2,1)S(1)} %get-tuple-element.23.refs_1_.refs_10_, ...), custom_call_target="tpu_custom_call" | custom-call | tf_op jit(solution)/shard_map/pallas_call | solution.py:307
  22.5 1.0 %collective-permute-start.6 = (f32[4,128]{1,0:T(4,128)S(1)}, f32[4,128]{1,0:T(4,128)S(1)}, u32[]{:S(2)}, u32[]{:S(2)}) collective-permute-start(f32[4,128]{1,0:T(4,128)S(1)} %get-tuple-element.27.refs_2_), channel_id=1, source_target_pairs={{8,0},{12,4},{0,8},{4,12},{24,16},{28,20},{16,24},{20,28},{9,1},{1... | collective-permute-start | bytes 6152 | tf_op jit(solution)/shard_map/ppermute | solution.py:33
  23.5 1.5 %collective-permute-start.7 = (f32[4,128]{1,0:T(4,128)S(1)}, f32[4,128]{1,0:T(4,128)S(1)}, u32[]{:S(2)}, u32[]{:S(2)}) collective-permute-start(f32[4,128]{1,0:T(4,128)S(1)} %get-tuple-element.28.refs_4_), channel_id=1, source_target_pairs={{4,0},{0,4},{12,8},{8,12},{20,16},{16,20},{28,24},{24,28},{5,1},{1... | collective-permute-start | bytes 6152 | tf_op jit(solution)/shard_map/ppermute | solution.py:33
  25.0 1.1 %collective-permute-done.6.refs_3_ = f32[4,128]{1,0:T(4,128)S(1)} collective-permute-done((f32[4,128]{1,0:T(4,128)S(1)}, f32[4,128]{1,0:T(4,128)S(1)}, u32[]{:S(2)}, u32[]{:S(2)}) %collective-permute-start.6) | collective-permute-done | bytes 2080 | tf_op jit(solution)/shard_map/ppermute | solution.py:33
  26.2 0.9 %collective-permute-done.7.refs_5_ = f32[4,128]{1,0:T(4,128)S(1)} collective-permute-done((f32[4,128]{1,0:T(4,128)S(1)}, f32[4,128]{1,0:T(4,128)S(1)}, u32[]{:S(2)}, u32[]{:S(2)}) %collective-permute-start.7) | collective-permute-done | bytes 2080 | tf_op jit(solution)/shard_map/ppermute | solution.py:33
  27.1 0.4 %shard_map.90 = (bf16[128,512]{1,0:T(8,128)(2,1)S(1)}, bf16[128,512]{1,0:T(8,128)(2,1)S(1)}) custom-call(f32[1,1]{1,0:T(1,128)} %bitcast.6.scale_ref, f32[384,512]{1,0:T(8,128)S(1)} %get-tuple-element.22.refs_0_, f32[128,512]{1,0:T(8,128)S(1)} %get-tuple-element.26.refs_1_, f32[4,128]{1,0:T(4,128)S(1)} %get-tuple-element.27.refs_2_, ...), custom_call_target="tpu_custom_call" | custom-call | tf_op jit(solution)/shard_map/pallas_call | solution.py:324
  27.5 1.2 %collective-permute-start.8 = (bf16[128,512]{1,0:T(8,128)(2,1)S(1)}, bf16[128,512]{1,0:T(8,128)(2,1)S(1)}, u32[]{:S(2)}, u32[]{:S(2)}) collective-permute-start(bf16[128,512]{1,0:T(8,128)(2,1)S(1)} %get-tuple-element.33), channel_id=1, source_target_pairs={{8,0},{12,4},{0,8},{4,12},{24,16},{28,20},{16,24},{20,28},{9,1},{1... | collective-permute-start | bytes 393224 | tf_op jit(solution)/shard_map/ppermute | solution.py:33
  28.7 1.5 %collective-permute-start.9 = (bf16[128,512]{1,0:T(8,128)(2,1)S(1)}, bf16[128,512]{1,0:T(8,128)(2,1)S(1)}, u32[]{:S(2)}, u32[]{:S(2)}) collective-permute-start(bf16[128,512]{1,0:T(8,128)(2,1)S(1)} %get-tuple-element.37), channel_id=1, source_target_pairs={{4,0},{0,4},{12,8},{8,12},{20,16},{16,20},{28,24},{24,28},{5,1},{1... | collective-permute-start | bytes 393224 | tf_op jit(solution)/shard_map/ppermute | solution.py:33
  30.2 0.4 %shard_map.89 = (f32[128,512]{1,0:T(8,128)S(1)}, f32[128,512]{1,0:T(8,128)S(1)}, f32[128,128]{1,0:T(8,128)S(1)}, f32[128,512]{1,0:T(8,128)S(1)}, f32[128,512]{1,0:T(8,128)S(1)}, /*index=5*/f32[128,128]{1,0:T(8,128)S(1)}) custom-call(f32[1,1]{1,0:T(1,128)} %bitcast.5.scale_ref, f32[384,512]{1,0:T(8,128)S(1)} %get-tuple-element.22.refs_0_, ...), custom_call_target="tpu_custom_call" | custom-call | tf_op jit(solution)/shard_map/pallas_call | solution.py:324
  30.6 2.0 %collective-permute-done.8.refs_3_ = bf16[128,512]{1,0:T(8,128)(2,1)S(1)} collective-permute-done((bf16[128,512]{1,0:T(8,128)(2,1)S(1)}, bf16[128,512]{1,0:T(8,128)(2,1)S(1)}, u32[]{:S(2)}, u32[]{:S(2)}) %collective-permute-start.8) | collective-permute-done | bytes 131104 | tf_op jit(solution)/shard_map/ppermute | solution.py:33
  32.6 0.9 %shard_map.91 = f32[128,512]{1,0:T(8,128)} custom-call(f32[1,1]{1,0:T(1,128)} %bitcast.7.scale_ref, f32[128,512]{1,0:T(8,128)S(1)} %get-tuple-element.30.refs_0_, f32[128,512]{1,0:T(8,128)S(1)} %get-tuple-element.31.refs_1_, f32[128,128]{1,0:T(8,128)S(1)} %get-tuple-element.32.refs_2_, bf16[128,512]{1,0:T(8,128)(2,1)S(1)} %collective-permute-done.8.refs_3_), custom_call_target="tpu_custom_call" | custom-call | tf_op jit(solution)/shard_map/pallas_call | solution.py:339
  33.4 0.2 collective-permute-done.9.refs_3_
  33.6 0.9 %shard_map.92 = f32[128,512]{1,0:T(8,128)} custom-call(f32[1,1]{1,0:T(1,128)} %bitcast.8.scale_ref, f32[128,512]{1,0:T(8,128)S(1)} %get-tuple-element.34.refs_0_, f32[128,512]{1,0:T(8,128)S(1)} %get-tuple-element.35.refs_1_, f32[128,128]{1,0:T(8,128)S(1)} %get-tuple-element.36.refs_2_, bf16[128,512]{1,0:T(8,128)(2,1)S(1)} %collective-permute-done.9.refs_3_), custom_call_target="tpu_custom_call" | custom-call | tf_op jit(solution)/shard_map/pallas_call | solution.py:339
  (5 shorter events, 0.0 us)
Async XLA Ops:
  0.6 10.5 %copy-start = (bf16[128,512]{1,0:T(8,128)(2,1)S(1)}, bf16[128,512]{1,0:T(8,128)(2,1)}, u32[]{:S(2)}) copy-start(bf16[128,512]{1,0:T(8,128)(2,1)} %refs_12_.1) | copy-start | bytes 393220
  0.6 12.3 %collective-permute-start.2 = (bf16[128,512]{1,0:T(8,128)(2,1)}, bf16[128,512]{1,0:T(8,128)(2,1)S(1)}, u32[]{:S(2)}, u32[]{:S(2)}) collective-permute-start(bf16[128,512]{1,0:T(8,128)(2,1)} %refs_12_.1), channel_id=1, source_target_pairs={{16,0},{20,4},{24,8},{28,12},{0,16},{4,20},{8,24},{12,28},{17,1},{... | collective-permute-start | bytes 393224 | tf_op jit(solution)/shard_map/ppermute | solution.py:33
  8.4 8.8 %collective-permute-start = (bf16[128,512]{1,0:T(8,128)(2,1)S(1)}, bf16[128,512]{1,0:T(8,128)(2,1)S(1)}, u32[]{:S(2)}, u32[]{:S(2)}) collective-permute-start(bf16[128,512]{1,0:T(8,128)(2,1)S(1)} %get-tuple-element.20.refs_0_.refs_6_), channel_id=1, source_target_pairs={{16,0},{20,4},{24,8},{28,12},{0,16},{4,20},{8,24},{12,28},{17,1},{... | collective-permute-start | bytes 393224 | tf_op jit(solution)/shard_map/ppermute | solution.py:33
  8.5 9.8 %collective-permute-start.1 = (bf16[128,512]{1,0:T(8,128)(2,1)S(1)}, bf16[128,512]{1,0:T(8,128)(2,1)S(1)}, u32[]{:S(2)}, u32[]{:S(2)}) collective-permute-start(bf16[128,512]{1,0:T(8,128)(2,1)S(1)} %get-tuple-element.20.refs_0_.refs_6_), channel_id=1, source_target_pairs={{8,0},{12,4},{0,8},{4,12},{24,16},{28,20},{16,24},{20,28},{9,1},{1... | collective-permute-start | bytes 393224 | tf_op jit(solution)/shard_map/ppermute | solution.py:33
  11.1 7.2 %collective-permute-start.3 = (bf16[128,512]{1,0:T(8,128)(2,1)S(1)}, bf16[128,512]{1,0:T(8,128)(2,1)S(1)}, u32[]{:S(2)}, u32[]{:S(2)}) collective-permute-start(bf16[128,512]{1,0:T(8,128)(2,1)S(1)} %copy-done), channel_id=1, source_target_pairs={{4,0},{0,4},{12,8},{8,12},{20,16},{16,20},{28,24},{24,28},{5,1},{1... | collective-permute-start | bytes 393224 | tf_op jit(solution)/shard_map/ppermute | solution.py:33
  12.9 5.4 %collective-permute-start.4 = (bf16[128,512]{1,0:T(8,128)(2,1)S(1)}, bf16[128,512]{1,0:T(8,128)(2,1)S(1)}, u32[]{:S(2)}, u32[]{:S(2)}) collective-permute-start(bf16[128,512]{1,0:T(8,128)(2,1)S(1)} %collective-permute-done.2.refs_4_), channel_id=1, source_target_pairs={{4,0},{0,4},{12,8},{8,12},{20,16},{16,20},{28,24},{24,28},{5,1},{1... | collective-permute-start | bytes 393224 | tf_op jit(solution)/shard_map/ppermute | solution.py:33
  17.2 5.0 %collective-permute-start.5 = (bf16[128,512]{1,0:T(8,128)(2,1)S(1)}, bf16[128,512]{1,0:T(8,128)(2,1)S(1)}, u32[]{:S(2)}, u32[]{:S(2)}) collective-permute-start(bf16[128,512]{1,0:T(8,128)(2,1)S(1)} %collective-permute-done.refs_1_.refs_7_), channel_id=1, source_target_pairs={{8,0},{12,4},{0,8},{4,12},{24,16},{28,20},{16,24},{20,28},{9,1},{1... | collective-permute-start | bytes 393224 | tf_op jit(solution)/shard_map/ppermute | solution.py:33
  22.5 3.7 %collective-permute-start.6 = (f32[4,128]{1,0:T(4,128)S(1)}, f32[4,128]{1,0:T(4,128)S(1)}, u32[]{:S(2)}, u32[]{:S(2)}) collective-permute-start(f32[4,128]{1,0:T(4,128)S(1)} %get-tuple-element.27.refs_2_), channel_id=1, source_target_pairs={{8,0},{12,4},{0,8},{4,12},{24,16},{28,20},{16,24},{20,28},{9,1},{1... | collective-permute-start | bytes 6152 | tf_op jit(solution)/shard_map/ppermute | solution.py:33
  23.5 3.6 %collective-permute-start.7 = (f32[4,128]{1,0:T(4,128)S(1)}, f32[4,128]{1,0:T(4,128)S(1)}, u32[]{:S(2)}, u32[]{:S(2)}) collective-permute-start(f32[4,128]{1,0:T(4,128)S(1)} %get-tuple-element.28.refs_4_), channel_id=1, source_target_pairs={{4,0},{0,4},{12,8},{8,12},{20,16},{16,20},{28,24},{24,28},{5,1},{1... | collective-permute-start | bytes 6152 | tf_op jit(solution)/shard_map/ppermute | solution.py:33
  27.5 5.0 %collective-permute-start.8 = (bf16[128,512]{1,0:T(8,128)(2,1)S(1)}, bf16[128,512]{1,0:T(8,128)(2,1)S(1)}, u32[]{:S(2)}, u32[]{:S(2)}) collective-permute-start(bf16[128,512]{1,0:T(8,128)(2,1)S(1)} %get-tuple-element.33), channel_id=1, source_target_pairs={{8,0},{12,4},{0,8},{4,12},{24,16},{28,20},{16,24},{20,28},{9,1},{1... | collective-permute-start | bytes 393224 | tf_op jit(solution)/shard_map/ppermute | solution.py:33
  28.7 5.0 %collective-permute-start.9 = (bf16[128,512]{1,0:T(8,128)(2,1)S(1)}, bf16[128,512]{1,0:T(8,128)(2,1)S(1)}, u32[]{:S(2)}, u32[]{:S(2)}) collective-permute-start(bf16[128,512]{1,0:T(8,128)(2,1)S(1)} %get-tuple-element.37), channel_id=1, source_target_pairs={{4,0},{0,4},{12,8},{8,12},{20,16},{16,20},{28,24},{24,28},{5,1},{1... | collective-permute-start | bytes 393224 | tf_op jit(solution)/shard_map/ppermute | solution.py:33
